TPU v7x, 128 devices: a whole 4x4x4 slice. The times are simulated.
128 devices in a mesh: lib: 8 (over y, x_hi), row: 4 (over z), col: 4 (over x_lo, core).
Axes of the slice: x: 4 (x_hi: 2, x_lo: 2; x = x_hi * 2 + x_lo), y: 4, z: 4, core: 2. Of those that a mesh axis runs over, the one named last changes fastest.
Arguments:
- abundance: float32 [1024, 128, 1024], P('lib', 'row', 'col'), may hold values from 0 to 1
- duals: float32 [2, 1024, 128, 1024], P(None, 'lib', 'row', 'col'), may hold values from -1 to 1
- reflectance: bfloat16 [224, 128, 1024], P(None, 'row', 'col'), may hold values from -6 to 6
- library: bfloat16 [224, 1024], P(None, 'lib'), may hold values from -0.375 to 0.375
Outputs:
- abund_next: float32 [1024, 128, 1024], P('lib', 'row', 'col')
- duals_next: float32 [2, 1024, 128, 1024], P(None, 'lib', 'row', 'col')
All inputs are finite; a program needn't handle non-finite values.
Results may differ from a plain program's by a relative error of at most 0.0018.
Values may be sent and summed in bfloat16 or wider, within the bound.
No kernel may reach another device: no remote copies, remote signals or barrier semaphores. Data moves between devices by JAX's collectives and lax.ppermute only.
A program may use at most 192 MiB of HBM per device.

v0:
```python
import jax
import jax.numpy as jnp
from jax import lax
from jax.sharding import Mesh
from jax.sharding import PartitionSpec as P

PASSES = 3
LIB = ("lib_0", "lib_1")


def sum_by_axis(array, axes, dim):
    if not axes:
        return array
    nearer = lax.psum_scatter(array, axes[0], scatter_dimension=dim, tiled=True)
    return sum_by_axis(nearer, axes[1:], dim)


def laid_out(pieces, dim):
    dims = list(pieces.shape[1:])
    dims[dim] *= pieces.shape[0]
    return jnp.moveaxis(pieces, 0, dim).reshape(dims)


def sent_to_all(array, axis):
    length = lax.axis_size(axis)
    return lax.all_to_all(
        jnp.broadcast_to(array[None], (length, *array.shape)), axis, 0, 0, tiled=True
    )


def collect(array, axis, dim):
    return laid_out(sent_to_all(array, axis), dim)


def for_sending(array):
    return jax.tree.map(lambda a: a.astype(jnp.bfloat16) if a.dtype == jnp.float32 else a, array)


def shifted(array, axis, by):
    length = lax.axis_size(axis)
    pairs = [(i, i + by) for i in range(length) if 0 <= i + by < length]
    return lax.ppermute(array, axis, pairs)


def on_device(abundance, duals, reflectance, library):
    maps, height, width = abundance.shape
    bands = library.shape[0]
    pixels = height * width
    total_rows = height * lax.axis_size("row")
    total_cols = width * lax.axis_size("col")
    row_place = lax.axis_index("row") * height + lax.broadcasted_iota(jnp.int32, (height, width), 0)
    col_place = lax.axis_index("col") * width + lax.broadcasted_iota(jnp.int32, (height, width), 1)
    keep_rows = (row_place < total_rows - 1).astype(jnp.float32)
    keep_cols = (col_place < total_cols - 1).astype(jnp.float32)
    dual = jnp.stack([duals[0] * keep_rows, duals[1] * keep_cols])
    compact = abundance.astype(jnp.bfloat16).reshape(maps, pixels)
    observed = reflectance.reshape(bands, pixels).astype(jnp.float32)
    partial_value = jnp.dot(library, compact, preferred_element_type=jnp.float32)
    share = sum_by_axis(partial_value, LIB, 1)
    share_width = share.shape[1]
    mine = lax.dynamic_slice_in_dim(observed, lax.axis_index(LIB) * share_width, share_width, 1)
    resid = share - mine
    whole_library = collect(library, LIB, 1)
    descent_share = jnp.einsum(
        "bm,bp->mp", whole_library, resid.astype(jnp.bfloat16), preferred_element_type=jnp.float32
    )
    descent = lax.all_to_all(descent_share, LIB, split_axis=0, concat_axis=1, tiled=True)
    start = abundance - 0.1 * descent.reshape(maps, height, width)

    def inner_field(current):
        above = shifted(for_sending(current[0][:, height - 1 :, :]), "row", 1)
        left = shifted(current[1][:, :, width - 1 :], "col", 1)
        first_prev = jnp.concatenate([above, current[0][:, : height - 1, :]], axis=1)
        second_prev = jnp.concatenate([left, current[1][:, :, : width - 1]], axis=2)
        return start - 0.25 * (current[0] - first_prev + (current[1] - second_prev))

    for step in range(PASSES):
        field = inner_field(dual)
        below = shifted(for_sending(field[:, :1, :]), "row", -1)
        beside = shifted(field[:, :, :1], "col", -1)
        down = (jnp.concatenate([field[:, 1:, :], below], axis=1) - field) * keep_rows
        right = (jnp.concatenate([field[:, :, 1:], beside], axis=2) - field) * keep_cols
        dual = jnp.clip(dual + 0.5 * jnp.stack([down, right]), -1.0, 1.0)
    final = inner_field(dual)
    abund_next = jnp.maximum(final - 0.02, 0.0)
    return (abund_next, dual)


def solution(mesh):
    torus = Mesh(
        mesh.devices.reshape(4, 2, mesh.shape["row"], mesh.shape["col"]),
        ("lib_0", "lib_1", "row", "col"),
    )
    placed = (P(LIB, "row", "col"), P(None, LIB, "row", "col"), P(None, "row", "col"), P(None, LIB))
    return jax.shard_map(
        on_device,
        mesh=torus,
        in_specs=placed,
        out_specs=(P(LIB, "row", "col"), P(None, LIB, "row", "col")),
        check_vma=False,
    )
```

profile of v0, /device:TPU:1, one launch (start us, length us, event | category | flops | bytes accessed | tf_op | source)
XLA Modules:
  0.0 354.5 jit_solution(4737494579723002652)
XLA Ops:
  15.4 75.9 %reduce-scatter.3.cloned.1.call-done = f32[224,2048]{1,0:T(8,128)} async-done(((f32[224,8192]{1,0:T(8,128)}), f32[224,2048]{1,0:T(8,128)}) %reduce-scatter.3.cloned.1.call-update) | async-done | bytes 1835024 | tf_op jit(solution)/shard_map/reduce_scatter | solution.py:14
  92.2 4.9 %all-to-all-start = ((bf16[8,224,128]{2,1,0:T(8,128)(2,1)}), bf16[8,224,128]{2,1,0:T(8,128)(2,1)S(1)}, u32[]{:S(2)}, u32[]{:S(2)}) async-start(bf16[8,224,128]{2,1,0:T(8,128)(2,1)} %broadcast_in_dim.2), calls=%async_computation.2 | async-start | bytes 917504 | tf_op jit(solution)/shard_map/all_to_all | solution.py:26
  97.0 8.4 %copy.39 = f32[28,8,32,256]{3,1,2,0:T(8,128)} copy(bf16[28,8,32,256]{3,2,1,0:T(8,128)(2,1)} %bitcast.92) | data formatting | bytes 11010048
  107.1 20.2 %reduce-scatter.5.cloned.1.call-done = f32[224,1024]{1,0:T(8,128)} async-done(((f32[224,2048]{1,0:T(8,128)}), f32[224,1024]{1,0:T(8,128)}) %reduce-scatter.5.cloned.1.call-update) | async-done | bytes 917520 | tf_op jit(solution)/shard_map/reduce_scatter | solution.py:14
  131.5 5.3 %copy.15 = f32[8,128,1024]{1,2,0:T(8,128)} copy(f32[8,128,1024]{2,1,0:T(8,128)} %bitcast.88) | data formatting | bytes 8388608 | tf_op jit(solution)/shard_map/all_to_all | solution.py:67
  136.9 4.5 %all-to-all-start.1 = ((f32[8,128,1024]{1,2,0:T(8,128)}), f32[8,128,1024]{1,2,0:T(8,128)}, u32[]{:S(2)}, u32[]{:S(2)}) async-start(f32[8,128,1024]{1,2,0:T(8,128)} %copy.15), calls=%async_computation.3 | async-start | bytes 8388608 | tf_op jit(solution)/shard_map/all_to_all | solution.py:67
  141.4 8.5 %fusion.35 = (f32[1,128,32,256]{3,2,1,0:T(8,128)}, f32[1,128,32,256]{3,2,1,0:T(8,128)}) fusion(f32[2,128,32,256]{3,2,1,0:T(8,128)} %param.5), kind=kLoop, calls=%fused_computation.74 | loop fusion | bytes 16777216 | tf_op jit(solution)/shard_map/slice | solution.py:55
  149.9 5.4 %copy.35 = f32[1,128,32,256]{1,3,2,0:T(8,128)} copy(f32[1,128,32,256]{3,2,1,0:T(8,128)} %get-tuple-element.15) | data formatting | bytes 8388608
  163.2 5.3 %copy.36 = f32[1,128,32,256]{1,3,2,0:T(8,128)} copy(f32[1,128,32,256]{3,2,1,0:T(8,128)} %get-tuple-element.14) | data formatting | bytes 8388608
  176.3 5.3 %copy.16 = f32[128,32,256]{0,2,1:T(8,128)} copy(f32[128,32,256]{2,1,0:T(8,128)} %param.4) | data formatting | bytes 8388608 | tf_op args[0]
  181.6 4.6 %slice.164 = f32[128,31,256]{0,2,1:T(8,128)} slice(f32[128,32,256]{0,2,1:T(8,128)} %copy-done.11), slice={[0:128], [0:31], [0:256]} | slice | bytes 8126464 | tf_op jit(solution)/shard_map/slice | solution.py:73
  186.2 5.7 %all-to-all-done.1 = f32[8,128,1024]{1,2,0:T(8,128)} async-done(((f32[8,128,1024]{1,2,0:T(8,128)}), f32[8,128,1024]{1,2,0:T(8,128)}, u32[]{:S(2)}, u32[]{:S(2)}) %all-to-all-start.1) | async-done | bytes 4194336 | tf_op jit(solution)/shard_map/all_to_all | solution.py:67
  192.0 4.9 %broadcast_multiply_fusion.2 = f32[8,128,1024]{1,2,0:T(8,128)} fusion(f32[8,128,1024]{1,2,0:T(8,128)} %all-to-all-done.1), kind=kLoop, calls=%fused_computation.59 | loop fusion | flops 1048576 | bytes 8388608 | tf_op jit(solution)/shard_map/mul | solution.py:68
  198.2 7.1 %fusion.7 = (f32[128,32,256]{0,2,1:T(8,128)S(1)}, f32[128,32,256]{0,2,1:T(8,128)S(1)}) fusion(f32[128,31,256]{0,2,1:T(8,128)} %slice.164, f32[128,1,256]{0,2,1:T(8,128)S(1)} %convert_element_type.56, f32[128,32,255]{0,2,1:T(8,128)} %bitcast.83, f32[128,32,1]{0,2,1:T(1,128)S(1)} %bitcast.93, f32[128,32,256]{0,2,1:T(8,128)} %copy.16, ...), kind=kLoop, calls=%fused_computation.18 | loop fusion | flops 10485760 | bytes 33555584 | tf_op jit(solution)/shard_map/sub | solution.py:75
  213.3 4.7 %slice.167 = f32[128,31,256]{0,2,1:T(8,128)} slice(f32[128,32,256]{0,2,1:T(8,128)} %copy-done.7), slice={[0:128], [1:32], [0:256]} | slice | bytes 8126464 | tf_op jit(solution)/shard_map/slice | solution.py:81
  218.4 5.2 %fusion.9 = (f32[1,128,32,256]{1,3,2,0:T(8,128)S(1)}, f32[1,128,32,256]{1,3,2,0:T(8,128)}) fusion(f32[128,32,256]{0,2,1:T(8,128)S(1)} %copy-done.8, f32[128,1,256]{0,2,1:T(8,128)S(1)} %convert_element_type.57, f32[128,31,256]{0,2,1:T(8,128)} %slice.167, f32[32]{0:T(128)S(1)} %compare_convert_fusion.1, f32[256]{0:T(256)S(1)} %compare_convert_fusion, ...), kind=kLoop, calls=%fused_computation.22 | loop fusion | flops 6291456 | bytes 20972672 | tf_op jit(solution)/shard_map/stack | solution.py:83
  241.0 4.5 %slice.173 = f32[128,31,256]{0,2,1:T(8,128)} slice(f32[128,32,256]{0,2,1:T(8,128)} %get-tuple-element.13), slice={[0:128], [0:31], [0:256]} | slice | bytes 8126464 | tf_op jit(solution)/shard_map/slice | solution.py:73
  256.3 4.4 %fusion.16 = (f32[1,128,32,256]{1,3,2,0:T(8,128)}, f32[1,128,32,256]{1,3,2,0:T(8,128)}) fusion(f32[128,32,256]{0,2,1:T(8,128)S(1)} %fusion.14, f32[128,1,256]{0,2,1:T(8,128)S(1)} %convert_element_type.59, f32[128,31,256]{0,2,1:T(8,128)S(1)} %slice.177, f32[32]{0:T(128)S(1)} %compare_convert_fusion.1, f32[256]{0:T(256)S(1)} %compare_convert_fusion, ...), kind=kLoop, calls=%fused_computation.33 | loop fusion | flops 6291456 | bytes 20972672 | tf_op jit(solution)/shard_map/stack | solution.py:83
  260.7 8.3 %fusion.2 = f32[2,128,32,256]{1,3,2,0:T(8,128)S(1)} fusion(f32[1,128,32,256]{1,3,2,0:T(8,128)} %get-tuple-element.19, f32[1,128,32,256]{1,3,2,0:T(8,128)} %get-tuple-element.18, f32[1,128,32,256]{1,3,2,0:T(8,128)} %get-tuple-element.21, f32[1,128,32,256]{1,3,2,0:T(8,128)} %copy-done.6, f32[1,128,32,256]{1,3,2,0:T(8,128)S(1)} %get-tuple-element.22, ...), kind=kLoop, calls=%fused_computation.5 | loop fusion | flops 18874368 | bytes 33554432 | tf_op jit(solution)/shard_map/jit(clip)/min | solution.py:83
  281.1 4.5 %slice.183 = f32[128,31,256]{0,2,1:T(8,128)} slice(f32[128,32,256]{0,2,1:T(8,128)} %get-tuple-element.11), slice={[0:128], [0:31], [0:256]} | slice | bytes 8126464 | tf_op jit(solution)/shard_map/slice | solution.py:73
  300.8 11.3 %fusion.4 = f32[2,128,32,256]{1,3,2,0:T(8,128)S(1)} fusion(f32[1,128,32,256]{1,3,2,0:T(8,128)} %get-tuple-element.17, f32[1,128,32,256]{1,3,2,0:T(8,128)} %get-tuple-element.16, f32[1,128,32,256]{1,3,2,0:T(8,128)} %get-tuple-element.19, f32[1,128,32,256]{1,3,2,0:T(8,128)} %get-tuple-element.18, f32[1,128,32,256]{1,3,2,0:T(8,128)} %get-tuple-element.21, ...), kind=kLoop, calls=%fused_computation.8 | loop fusion | flops 27262976 | bytes 41943040 | tf_op jit(solution)/shard_map/jit(clip)/min | solution.py:83
  321.6 10.2 %copy.34 = f32[2,128,32,256]{3,2,1,0:T(8,128)} copy(f32[2,128,32,256]{1,3,2,0:T(8,128)} %copy-done) | data formatting | bytes 16777216
  335.3 7.0 %fusion.30 = f32[128,32,256]{0,2,1:T(8,128)} fusion(f32[128,32,256]{0,2,1:T(8,128)S(1)} %copy-done.4, f32[128,31,256]{0,2,1:T(8,128)S(1)} %slice.193, f32[128,1,256]{0,2,1:T(8,128)S(1)} %convert_element_type.62, f32[128,32,255]{0,2,1:T(8,128)} %bitcast.84, f32[128,32,1]{0,2,1:T(1,128)S(1)} %bitcast.103, f32[2,128,32,256]{1,3,2,0:T(8,128)} %copy-done), kind=kLoop, calls=%fused_computation.53 | loop fusion | flops 9437184 | bytes 25165824 | tf_op jit(solution)/shard_map/max | solution.py:85
  342.3 5.4 %copy.33 = f32[128,32,256]{2,1,0:T(8,128)} copy(f32[128,32,256]{0,2,1:T(8,128)} %fusion.30) | data formatting | bytes 8388608
  (105 shorter events, 108.2 us)
Async XLA Ops:
  7.2 84.1 %reduce-scatter.3.cloned.1.call-start = ((), (), s32[]{:S(2)}) async-start(), calls=%async_computation.4 | async-start | bytes 9175040 | tf_op jit(solution)/shard_map/reduce_scatter | solution.py:14
  15.4 111.9 %reduce-scatter.5.cloned.1.call-start = ((), (), s32[]{:S(2)}) async-start(), calls=%async_computation.5 | async-start | bytes 2752512 | tf_op jit(solution)/shard_map/reduce_scatter | solution.py:14
  92.2 14.9 %all-to-all-start = ((bf16[8,224,128]{2,1,0:T(8,128)(2,1)}), bf16[8,224,128]{2,1,0:T(8,128)(2,1)S(1)}, u32[]{:S(2)}, u32[]{:S(2)}) async-start(bf16[8,224,128]{2,1,0:T(8,128)(2,1)} %broadcast_in_dim.2), calls=%async_computation.2 | async-start | bytes 917504 | tf_op jit(solution)/shard_map/all_to_all | solution.py:26
  136.9 55.1 %all-to-all-start.1 = ((f32[8,128,1024]{1,2,0:T(8,128)}), f32[8,128,1024]{1,2,0:T(8,128)}, u32[]{:S(2)}, u32[]{:S(2)}) async-start(f32[8,128,1024]{1,2,0:T(8,128)} %copy.15), calls=%async_computation.3 | async-start | bytes 8388608 | tf_op jit(solution)/shard_map/all_to_all | solution.py:67
  160.0 26.2 %collective-permute-start = (bf16[128,1,256]{0,2,1:T(8,128)(2,1)S(1)}, bf16[128,1,256]{0,2,1:T(8,128)(2,1)S(1)}, u32[]{:S(2)}, u32[]{:S(2)}) collective-permute-start(bf16[128,1,256]{0,2,1:T(8,128)(2,1)S(1)} %slice.228), channel_id=1, source_target_pairs={{0,4},{4,8},{8,12},{1,5},{5,9},{9,13},{2,6},{6,10},{10,14},{3,7},{... | collective-permute-start | bytes 196616 | tf_op jit(solution)/shard_map/ppermute | solution.py:42
  173.3 23.5 %collective-permute-start.1 = (f32[128,32,1]{0,1,2:T(8,128)S(1)}, f32[128,32,1]{0,1,2:T(8,128)S(1)}, u32[]{:S(2)}, u32[]{:S(2)}) collective-permute-start(f32[128,32,1]{0,1,2:T(8,128)S(1)} %bitcast.95), channel_id=1, source_target_pairs={{0,1},{1,2},{2,3},{4,5},{5,6},{6,7},{8,9},{9,10},{10,11},{12,13},{... | collective-permute-start | bytes 49160 | tf_op jit(solution)/shard_map/ppermute | solution.py:42
  192.0 4.9 %copy-start.1 = (f32[1,128,32,256]{1,3,2,0:T(8,128)S(1)}, f32[1,128,32,256]{1,3,2,0:T(8,128)}, u32[]{:S(2)}) copy-start(f32[1,128,32,256]{1,3,2,0:T(8,128)} %copy.35) | copy-start | bytes 12582916
  192.0 6.2 %copy-start.2 = (f32[1,128,32,256]{1,3,2,0:T(8,128)S(1)}, f32[1,128,32,256]{1,3,2,0:T(8,128)}, u32[]{:S(2)}) copy-start(f32[1,128,32,256]{1,3,2,0:T(8,128)} %copy.36) | copy-start | bytes 12582916
  205.4 80.3 %copy-start.3 = (f32[128,32,256]{0,2,1:T(8,128)}, f32[128,32,256]{0,2,1:T(8,128)S(1)}, u32[]{:S(2)}) copy-start(f32[128,32,256]{0,2,1:T(8,128)S(1)} %get-tuple-element.7) | copy-start | bytes 12582916
  205.4 13.0 %collective-permute-start.3 = (f32[128,32,1]{0,1,2:T(8,128)S(1)}, f32[128,32,1]{0,1,2:T(8,128)S(1)}, u32[]{:S(2)}, u32[]{:S(2)}) collective-permute-start(f32[128,32,1]{0,1,2:T(8,128)S(1)} %bitcast.94), channel_id=1, source_target_pairs={{1,0},{2,1},{3,2},{5,4},{6,5},{7,6},{9,8},{10,9},{11,10},{13,12},{... | collective-permute-start | bytes 49160 | tf_op jit(solution)/shard_map/ppermute | solution.py:42
  208.8 9.6 %collective-permute-start.2 = (bf16[128,1,256]{0,2,1:T(8,128)(2,1)S(1)}, bf16[128,1,256]{0,2,1:T(8,128)(2,1)S(1)}, u32[]{:S(2)}, u32[]{:S(2)}) collective-permute-start(bf16[128,1,256]{0,2,1:T(8,128)(2,1)S(1)} %slice.227), channel_id=1, source_target_pairs={{4,0},{8,4},{12,8},{5,1},{9,5},{13,9},{6,2},{10,6},{14,10},{7,3},{... | collective-permute-start | bytes 196616 | tf_op jit(solution)/shard_map/ppermute | solution.py:42
  213.3 4.7 %copy-start.8 = (f32[128,32,256]{0,2,1:T(8,128)S(1)}, f32[128,32,256]{0,2,1:T(8,128)}, u32[]{:S(2)}) copy-start(f32[128,32,256]{0,2,1:T(8,128)} %copy-done.7) | copy-start | bytes 12582916
  218.4 7.3 %copy-start.5 = (f32[1,128,32,256]{1,3,2,0:T(8,128)S(1)}, f32[1,128,32,256]{1,3,2,0:T(8,128)}, u32[]{:S(2)}) copy-start(f32[1,128,32,256]{1,3,2,0:T(8,128)} %get-tuple-element.23) | copy-start | bytes 12582916
  233.4 12.1 %collective-permute-start.4 = (bf16[128,1,256]{0,2,1:T(8,128)(2,1)S(1)}, bf16[128,1,256]{0,2,1:T(8,128)(2,1)S(1)}, u32[]{:S(2)}, u32[]{:S(2)}) collective-permute-start(bf16[128,1,256]{0,2,1:T(8,128)(2,1)S(1)} %slice.226), channel_id=1, source_target_pairs={{0,4},{4,8},{8,12},{1,5},{5,9},{9,13},{2,6},{6,10},{10,14},{3,7},{... | collective-permute-start | bytes 196616 | tf_op jit(solution)/shard_map/ppermute | solution.py:42
  238.3 7.2 %collective-permute-start.5 = (f32[128,32,1]{0,1,2:T(8,128)S(1)}, f32[128,32,1]{0,1,2:T(8,128)S(1)}, u32[]{:S(2)}, u32[]{:S(2)}) collective-permute-start(f32[128,32,1]{0,1,2:T(8,128)S(1)} %bitcast.97), channel_id=1, source_target_pairs={{0,1},{1,2},{2,3},{4,5},{5,6},{6,7},{8,9},{9,10},{10,11},{12,13},{... | collective-permute-start | bytes 49160 | tf_op jit(solution)/shard_map/ppermute | solution.py:42
  249.9 5.9 %collective-permute-start.6 = (bf16[128,1,256]{0,2,1:T(8,128)(2,1)S(1)}, bf16[128,1,256]{0,2,1:T(8,128)(2,1)S(1)}, u32[]{:S(2)}, u32[]{:S(2)}) collective-permute-start(bf16[128,1,256]{0,2,1:T(8,128)(2,1)S(1)} %slice.225), channel_id=1, source_target_pairs={{4,0},{8,4},{12,8},{5,1},{9,5},{13,9},{6,2},{10,6},{14,10},{7,3},{... | collective-permute-start | bytes 196616 | tf_op jit(solution)/shard_map/ppermute | solution.py:42
  251.2 5.1 %collective-permute-start.7 = (f32[128,32,1]{0,1,2:T(8,128)S(1)}, f32[128,32,1]{0,1,2:T(8,128)S(1)}, u32[]{:S(2)}, u32[]{:S(2)}) collective-permute-start(f32[128,32,1]{0,1,2:T(8,128)S(1)} %bitcast.98), channel_id=1, source_target_pairs={{1,0},{2,1},{3,2},{5,4},{6,5},{7,6},{9,8},{10,9},{11,10},{13,12},{... | collective-permute-start | bytes 49160 | tf_op jit(solution)/shard_map/ppermute | solution.py:42
  273.7 11.9 %collective-permute-start.8 = (bf16[128,1,256]{0,2,1:T(8,128)(2,1)S(1)}, bf16[128,1,256]{0,2,1:T(8,128)(2,1)S(1)}, u32[]{:S(2)}, u32[]{:S(2)}) collective-permute-start(bf16[128,1,256]{0,2,1:T(8,128)(2,1)S(1)} %slice.224), channel_id=1, source_target_pairs={{0,4},{4,8},{8,12},{1,5},{5,9},{9,13},{2,6},{6,10},{10,14},{3,7},{... | collective-permute-start | bytes 196616 | tf_op jit(solution)/shard_map/ppermute | solution.py:42
  278.6 7.0 %collective-permute-start.9 = (f32[128,32,1]{0,1,2:T(8,128)S(1)}, f32[128,32,1]{0,1,2:T(8,128)S(1)}, u32[]{:S(2)}, u32[]{:S(2)}) collective-permute-start(f32[128,32,1]{0,1,2:T(8,128)S(1)} %bitcast.99), channel_id=1, source_target_pairs={{0,1},{1,2},{2,3},{4,5},{5,6},{6,7},{8,9},{9,10},{10,11},{12,13},{... | collective-permute-start | bytes 49160 | tf_op jit(solution)/shard_map/ppermute | solution.py:42
  290.0 5.4 %collective-permute-start.10 = (bf16[128,1,256]{0,2,1:T(8,128)(2,1)S(1)}, bf16[128,1,256]{0,2,1:T(8,128)(2,1)S(1)}, u32[]{:S(2)}, u32[]{:S(2)}) collective-permute-start(bf16[128,1,256]{0,2,1:T(8,128)(2,1)S(1)} %slice.223), channel_id=1, source_target_pairs={{4,0},{8,4},{12,8},{5,1},{9,5},{13,9},{6,2},{10,6},{14,10},{7,3},{... | collective-permute-start | bytes 196616 | tf_op jit(solution)/shard_map/ppermute | solution.py:42
  291.4 5.1 %collective-permute-start.11 = (f32[128,32,1]{0,1,2:T(8,128)S(1)}, f32[128,32,1]{0,1,2:T(8,128)S(1)}, u32[]{:S(2)}, u32[]{:S(2)}) collective-permute-start(f32[128,32,1]{0,1,2:T(8,128)S(1)} %bitcast.100), channel_id=1, source_target_pairs={{1,0},{2,1},{3,2},{5,4},{6,5},{7,6},{9,8},{10,9},{11,10},{13,12},{... | collective-permute-start | bytes 49160 | tf_op jit(solution)/shard_map/ppermute | solution.py:42
  315.4 4.1 %copy-start.12 = (f32[128,32,256]{0,2,1:T(8,128)}, f32[128,32,256]{0,2,1:T(8,128)S(1)}, u32[]{:S(2)}) copy-start(f32[128,32,256]{0,2,1:T(8,128)S(1)} %get-tuple-element.9) | copy-start | bytes 12582916
  315.4 19.2 %collective-permute-start.12 = (bf16[128,1,256]{0,2,1:T(8,128)(2,1)S(1)}, bf16[128,1,256]{0,2,1:T(8,128)(2,1)S(1)}, u32[]{:S(2)}, u32[]{:S(2)}) collective-permute-start(bf16[128,1,256]{0,2,1:T(8,128)(2,1)S(1)} %slice.222), channel_id=1, source_target_pairs={{0,4},{4,8},{8,12},{1,5},{5,9},{9,13},{2,6},{6,10},{10,14},{3,7},{... | collective-permute-start | bytes 196616 | tf_op jit(solution)/shard_map/ppermute | solution.py:42
  319.4 15.2 %collective-permute-start.13 = (f32[128,32,1]{0,1,2:T(8,128)S(1)}, f32[128,32,1]{0,1,2:T(8,128)S(1)}, u32[]{:S(2)}, u32[]{:S(2)}) collective-permute-start(f32[128,32,1]{0,1,2:T(8,128)S(1)} %bitcast.96), channel_id=1, source_target_pairs={{0,1},{1,2},{2,3},{4,5},{5,6},{6,7},{8,9},{9,10},{10,11},{12,13},{... | collective-permute-start | bytes 49160 | tf_op jit(solution)/shard_map/ppermute | solution.py:42
  (8 other events, 24.3 us)
Sparse Core Ops, SparseCore 0:
  15.5 75.7 reduce-scatter.2
  93.7 33.5 reduce-scatter.4
where the time goes:
time: 356 us; the launch traced here: 355 us
  waiting for transfers between devices  108 us (30%)
  local copies, waits for them, and re-layouts  102 us (29%)
  other arithmetic  75.3 us (21%)
  starting transfers between devices  46.3 us (13%)
  between operations  14.6 us (4%)
  matrix products  8.38 us (2%)
    reduce_scatter x2, waiting for transfers between devices, sum_by_axis(): nearer = lax.psum_scatter(array, axes[0], scatter_dimension=dim, tiled=True)  96.1 us
    unnamed x35, local copies, waits for them, and re-layouts  52 us
    ppermute x14, starting transfers between devices, shifted(): return lax.ppermute(array, axis, pairs)  36.8 us
    min x3, other arithmetic, on_device(): dual = jnp.clip(dual + 0.5 * jnp.stack([down, right]), -1.0, 1.0)  22.5 us
    slice x4, local copies, waits for them, and re-layouts, inner_field(): first_prev = jnp.concatenate([above, current[0][:, :height - 1, :]], axis=1)  16.3 us
    sub x3, other arithmetic, inner_field(): return start - 0.25 * (current[0] - first_prev + (current[1] - second_prev))  15.9 us
    another operation x3, other arithmetic, on_device(): dual = jnp.clip(dual + 0.5 * jnp.stack([down, right]), -1.0, 1.0)  13.9 us
    squeeze x3, local copies, waits for them, and re-layouts, inner_field(): return start - 0.25 * (current[0] - first_prev + (current[1] - second_prev))  8.61 us
  transfers between devices with their start and end apart: 18, of which 8 were waited for; matrix products, arithmetic and copies ran while one was open for 23% of the time, Pallas kernels for 0%

commit v1 on v0

v1 whole, which is shorter than its diff:
```python
import functools

import jax
import jax.numpy as jnp
from jax import lax
from jax.experimental import pallas as pl
from jax.experimental.pallas import tpu as pltpu
from jax.sharding import Mesh
from jax.sharding import PartitionSpec as P

PASSES = 3
LIB = ("lib_0", "lib_1")
BF16 = jnp.bfloat16
F32 = jnp.float32
LIMIT = 56 * 1024 * 1024
WHOLE = pl.BlockSpec(memory_space=pltpu.VMEM)
SCALARS = pl.BlockSpec(memory_space=pltpu.SMEM)
HOPS = ((2, 0), (2, 1), (1, 0), (3, 0), (1, 1), (3, 1), (0, 1))


def to_lib(array, hop):
    dy, dx = hop
    pairs = [(y * 2 + x, (y + dy) % 4 * 2 + (x ^ dx)) for y in range(4) for x in range(2)]
    return lax.ppermute(array, LIB, pairs)


def shifted(array, axis, by):
    length = lax.axis_size(axis)
    pairs = [(i, i + by) for i in range(length) if 0 <= i + by < length]
    return lax.ppermute(array, axis, pairs)


def shifted_both(array, down, right):
    rows, cols = lax.axis_size("row"), lax.axis_size("col")
    pairs = [
        (r * cols + c, (r + down) * cols + c + right)
        for r in range(rows)
        for c in range(cols)
        if 0 <= r + down < rows and 0 <= c + right < cols
    ]
    return lax.ppermute(array, ("row", "col"), pairs)


def resid_kernel(place, blocks_and_more):
    *blocks, library, observed, out = blocks_and_more
    for r in range(out.shape[0]):
        total = -observed[r].astype(F32)
        for k, block in enumerate(blocks):
            total += jnp.dot(library[place[k]], block[r], preferred_element_type=F32)
        out[r] = total.astype(BF16)


def residual(place, blocks, library, observed):
    return pl.pallas_call(
        lambda place, *refs: resid_kernel(place, refs),
        out_shape=jax.ShapeDtypeStruct(observed.shape, BF16),
        in_specs=[SCALARS] + [WHOLE] * (len(blocks) + 2),
        out_specs=WHOLE,
        compiler_params=pltpu.CompilerParams(vmem_limit_bytes=LIMIT),
        name="residual",
    )(place, *blocks, library, observed)


def gathered(mine):
    half = mine.shape[0] // 2
    a, b = mine[:half], mine[half:]
    up, down, across = (1, 0), (3, 0), (0, 1)
    bu, bd = to_lib(b, up), to_lib(b, down)
    ax = to_lib(a, across)
    au, ad = to_lib(a, up), to_lib(a, down)
    axu, axd = to_lib(ax, up), to_lib(ax, down)
    b2u, b2d = to_lib(bu[: half // 2], up), to_lib(bd[half // 2 :], down)
    a2, ax2 = to_lib(au, up), to_lib(axd, down)
    pieces = [
        (a, (0, 0), 0),
        (ax, (0, 1), 0),
        (au, (3, 0), 0),
        (ad, (1, 0), 0),
        (axu, (3, 1), 0),
        (axd, (1, 1), 0),
        (a2, (2, 0), 0),
        (ax2, (2, 1), 0),
    ]
    second = [
        (b, (0, 0), half),
        (bu, (3, 0), half),
        (bd, (1, 0), half),
        (b2u, (2, 0), half),
        (b2d, (2, 0), half + half // 2),
    ]
    pieces += second
    pieces += [(to_lib(v, across), (dy, 1), first) for v, (dy, _), first in second]
    return pieces


def descent_kernel(firsts, refs):
    *pieces, library_t, out = refs
    for k, piece in enumerate(pieces):
        for r in range(piece.shape[0]):
            d = jnp.dot(library_t[...], piece[r], preferred_element_type=F32)
            out[firsts[k] + r, 0] = d[:, :128]
            out[firsts[k] + r, 1] = d[:, 128:]


def descent(firsts, pieces, library_t, rows):
    maps = library_t.shape[0]
    return pl.pallas_call(
        lambda firsts, *refs: descent_kernel(firsts, refs),
        out_shape=jax.ShapeDtypeStruct((rows, 2, maps, 128), F32),
        in_specs=[SCALARS] + [WHOLE] * (len(pieces) + 1),
        out_specs=WHOLE,
        compiler_params=pltpu.CompilerParams(vmem_limit_bytes=LIMIT),
        cost_estimate=pl.CostEstimate(flops=2 * 224 * 128 * 8192, bytes_accessed=8_000_000, transcendentals=0),
        name="descent",
    )(firsts, *pieces, library_t)


def edges_kernel(d_ref, first_ref, last_ref, strip_ref):
    rows = d_ref.shape[0]
    first_ref[...] = d_ref[:4].astype(BF16)
    last_ref[...] = d_ref[rows - 4 :].astype(BF16)
    sub = lax.broadcasted_iota(jnp.int32, (8, 128), 0)

    def one(r, _):
        left = d_ref[r, 0].T[:8]
        right = d_ref[r, 1].T[120:]
        strip_ref[r] = pltpu.roll(jnp.where(sub < 4, left, right), 4, 0)
        return 0

    lax.fori_loop(0, rows, one, 0)


def edges(d):
    rows, _, maps, _ = d.shape
    band = jax.ShapeDtypeStruct((4, 2, maps, 128), BF16)
    return pl.pallas_call(
        edges_kernel,
        out_shape=(band, band, jax.ShapeDtypeStruct((rows, 8, maps), F32)),
        in_specs=[WHOLE],
        out_specs=(WHOLE,) * 3,
        compiler_params=pltpu.CompilerParams(vmem_limit_bytes=LIMIT),
        name="edges",
    )(d)


def below_then_above(array, dim, reach=4):
    size = array.shape[dim]
    below = shifted(lax.slice_in_dim(array, 0, reach, axis=dim), "row", -1)
    above = shifted(lax.slice_in_dim(array, size - reach, size, axis=dim), "row", 1)
    return lax.concatenate([below, above], dim)


def strips_two_steps(own):
    dim = own.ndim - 3
    tall = lax.concatenate([own, below_then_above(own, dim)], dim)
    return tall, shifted(tall, "col", 1), shifted(tall, "col", -1)


def strips_one_step(own):
    dim = own.ndim - 3
    rows = own.shape[dim]
    first = lax.slice_in_dim(own, 0, 4, axis=dim)
    last = lax.slice_in_dim(own, rows - 4, rows, axis=dim)

    def tall(right):
        middle = shifted(own, "col", right) if right else own
        return lax.concatenate(
            [middle, shifted_both(first, -1, right), shifted_both(last, 1, right)], dim
        )

    return tall(0), tall(1), tall(-1)


def tv_kernel(
    origin,
    ab_ref,
    q_ref,
    rim_ref,
    d_ref,
    drim_ref,
    own_ref,
    left_ref,
    right_ref,
    down_ref,
    dleft_ref,
    dright_ref,
    abn_ref,
    qn_ref,
    lefts,
    rights,
    turn,
):
    block, rows, _ = ab_ref.shape
    tall = rows + 8
    maps = own_ref.shape[-1]
    first_row, first_col, total_rows, total_cols = (origin[i] for i in range(4))

    def row_bound(shape, axis):
        r = lax.broadcasted_iota(jnp.int32, shape, axis)
        g = first_row + jnp.where(r < rows + 4, r, r - tall)
        return jnp.where((g >= 0) & (g < total_rows - 1), 1.0, 0.0).astype(F32)

    @pl.when(pl.program_id(0) == 0)
    def _():
        b0 = row_bound((tall, 8, maps), 0)
        sub = lax.broadcasted_iota(jnp.int32, (tall, 8, maps), 1)

        def strip(nearer, further, offset, is_left):
            def pick(i):
                return jnp.where(sub < 4, nearer[i], further[i])

            g = first_col + offset + sub
            b1 = jnp.where((g >= 0) & (g < total_cols - 1), 1.0, 0.0).astype(F32)
            s = pick(0) - 0.1 * pick(3)
            u, v = jnp.clip(pick(1), -b0, b0), jnp.clip(pick(2), -b1, b1)
            for p in range(PASSES):
                if is_left:
                    turn[...] = v.reshape(tall * 8, maps)
                    lefts[p] = turn[pl.ds(3, tall, 8), :]
                uu = jnp.concatenate([u[tall - 1 :], u[: tall - 1]], axis=0)
                z = s - 0.25 * (u - uu + (v - pltpu.roll(v, 1, 1)))
                if not is_left:
                    turn[...] = z.reshape(tall * 8, maps)
                    rights[p] = turn[pl.ds(4, tall, 8), :]
                zd = jnp.concatenate([z[1:], z[:1]], axis=0)
                zr = pltpu.roll(z, 7, 1)
                u = jnp.clip(u + 0.5 * (zd - z), -b0, b0)
                v = jnp.clip(v + 0.5 * (zr - z), -b1, b1)
            if is_left:
                turn[...] = v.reshape(tall * 8, maps)
                lefts[PASSES] = turn[pl.ds(3, tall, 8), :]

        own = [own_ref[0], own_ref[1], own_ref[2], down_ref[...]]
        strip([left_ref[0], left_ref[1], left_ref[2], dleft_ref[...]], own, -4, True)
        strip(own, [right_ref[0], right_ref[1], right_ref[2], dright_ref[...]], 252, False)

    lane = lax.broadcasted_iota(jnp.int32, (tall, 128), 1)
    at_start, at_end = lane == 0, lane == 127
    b0 = row_bound((tall, 128), 0)
    b1 = jnp.where(first_col + 128 + lane < total_cols - 1, 1.0, 0.0).astype(F32)

    def one(m, _):
        gm = pl.program_id(0) * block + m
        s, u, v = [], [], []
        for c in range(2):
            cols = pl.ds(128 * c, 128)
            d = jnp.concatenate(
                [
                    d_ref[pl.ds(c * maps + gm, rows, 2 * maps), :],
                    drim_ref[pl.ds(c * maps + gm, 8, 2 * maps), :],
                ],
                axis=0,
            )
            s.append(jnp.concatenate([ab_ref[m, :, cols], rim_ref[0, m, :, cols]], axis=0) - 0.1 * d)
            u.append(jnp.clip(jnp.concatenate([q_ref[0, m, :, cols], rim_ref[1, m, :, cols]], axis=0), -b0, b0))
            v.append(jnp.concatenate([q_ref[1, m, :, cols], rim_ref[2, m, :, cols]], axis=0))
        v[1] = jnp.clip(v[1], -b1, b1)

        def field(p):
            edge = pltpu.roll(lefts[p], lax.rem(128 - gm, 128), 1)
            t0, t1 = pltpu.roll(v[0], 1, 1), pltpu.roll(v[1], 1, 1)
            before = [jnp.where(at_start, edge, t0), jnp.where(at_start, t0, t1)]
            return [s[c] - 0.25 * (u[c] - pltpu.roll(u[c], 1, 0) + (v[c] - before[c])) for c in range(2)]

        for p in range(PASSES):
            z = field(p)
            edge = pltpu.roll(rights[p], 127 - gm, 1)
            t0, t1 = pltpu.roll(z[0], 127, 1), pltpu.roll(z[1], 127, 1)
            after = [jnp.where(at_end, t1, t0), jnp.where(at_end, edge, t1)]
            u = [jnp.clip(u[c] + 0.5 * (pltpu.roll(z[c], tall - 1, 0) - z[c]), -b0, b0) for c in range(2)]
            v = [v[c] + 0.5 * (after[c] - z[c]) for c in range(2)]
            v = [jnp.clip(v[0], -1.0, 1.0), jnp.clip(v[1], -b1, b1)]
        z = field(PASSES)
        for c in range(2):
            cols = pl.ds(128 * c, 128)
            abn_ref[m, :, cols] = jnp.maximum(z[c][:rows] - 0.02, 0.0)
            qn_ref[0, m, :, cols] = u[c][:rows]
            qn_ref[1, m, :, cols] = v[c][:rows]
        return 0

    lax.fori_loop(0, block, one, 0)


def tv(origin, abundance, duals, rim, d, drim, strips, dstrips):
    maps, rows, cols = abundance.shape
    block = 8
    tile = pl.BlockSpec((block, rows, cols), lambda i: (i, 0, 0))
    pair = pl.BlockSpec((2, block, rows, cols), lambda i: (0, i, 0, 0))
    rims = pl.BlockSpec((3, block, 8, cols), lambda i: (0, i, 0, 0))
    tall = rows + 8
    return pl.pallas_call(
        tv_kernel,
        grid=(maps // block,),
        out_shape=(
            jax.ShapeDtypeStruct(abundance.shape, F32),
            jax.ShapeDtypeStruct(duals.shape, F32),
        ),
        in_specs=[SCALARS, tile, pair, rims] + [WHOLE] * 8,
        out_specs=(tile, pair),
        scratch_shapes=[
            pltpu.VMEM((PASSES + 1, tall, maps), F32),
            pltpu.VMEM((PASSES, tall, maps), F32),
            pltpu.VMEM((tall * 8, maps), F32),
        ],
        compiler_params=pltpu.CompilerParams(vmem_limit_bytes=LIMIT),
        name="tv",
    )(origin, abundance, duals, rim, d.reshape(-1, 128), drim.reshape(-1, 128), *strips, *dstrips)


def on_device(abundance, duals, reflectance, library):
    maps, height, width = abundance.shape
    y, x = lax.axis_index("lib_0"), lax.axis_index("lib_1")
    share = height // 8
    me = y * 2 + x
    whole_library = lax.all_gather(library, LIB, axis=0, tiled=False)

    compact = abundance.astype(BF16).transpose(1, 0, 2).reshape(8, share, maps, width)
    mine = lax.dynamic_index_in_dim(compact, me, 0, keepdims=False)
    blocks, place = [mine], [me]
    for dy, dx in HOPS:
        to = lax.rem(y + dy, 4) * 2 + (x + dx) % 2
        blocks.append(to_lib(lax.dynamic_index_in_dim(compact, to, 0, keepdims=False), (dy, dx)))
        place.append(lax.rem(y + 4 - dy, 4) * 2 + (x + dx) % 2)
    observed = lax.dynamic_slice_in_dim(reflectance, me * share, share, 1).transpose(1, 0, 2)
    rb = residual(jnp.stack(place), blocks, whole_library, observed)

    state = jnp.concatenate([abundance[None], duals], axis=0)
    first = lax.slice_in_dim(state, 0, 4, axis=2).astype(BF16)
    last = lax.slice_in_dim(state, height - 4, height, axis=2).astype(BF16)
    rim = lax.concatenate([shifted(first, "row", -1), shifted(last, "row", 1)], 2).astype(F32)
    columns = jnp.concatenate([state[..., width - 4 :], state[..., :4]], axis=3)
    strips = strips_two_steps(columns.transpose(0, 2, 3, 1))

    pieces = gathered(rb)
    firsts = [(lax.rem(y + dy, 4) * 2 + (x + dx) % 2) * share + row for _, (dy, dx), row in pieces]
    d = descent(jnp.stack(firsts), [piece for piece, _, _ in pieces], library.T, height)
    d_first, d_last, own = edges(d)
    drim = lax.concatenate([shifted(d_first, "row", -1), shifted(d_last, "row", 1)], 0).astype(F32)
    dstrips = strips_one_step(own)
    origin = jnp.stack(
        [
            lax.axis_index("row") * height,
            lax.axis_index("col") * width,
            height * lax.axis_size("row"),
            width * lax.axis_size("col"),
        ]
    )
    return tv(origin, abundance, duals, rim, d, drim, strips, dstrips)


def solution(mesh):
    torus = Mesh(
        mesh.devices.reshape(4, 2, mesh.shape["row"], mesh.shape["col"]),
        ("lib_0", "lib_1", "row", "col"),
    )
    placed = (P(LIB, "row", "col"), P(None, LIB, "row", "col"), P(None, "row", "col"), P(None, LIB))
    return jax.shard_map(
        on_device,
        mesh=torus,
        in_specs=placed,
        out_specs=(P(LIB, "row", "col"), P(None, LIB, "row", "col")),
        check_vma=False,
    )
```

time: 356 us -> 282 us (0.79)
  waiting for transfers between devices: 108 us -> 14.5 us
  Pallas kernels: 0 us -> 90.4 us
  local copies, waits for them, and re-layouts: 102 us -> 31.6 us
  other arithmetic: 75.3 us -> 17.9 us
  starting transfers between devices: 46.3 us -> 90.9 us
  blocking collectives: 0 us -> 33.8 us
  between operations: 14.6 us -> 1.35 us
  matrix products: 8.38 us -> 0 us
    reduce_scatter x2 -> x0, waiting for transfers between devices: 96.1 us -> none  [sum_by_axis(): nearer = lax.psum_scatter(array, axes[0], scatter_dimension=dim, tiled=True)]
    pallas_call x0 -> x4, Pallas kernels: none -> 90.4 us  [the longest x1 75.7 us: tv(): pl.pallas_call(tv_kernel, grid=(maps // block,), out_shape=(jax.ShapeDtyp...]
    ppermute x0 -> x29, starting transfers between devices: none -> 64.4 us  [the longest x23 35.2 us: to_lib(): return lax.ppermute(array, LIB, pairs)]
    all_gather x0 -> x1, blocking collectives: none -> 33.8 us  [on_device(): whole_library = lax.all_gather(library, LIB, axis=0, tiled=False)]
    slice x25 -> x6, local copies, waits for them, and re-layouts: 35.1 us -> 3.32 us  [the longest x1 1.47 us: on_device(): first = lax.slice_in_dim(state, 0, 4, axis=2).astype(BF16)]
    unnamed x35 -> x56, local copies, waits for them, and re-layouts: 52 us -> 20.9 us
    min x3 -> x0, other arithmetic: 22.5 us -> none  [on_device(): dual = jnp.clip(dual + 0.5 * jnp.stack([down, right]), -1.0, 1.0)]
    sub x3 -> x0, other arithmetic: 15.9 us -> none  [inner_field(): return start - 0.25 * (current[0] - first_prev + (current[1] - second_prev))]
  transfers between devices with their start and end apart: 18 -> 39, of which waited for: 8 -> 6; matrix products, arithmetic and copies ran while one was open for 23% -> 14% of each run, Pallas kernels for 0% -> 4%
where the time goes in v1:
time: 282 us; the launch traced here: 280 us
  starting transfers between devices  90.9 us (32%)
  Pallas kernels  90.4 us (32%)
  blocking collectives  33.8 us (12%)
  local copies, waits for them, and re-layouts  31.6 us (11%)
  other arithmetic  17.9 us (6%)
  waiting for transfers between devices  14.5 us (5%)
    pallas_call x1, Pallas kernels, tv(): pl.pallas_call(tv_kernel, grid=(maps // block,), out_shape=(jax.ShapeDtyp...  75.7 us
    ppermute x23, starting transfers between devices, to_lib(): return lax.ppermute(array, LIB, pairs)  35.2 us
    all_gather x1, blocking collectives, on_device(): whole_library = lax.all_gather(library, LIB, axis=0, tiled=False)  33.8 us
    ppermute x6, starting transfers between devices, shifted_both(): return lax.ppermute(array, ('row', 'col'), pairs)  29.2 us
    ppermute x10, starting transfers between devices, shifted(): return lax.ppermute(array, axis, pairs)  26.5 us
    unnamed x56, local copies, waits for them, and re-layouts  20.9 us
    another operation x1, other arithmetic  7.92 us
    ppermute x23, waiting for transfers between devices, to_lib(): return lax.ppermute(array, LIB, pairs)  7.26 us
  transfers between devices with their start and end apart: 39, of which 6 were waited for; matrix products, arithmetic and copies ran while one was open for 14% of the time, Pallas kernels for 4%

profile of v1, /device:TPU:1, one launch (start us, length us, event | category | flops | bytes accessed | tf_op | source)
XLA Modules:
  0.0 280.4 jit_solution(5410165791394468227)
XLA Ops:
  5.4 3.7 %collective-permute-start.2 = (bf16[4,128,256]{2,1,0:T(8,128)(2,1)}, bf16[4,128,256]{2,1,0:T(8,128)(2,1)S(1)}, u32[]{:S(2)}, u32[]{:S(2)}) collective-permute-start(bf16[4,128,256]{2,1,0:T(8,128)(2,1)} %get-tuple-element.18), channel_id=1, source_target_pairs={{0,64},{16,80},{32,96},{48,112},{64,0},{80,16},{96,32},{112,48},{1... | collective-permute-start | bytes 786440 | tf_op jit(solution)/shard_map/ppermute | solution.py:24
  14.4 5.3 %copy.6 = f32[128,32,256]{0,2,1:T(8,128)} copy(f32[128,32,256]{2,1,0:T(8,128)} %ab_ref.1) | data formatting | bytes 8388608 | tf_op args[0]
  19.7 10.0 %copy.7 = f32[2,128,32,256]{1,3,2,0:T(8,128)} copy(f32[2,128,32,256]{3,2,1,0:T(8,128)} %q_ref.1) | data formatting | bytes 16777216 | tf_op args[1]
  32.7 5.1 %collective-permute-start.7 = (bf16[4,128,256]{2,1,0:T(8,128)(2,1)S(1)}, bf16[4,128,256]{2,1,0:T(8,128)(2,1)S(1)}, u32[]{:S(2)}, u32[]{:S(2)}) collective-permute-start(bf16[4,128,256]{2,1,0:T(8,128)(2,1)S(1)} %get-tuple-element.13), channel_id=1, source_target_pairs={{0,112},{16,96},{32,16},{48,0},{64,48},{80,32},{96,80},{112,64},{1... | collective-permute-start | bytes 786440 | tf_op jit(solution)/shard_map/ppermute | solution.py:24
  39.3 33.8 %all-gather = bf16[1792,128]{1,0:T(8,128)(2,1)} all-gather(bf16[224,128]{1,0:T(8,128)(2,1)S(1)} %copy-done.14), channel_id=2, replica_groups=mesh['lib_0'=4,'lib_1'=2,'row'=4,'col'=4] {'lib_0','lib_1'}, dimensions={0}, use_global_device_ids=true | all-gather | bytes 516096 | tf_op jit(solution)/shard_map/all_gather | solution.py:315
  74.1 3.7 %residual.1 = bf16[4,224,256]{2,1,0:T(8,128)(2,1)} custom-call(s32[8]{0:T(128)} %stack.123.place, bf16[4,128,256]{2,1,0:T(8,128)(2,1)} %get-tuple-element.19.refs_0_, bf16[4,128,256]{2,1,0:T(8,128)(2,1)} %copy-done.7, bf16[4,128,256]{2,1,0:T(8,128)(2,1)} %copy-done.8, bf16[4,128,256]{2,1,0:T(8,128)(2,1)} %copy-done.9, bf16[4,128,256]{2,1,0:T(8,128)(2,1)} %copy-done.10, ...), custom_call_target="tpu_custom_call" | custom-call | tf_op jit(solution)/shard_map/residual/pallas_call | solution.py:54
  78.9 2.7 collective-permute-start.17
  81.7 3.5 %collective-permute-start.28 = (f32[3,4,8,128]{3,2,1,0:T(8,128)S(1)}, f32[3,4,8,128]{3,2,1,0:T(8,128)S(1)}, u32[]{:S(2)}, u32[]{:S(2)}) collective-permute-start(f32[3,4,8,128]{3,2,1,0:T(8,128)S(1)} %get-tuple-element.23), channel_id=1, source_target_pairs={{0,4},{4,8},{8,12},{1,5},{5,9},{9,13},{2,6},{6,10},{10,14},{3,7},{... | collective-permute-start | bytes 147464 | tf_op jit(solution)/shard_map/ppermute | solution.py:30
  86.5 3.0 %collective-permute-start.9 = (bf16[2,224,256]{2,1,0:T(8,128)(2,1)S(1)}, bf16[2,224,256]{2,1,0:T(8,128)(2,1)}, u32[]{:S(2)}, u32[]{:S(2)}) collective-permute-start(bf16[2,224,256]{2,1,0:T(8,128)(2,1)S(1)} %get-tuple-element.21.refs_0_), channel_id=1, source_target_pairs={{0,16},{16,0},{32,48},{48,32},{64,80},{80,64},{96,112},{112,96},{1... | collective-permute-start | bytes 688136 | tf_op jit(solution)/shard_map/ppermute | solution.py:24
  92.1 7.9 %fusion = bf16[3,128,32,256]{1,3,2,0:T(8,128)(2,1)} fusion(f32[2,128,32,256]{1,3,2,0:T(8,128)} %copy.7, f32[1,128,32,256]{1,3,2,0:T(8,128)} %bitcast.61), kind=kLoop, calls=%fused_computation.5 | loop fusion | flops 3145728 | bytes 18874368 | tf_op jit(solution)/shard_map/convert.2
  100.3 2.7 collective-permute-start.19
  107.8 4.2 %collective-permute-start.1 = (bf16[3,128,4,256]{1,3,2,0:T(8,128)(2,1)S(1)}, bf16[3,128,4,256]{1,3,2,0:T(8,128)(2,1)S(1)}, u32[]{:S(2)}, u32[]{:S(2)}) collective-permute-start(bf16[3,128,4,256]{1,3,2,0:T(8,128)(2,1)S(1)} %get-tuple-element.11), channel_id=1, source_target_pairs={{0,4},{4,8},{8,12},{1,5},{5,9},{9,13},{2,6},{6,10},{10,14},{3,7},{... | collective-permute-start | bytes 2359304 | tf_op jit(solution)/shard_map/ppermute | solution.py:30
  113.5 3.1 %collective-permute-start.21 = (bf16[2,224,256]{2,1,0:T(8,128)(2,1)S(1)}, bf16[2,224,256]{2,1,0:T(8,128)(2,1)}, u32[]{:S(2)}, u32[]{:S(2)}) collective-permute-start(bf16[2,224,256]{2,1,0:T(8,128)(2,1)S(1)} %collective-permute-done.16.refs_9_), channel_id=1, source_target_pairs={{0,16},{16,0},{32,48},{48,32},{64,80},{80,64},{96,112},{112,96},{1... | collective-permute-start | bytes 688136 | tf_op jit(solution)/shard_map/ppermute | solution.py:24
  122.5 2.7 collective-permute-start.23
  127.6 3.7 %collective-permute-done.24.refs_17_ = bf16[1,224,256]{2,1,0:T(8,128)(2,1)S(1)} collective-permute-done((bf16[1,224,256]{2,1,0:T(8,128)(2,1)}, bf16[1,224,256]{2,1,0:T(8,128)(2,1)S(1)}, u32[]{:S(2)}, u32[]{:S(2)}) %collective-permute-start.24) | collective-permute-done | bytes 114720 | tf_op jit(solution)/shard_map/ppermute | solution.py:24
  132.1 4.8 %descent.1.d_ref = f32[32,2,128,128]{3,2,1,0:T(8,128)} custom-call(s32[18]{0:T(128)} %stack.114.firsts, bf16[2,224,256]{2,1,0:T(8,128)(2,1)} %copy-done.1, bf16[2,224,256]{2,1,0:T(8,128)(2,1)} %collective-permute-done.9.refs_1_, bf16[2,224,256]{2,1,0:T(8,128)(2,1)} %copy-done.15, bf16[2,224,256]{2,1,0:T(8,128)(2,1)} %copy-done.16, ...), custom_call_target="tpu_custom_call" | custom-call | flops 469762048 | bytes 8000000 | tf_op jit(solution)/shard_map/descent/pallas_call | solution.py:107
  136.9 6.2 %edges.1 = (bf16[4,2,128,128]{3,2,1,0:T(8,128)(2,1)}, bf16[4,2,128,128]{3,2,1,0:T(8,128)(2,1)}, f32[32,8,128]{2,1,0:T(8,128)}) custom-call(f32[32,2,128,128]{3,2,1,0:T(8,128)} %descent.1.d_ref), custom_call_target="tpu_custom_call" | custom-call | tf_op jit(solution)/shard_map/edges/pallas_call | solution.py:136
  143.8 3.1 %collective-permute-start.32 = (f32[4,8,128]{2,1,0:T(8,128)S(1)}, f32[4,8,128]{2,1,0:T(8,128)S(1)}, u32[]{:S(2)}, u32[]{:S(2)}) collective-permute-start(f32[4,8,128]{2,1,0:T(8,128)S(1)} %get-tuple-element.25), channel_id=1, source_target_pairs={{0,4},{1,5},{2,6},{3,7},{4,8},{5,9},{6,10},{7,11},{8,12},{9,13},{1... | collective-permute-start | bytes 49160 | tf_op jit(solution)/shard_map/ppermute | solution.py:41
  146.9 18.4 %collective-permute-start.35 = (f32[4,8,128]{2,1,0:T(8,128)S(1)}, f32[4,8,128]{2,1,0:T(8,128)S(1)}, u32[]{:S(2)}, u32[]{:S(2)}) collective-permute-start(f32[4,8,128]{2,1,0:T(8,128)S(1)} %get-tuple-element.25), channel_id=1, source_target_pairs={{0,5},{1,6},{2,7},{4,9},{5,10},{6,11},{8,13},{9,14},{10,15},{16,21... | collective-permute-start | bytes 49160 | tf_op jit(solution)/shard_map/ppermute | solution.py:41
  175.8 5.3 %collective-permute-start.26 = (bf16[4,2,128,128]{3,2,1,0:T(8,128)(2,1)}, bf16[4,2,128,128]{3,2,1,0:T(8,128)(2,1)S(1)}, u32[]{:S(2)}, u32[]{:S(2)}) collective-permute-start(bf16[4,2,128,128]{3,2,1,0:T(8,128)(2,1)} %get-tuple-element.6), channel_id=1, source_target_pairs={{0,4},{4,8},{8,12},{1,5},{5,9},{9,13},{2,6},{6,10},{10,14},{3,7},{... | collective-permute-start | bytes 786440 | tf_op jit(solution)/shard_map/ppermute | solution.py:30
  183.2 3.9 %collective-permute-start.38 = (f32[4,8,128]{2,1,0:T(8,128)S(1)}, f32[4,8,128]{2,1,0:T(8,128)S(1)}, u32[]{:S(2)}, u32[]{:S(2)}) collective-permute-start(f32[4,8,128]{2,1,0:T(8,128)S(1)} %get-tuple-element.25), channel_id=1, source_target_pairs={{1,4},{2,5},{3,6},{5,8},{6,9},{7,10},{9,12},{10,13},{11,14},{17,20... | collective-permute-start | bytes 49160 | tf_op jit(solution)/shard_map/ppermute | solution.py:41
  189.1 3.8 %collective-permute-start.29 = (f32[3,40,8,128]{3,2,1,0:T(8,128)}, f32[3,40,8,128]{3,2,1,0:T(8,128)S(1)}, u32[]{:S(2)}, u32[]{:S(2)}) collective-permute-start(f32[3,40,8,128]{3,2,1,0:T(8,128)} %pad_maximum_fusion.2.own_ref), channel_id=1, source_target_pairs={{0,1},{1,2},{2,3},{4,5},{5,6},{6,7},{8,9},{9,10},{10,11},{12,13},{... | collective-permute-start | bytes 1474568 | tf_op jit(solution)/shard_map/ppermute | solution.py:30
  199.0 4.9 %collective-permute-done.30.right_ref = f32[3,40,8,128]{3,2,1,0:T(8,128)S(1)} collective-permute-done((f32[3,40,8,128]{3,2,1,0:T(8,128)}, f32[3,40,8,128]{3,2,1,0:T(8,128)S(1)}, u32[]{:S(2)}, u32[]{:S(2)}) %collective-permute-start.30) | collective-permute-done | bytes 491552 | tf_op jit(solution)/shard_map/ppermute | solution.py:30
  204.7 75.7 %tv.1 = (f32[128,32,256]{2,1,0:T(8,128)}, f32[2,128,32,256]{3,2,1,0:T(8,128)}) custom-call(s32[4]{0:T(128)} %pad_add_fusion.origin, f32[128,32,256]{2,1,0:T(8,128)} %ab_ref.1, f32[2,128,32,256]{3,2,1,0:T(8,128)} %q_ref.1, f32[3,128,8,256]{3,2,1,0:T(8,128)} %copy.18.rim_ref, f32[8192,128]{1,0:T(8,128)} %bitcast.59, f32[2048,128]{1,0:T(8,128)} %bitcast_convert_fusion.drim_ref, ...), custom_call_target="tpu_custom_call" | custom-call | tf_op jit(solution)/shard_map/tv/pallas_call | solution.py:291
  (139 shorter events, 57.9 us)
Async XLA Ops:
  5.4 27.3 %collective-permute-start.2 = (bf16[4,128,256]{2,1,0:T(8,128)(2,1)}, bf16[4,128,256]{2,1,0:T(8,128)(2,1)S(1)}, u32[]{:S(2)}, u32[]{:S(2)}) collective-permute-start(bf16[4,128,256]{2,1,0:T(8,128)(2,1)} %get-tuple-element.18), channel_id=1, source_target_pairs={{0,64},{16,80},{32,96},{48,112},{64,0},{80,16},{96,32},{112,48},{1... | collective-permute-start | bytes 786440 | tf_op jit(solution)/shard_map/ppermute | solution.py:24
  9.2 28.6 %collective-permute-start.3 = (bf16[4,128,256]{2,1,0:T(8,128)(2,1)}, bf16[4,128,256]{2,1,0:T(8,128)(2,1)S(1)}, u32[]{:S(2)}, u32[]{:S(2)}) collective-permute-start(bf16[4,128,256]{2,1,0:T(8,128)(2,1)} %get-tuple-element.17), channel_id=1, source_target_pairs={{0,80},{16,64},{32,112},{48,96},{64,16},{80,0},{96,48},{112,32},{1... | collective-permute-start | bytes 786440 | tf_op jit(solution)/shard_map/ppermute | solution.py:24
  11.7 61.3 %collective-permute-start.4 = (bf16[4,128,256]{2,1,0:T(8,128)(2,1)S(1)}, bf16[4,128,256]{2,1,0:T(8,128)(2,1)S(1)}, u32[]{:S(2)}, u32[]{:S(2)}) collective-permute-start(bf16[4,128,256]{2,1,0:T(8,128)(2,1)S(1)} %get-tuple-element.16), channel_id=1, source_target_pairs={{0,32},{16,48},{32,64},{48,80},{64,96},{80,112},{96,0},{112,16},{1... | collective-permute-start | bytes 786440 | tf_op jit(solution)/shard_map/ppermute | solution.py:24
  13.0 60.0 %collective-permute-start.5 = (bf16[4,128,256]{2,1,0:T(8,128)(2,1)S(1)}, bf16[4,128,256]{2,1,0:T(8,128)(2,1)S(1)}, u32[]{:S(2)}, u32[]{:S(2)}) collective-permute-start(bf16[4,128,256]{2,1,0:T(8,128)(2,1)S(1)} %get-tuple-element.15), channel_id=1, source_target_pairs={{0,96},{16,112},{32,0},{48,16},{64,32},{80,48},{96,64},{112,80},{1... | collective-permute-start | bytes 786440 | tf_op jit(solution)/shard_map/ppermute | solution.py:24
  14.4 58.6 %collective-permute-start.6 = (bf16[4,128,256]{2,1,0:T(8,128)(2,1)S(1)}, bf16[4,128,256]{2,1,0:T(8,128)(2,1)S(1)}, u32[]{:S(2)}, u32[]{:S(2)}) collective-permute-start(bf16[4,128,256]{2,1,0:T(8,128)(2,1)S(1)} %get-tuple-element.14), channel_id=1, source_target_pairs={{0,48},{16,32},{32,80},{48,64},{64,112},{80,96},{96,16},{112,0},{1... | collective-permute-start | bytes 786440 | tf_op jit(solution)/shard_map/ppermute | solution.py:24
  32.7 40.3 %collective-permute-start.7 = (bf16[4,128,256]{2,1,0:T(8,128)(2,1)S(1)}, bf16[4,128,256]{2,1,0:T(8,128)(2,1)S(1)}, u32[]{:S(2)}, u32[]{:S(2)}) collective-permute-start(bf16[4,128,256]{2,1,0:T(8,128)(2,1)S(1)} %get-tuple-element.13), channel_id=1, source_target_pairs={{0,112},{16,96},{32,16},{48,0},{64,48},{80,32},{96,80},{112,64},{1... | collective-permute-start | bytes 786440 | tf_op jit(solution)/shard_map/ppermute | solution.py:24
  37.8 35.3 %collective-permute-start.8 = (bf16[4,128,256]{2,1,0:T(8,128)(2,1)S(1)}, bf16[4,128,256]{2,1,0:T(8,128)(2,1)S(1)}, u32[]{:S(2)}, u32[]{:S(2)}) collective-permute-start(bf16[4,128,256]{2,1,0:T(8,128)(2,1)S(1)} %get-tuple-element.12), channel_id=1, source_target_pairs={{0,16},{16,0},{32,48},{48,32},{64,80},{80,64},{96,112},{112,96},{1... | collective-permute-start | bytes 786440 | tf_op jit(solution)/shard_map/ppermute | solution.py:24
  81.7 18.4 %collective-permute-start.28 = (f32[3,4,8,128]{3,2,1,0:T(8,128)S(1)}, f32[3,4,8,128]{3,2,1,0:T(8,128)S(1)}, u32[]{:S(2)}, u32[]{:S(2)}) collective-permute-start(f32[3,4,8,128]{3,2,1,0:T(8,128)S(1)} %get-tuple-element.23), channel_id=1, source_target_pairs={{0,4},{4,8},{8,12},{1,5},{5,9},{9,13},{2,6},{6,10},{10,14},{3,7},{... | collective-permute-start | bytes 147464 | tf_op jit(solution)/shard_map/ppermute | solution.py:30
  85.2 15.1 %collective-permute-start.27 = (f32[3,4,8,128]{3,2,1,0:T(8,128)S(1)}, f32[3,4,8,128]{3,2,1,0:T(8,128)S(1)}, u32[]{:S(2)}, u32[]{:S(2)}) collective-permute-start(f32[3,4,8,128]{3,2,1,0:T(8,128)S(1)} %get-tuple-element.22), channel_id=1, source_target_pairs={{4,0},{8,4},{12,8},{5,1},{9,5},{13,9},{6,2},{10,6},{14,10},{7,3},{... | collective-permute-start | bytes 147464 | tf_op jit(solution)/shard_map/ppermute | solution.py:30
  86.5 13.8 %collective-permute-start.9 = (bf16[2,224,256]{2,1,0:T(8,128)(2,1)S(1)}, bf16[2,224,256]{2,1,0:T(8,128)(2,1)}, u32[]{:S(2)}, u32[]{:S(2)}) collective-permute-start(bf16[2,224,256]{2,1,0:T(8,128)(2,1)S(1)} %get-tuple-element.21.refs_0_), channel_id=1, source_target_pairs={{0,16},{16,0},{32,48},{48,32},{64,80},{80,64},{96,112},{112,96},{1... | collective-permute-start | bytes 688136 | tf_op jit(solution)/shard_map/ppermute | solution.py:24
  89.4 13.5 %collective-permute-start.10 = (bf16[2,224,256]{2,1,0:T(8,128)(2,1)S(1)}, bf16[2,224,256]{2,1,0:T(8,128)(2,1)S(1)}, u32[]{:S(2)}, u32[]{:S(2)}) collective-permute-start(bf16[2,224,256]{2,1,0:T(8,128)(2,1)S(1)} %get-tuple-element.21.refs_0_), channel_id=1, source_target_pairs={{0,32},{16,48},{32,64},{48,80},{64,96},{80,112},{96,0},{112,16},{1... | collective-permute-start | bytes 688136 | tf_op jit(solution)/shard_map/ppermute | solution.py:24
  89.5 13.5 %collective-permute-start.11 = (bf16[2,224,256]{2,1,0:T(8,128)(2,1)S(1)}, bf16[2,224,256]{2,1,0:T(8,128)(2,1)S(1)}, u32[]{:S(2)}, u32[]{:S(2)}) collective-permute-start(bf16[2,224,256]{2,1,0:T(8,128)(2,1)S(1)} %get-tuple-element.21.refs_0_), channel_id=1, source_target_pairs={{0,96},{16,112},{32,0},{48,16},{64,32},{80,48},{96,64},{112,80},{1... | collective-permute-start | bytes 688136 | tf_op jit(solution)/shard_map/ppermute | solution.py:24
  100.3 11.8 %collective-permute-start.18 = (bf16[1,224,256]{2,1,0:T(8,128)(2,1)S(1)}, bf16[1,224,256]{2,1,0:T(8,128)(2,1)S(1)}, u32[]{:S(2)}, u32[]{:S(2)}) collective-permute-start(bf16[1,224,256]{2,1,0:T(8,128)(2,1)S(1)} %slice.54), channel_id=1, source_target_pairs={{0,32},{16,48},{32,64},{48,80},{64,96},{80,112},{96,0},{112,16},{1... | collective-permute-start | bytes 344072 | tf_op jit(solution)/shard_map/ppermute | solution.py:24
  100.3 13.1 %collective-permute-start.19 = (bf16[1,224,256]{2,1,0:T(8,128)(2,1)S(1)}, bf16[1,224,256]{2,1,0:T(8,128)(2,1)S(1)}, u32[]{:S(2)}, u32[]{:S(2)}) collective-permute-start(bf16[1,224,256]{2,1,0:T(8,128)(2,1)S(1)} %slice.55), channel_id=1, source_target_pairs={{0,96},{16,112},{32,0},{48,16},{64,32},{80,48},{96,64},{112,80},{1... | collective-permute-start | bytes 344072 | tf_op jit(solution)/shard_map/ppermute | solution.py:24
  103.7 13.0 %collective-permute-start.13 = (bf16[2,224,256]{2,1,0:T(8,128)(2,1)}, bf16[2,224,256]{2,1,0:T(8,128)(2,1)S(1)}, u32[]{:S(2)}, u32[]{:S(2)}) collective-permute-start(bf16[2,224,256]{2,1,0:T(8,128)(2,1)} %collective-permute-done.9.refs_1_), channel_id=1, source_target_pairs={{0,96},{16,112},{32,0},{48,16},{64,32},{80,48},{96,64},{112,80},{1... | collective-permute-start | bytes 688136 | tf_op jit(solution)/shard_map/ppermute | solution.py:24
  107.8 59.4 %collective-permute-start.1 = (bf16[3,128,4,256]{1,3,2,0:T(8,128)(2,1)S(1)}, bf16[3,128,4,256]{1,3,2,0:T(8,128)(2,1)S(1)}, u32[]{:S(2)}, u32[]{:S(2)}) collective-permute-start(bf16[3,128,4,256]{1,3,2,0:T(8,128)(2,1)S(1)} %get-tuple-element.11), channel_id=1, source_target_pairs={{0,4},{4,8},{8,12},{1,5},{5,9},{9,13},{2,6},{6,10},{10,14},{3,7},{... | collective-permute-start | bytes 2359304 | tf_op jit(solution)/shard_map/ppermute | solution.py:30
  112.1 56.5 %collective-permute-start = (bf16[3,128,4,256]{1,3,2,0:T(8,128)(2,1)S(1)}, bf16[3,128,4,256]{1,3,2,0:T(8,128)(2,1)}, u32[]{:S(2)}, u32[]{:S(2)}) collective-permute-start(bf16[3,128,4,256]{1,3,2,0:T(8,128)(2,1)S(1)} %get-tuple-element.10), channel_id=1, source_target_pairs={{4,0},{8,4},{12,8},{5,1},{9,5},{13,9},{6,2},{10,6},{14,10},{7,3},{... | collective-permute-start | bytes 2359304 | tf_op jit(solution)/shard_map/ppermute | solution.py:30
  143.8 30.0 %collective-permute-start.32 = (f32[4,8,128]{2,1,0:T(8,128)S(1)}, f32[4,8,128]{2,1,0:T(8,128)S(1)}, u32[]{:S(2)}, u32[]{:S(2)}) collective-permute-start(f32[4,8,128]{2,1,0:T(8,128)S(1)} %get-tuple-element.25), channel_id=1, source_target_pairs={{0,4},{1,5},{2,6},{3,7},{4,8},{5,9},{6,10},{7,11},{8,12},{9,13},{1... | collective-permute-start | bytes 49160 | tf_op jit(solution)/shard_map/ppermute | solution.py:41
  146.9 34.3 %collective-permute-start.35 = (f32[4,8,128]{2,1,0:T(8,128)S(1)}, f32[4,8,128]{2,1,0:T(8,128)S(1)}, u32[]{:S(2)}, u32[]{:S(2)}) collective-permute-start(f32[4,8,128]{2,1,0:T(8,128)S(1)} %get-tuple-element.25), channel_id=1, source_target_pairs={{0,5},{1,6},{2,7},{4,9},{5,10},{6,11},{8,13},{9,14},{10,15},{16,21... | collective-permute-start | bytes 49160 | tf_op jit(solution)/shard_map/ppermute | solution.py:41
  165.3 21.8 %collective-permute-start.33 = (f32[32,8,128]{2,1,0:T(8,128)}, f32[32,8,128]{2,1,0:T(8,128)S(1)}, u32[]{:S(2)}, u32[]{:S(2)}) collective-permute-start(f32[32,8,128]{2,1,0:T(8,128)} %get-tuple-element.7), channel_id=1, source_target_pairs={{0,1},{1,2},{2,3},{4,5},{5,6},{6,7},{8,9},{9,10},{10,11},{12,13},{... | collective-permute-start | bytes 393224 | tf_op jit(solution)/shard_map/ppermute | solution.py:30
  172.6 10.6 %collective-permute-start.34 = (f32[4,8,128]{2,1,0:T(8,128)S(1)}, f32[4,8,128]{2,1,0:T(8,128)S(1)}, u32[]{:S(2)}, u32[]{:S(2)}) collective-permute-start(f32[4,8,128]{2,1,0:T(8,128)S(1)} %get-tuple-element.24), channel_id=1, source_target_pairs={{4,1},{5,2},{6,3},{8,5},{9,6},{10,7},{12,9},{13,10},{14,11},{20,17... | collective-permute-start | bytes 49160 | tf_op jit(solution)/shard_map/ppermute | solution.py:41
  173.9 21.5 %collective-permute-start.36 = (f32[32,8,128]{2,1,0:T(8,128)S(1)}, f32[32,8,128]{2,1,0:T(8,128)S(1)}, u32[]{:S(2)}, u32[]{:S(2)}) collective-permute-start(f32[32,8,128]{2,1,0:T(8,128)S(1)} %copy-done.21), channel_id=1, source_target_pairs={{1,0},{2,1},{3,2},{5,4},{6,5},{7,6},{9,8},{10,9},{11,10},{13,12},{... | collective-permute-start | bytes 393224 | tf_op jit(solution)/shard_map/ppermute | solution.py:30
  175.8 20.3 %collective-permute-start.26 = (bf16[4,2,128,128]{3,2,1,0:T(8,128)(2,1)}, bf16[4,2,128,128]{3,2,1,0:T(8,128)(2,1)S(1)}, u32[]{:S(2)}, u32[]{:S(2)}) collective-permute-start(bf16[4,2,128,128]{3,2,1,0:T(8,128)(2,1)} %get-tuple-element.6), channel_id=1, source_target_pairs={{0,4},{4,8},{8,12},{1,5},{5,9},{9,13},{2,6},{6,10},{10,14},{3,7},{... | collective-permute-start | bytes 786440 | tf_op jit(solution)/shard_map/ppermute | solution.py:30
  181.2 14.9 %collective-permute-start.25 = (bf16[4,2,128,128]{3,2,1,0:T(8,128)(2,1)}, bf16[4,2,128,128]{3,2,1,0:T(8,128)(2,1)S(1)}, u32[]{:S(2)}, u32[]{:S(2)}) collective-permute-start(bf16[4,2,128,128]{3,2,1,0:T(8,128)(2,1)} %get-tuple-element.5), channel_id=1, source_target_pairs={{4,0},{8,4},{12,8},{5,1},{9,5},{13,9},{6,2},{10,6},{14,10},{7,3},{... | collective-permute-start | bytes 786440 | tf_op jit(solution)/shard_map/ppermute | solution.py:30
  (41 other events, 290.2 us)

commit v2 on v0

v2 whole, which is shorter than its diff:
```python
import functools

import jax
import jax.numpy as jnp
from jax import lax
from jax.experimental import pallas as pl
from jax.experimental.pallas import tpu as pltpu
from jax.sharding import Mesh
from jax.sharding import PartitionSpec as P

PASSES = 3
LIB = ("lib_0", "lib_1")
BF16 = jnp.bfloat16
F32 = jnp.float32
MIB = 1024 * 1024
WHOLE = pl.BlockSpec(memory_space=pltpu.VMEM)
SCALARS = pl.BlockSpec(memory_space=pltpu.SMEM)


def shifted(array, axis, by):
    length = lax.axis_size(axis)
    pairs = [(i, i + by) for i in range(length) if 0 <= i + by < length]
    return lax.ppermute(array, axis, pairs)


def to_all(array):
    return lax.all_to_all(array, LIB, 0, 0, tiled=True)


def tiles_of(array):
    *lead, rows, cols = array.shape
    n = len(lead)
    split = array.reshape(*lead, rows // 8, 8, cols // 128, 128)
    turned = split.transpose(*range(n), n, n + 2, n + 1, n + 3)
    return turned.reshape(*lead, rows // 8, cols // 16, 128)


def outer_columns(halves, lane, spot):
    joined = jnp.where(lane < 64, halves[0], halves[1])
    return pltpu.roll(joined, 4 + 8 * spot, 1)


def columns_of_eight(rows, maps):
    lane = lax.broadcasted_iota(jnp.int32, (maps, 128), 1)
    total = outer_columns(rows(0), lane, 0)
    for j in range(1, 8):
        total = jnp.where(lane // 8 == j, outer_columns(rows(j), lane, j), total)
    return total.T[:64]


def front_kernel(with_compact, *refs):
    in_ref, refs = refs[0], refs[1 if with_compact else 2 :]
    maps = in_ref.shape[-4]
    flat = in_ref.reshape(maps * 16, 128)

    def rows(j):
        return [flat[pl.ds(8 * c + j, maps, 16), :] for c in range(2)]

    if with_compact:
        library, out = refs[0], refs[1]
        share = (out.shape[1] - library.shape[0]) // maps
        for j in range(8):
            for c, half in enumerate(rows(j)):
                out[j // share, pl.ds(j % share * maps, maps), pl.ds(128 * c, 128)] = half.astype(BF16)
        for k in range(8 // share):
            out[k, pl.ds(share * maps, library.shape[0])] = library[...]
    else:
        step = pl.program_id(1)
        for at, out, start in ((0, refs[0], 0), (pl.num_programs(1) - 1, refs[1], 4)):

            @pl.when(step == at)
            def _():
                for j in range(4):
                    for c, half in enumerate(rows(start + j)):
                        out[0, j, :, pl.ds(128 * c, 128)] = half.astype(BF16)

    refs[-1][...] = columns_of_eight(rows, maps).reshape(refs[-1].shape)


def front_abundance(abundance, library):
    maps, height, width = abundance.shape
    share = height // 8
    flat = jnp.concatenate(jnp.split(library, 2), axis=1)
    length = share * maps + flat.shape[0]
    return pl.pallas_call(
        functools.partial(front_kernel, True),
        grid=(height // 8,),
        out_shape=(
            jax.ShapeDtypeStruct((8, length, width), BF16),
            jax.ShapeDtypeStruct((height, 8, maps), F32),
        ),
        in_specs=[pl.BlockSpec((maps, 1, 16, 128), lambda i: (0, i, 0, 0)), WHOLE],
        out_specs=(
            pl.BlockSpec((8 // share, length, width), lambda i: (i, 0, 0)),
            pl.BlockSpec((8, 8, maps), lambda i: (i, 0, 0)),
        ),
        compiler_params=pltpu.CompilerParams(vmem_limit_bytes=56 * MIB),
        name="front_abundance",
    )(tiles_of(abundance), flat)


def front_duals(duals, after):
    _, maps, height, width = duals.shape
    return pl.pallas_call(
        functools.partial(front_kernel, False),
        grid=(2, height // 8),
        out_shape=(
            jax.ShapeDtypeStruct((2, 4, maps, width), BF16),
            jax.ShapeDtypeStruct((2, 4, maps, width), BF16),
            jax.ShapeDtypeStruct((2, height, 8, maps), F32),
        ),
        in_specs=[
            pl.BlockSpec((1, maps, 1, 16, 128), lambda k, i: (k, 0, i, 0, 0)),
            pl.BlockSpec(memory_space=pl.ANY),
        ],
        out_specs=(
            pl.BlockSpec((1, 4, maps, width), lambda k, i: (k, 0, 0, 0)),
            pl.BlockSpec((1, 4, maps, width), lambda k, i: (k, 0, 0, 0)),
            pl.BlockSpec((1, 8, 8, maps), lambda k, i: (k, i, 0, 0)),
        ),
        compiler_params=pltpu.CompilerParams(vmem_limit_bytes=48 * MIB),
        cost_estimate=pl.CostEstimate(flops=0, bytes_accessed=8_000_000, transcendentals=0),
        name="front_duals",
    )(tiles_of(duals), after)


def middle_kernel(blocks, observed, *refs):
    descents = refs[-1]
    parts, share, maps, width = descents.shape
    start = share * maps

    def library(k):
        flat = blocks[k, start:]
        return jnp.concatenate([flat[:, :128], flat[:, 128:]])

    wide = jnp.concatenate([library(k) for k in range(parts)], axis=1)
    tall = jnp.concatenate([library(k).astype(F32).T.astype(BF16) for k in range(parts)])
    for r in range(share):
        pixels = jnp.concatenate([blocks[k, r * maps : r * maps + maps] for k in range(parts)])
        total = jnp.dot(wide, pixels, preferred_element_type=F32) - observed[r].astype(F32)
        d = jnp.dot(tall, total.astype(BF16), preferred_element_type=F32).astype(BF16)
        descents[:, r] = d.reshape(parts, maps, width)


def middle(blocks, observed, maps, first):
    share, _, width = observed.shape
    return pl.pallas_call(
        middle_kernel,
        out_shape=jax.ShapeDtypeStruct((8, share, maps, width), BF16),
        in_specs=[WHOLE] * 2 + [pl.BlockSpec(memory_space=pl.ANY)] * len(first),
        out_specs=WHOLE,
        compiler_params=pltpu.CompilerParams(vmem_limit_bytes=16 * MIB),
        name="middle",
    )(blocks, observed, *first)


def below_then_above(array, dim, reach=4):
    size = array.shape[dim]
    below = shifted(lax.slice_in_dim(array, 0, reach, axis=dim), "row", -1)
    above = shifted(lax.slice_in_dim(array, size - reach, size, axis=dim), "row", 1)
    return lax.concatenate([below, above], dim)


def columns_kernel(in_ref, out_ref):
    fields, rows, maps, _ = in_ref.shape
    for k in range(fields):
        for i in range(rows // 8):

            def pair(j):
                row = in_ref[k, 8 * i + j].astype(F32)
                return [row[:, :128], row[:, 128:]]

            out_ref[k, pl.ds(8 * i, 8)] = columns_of_eight(pair, maps).reshape(8, 8, maps)


def outer_columns_of(array, name):
    fields, rows, maps, _ = array.shape
    return pl.pallas_call(
        columns_kernel,
        out_shape=jax.ShapeDtypeStruct((fields, rows, 8, maps), F32),
        in_specs=[WHOLE],
        out_specs=WHOLE,
        compiler_params=pltpu.CompilerParams(vmem_limit_bytes=8 * MIB),
        name=name,
    )(array)


def beside(columns):
    return columns, shifted(columns, "col", 1), shifted(columns, "col", -1)


def tv_kernel(
    origin,
    ab_ref,
    q_ref,
    rim_ref,
    d_ref,
    drim_ref,
    own_ref,
    left_ref,
    right_ref,
    down_ref,
    dleft_ref,
    dright_ref,
    abn_ref,
    qn_ref,
    lefts,
    rights,
    turn,
):
    block = ab_ref.shape[0]
    rows = d_ref.shape[0]
    tall = rows + 8
    maps = own_ref.shape[-1]
    first_row, first_col, total_rows, total_cols = (origin[i] for i in range(4))

    @pl.when(pl.program_id(0) == 0)
    def _():
        r = lax.broadcasted_iota(jnp.int32, (tall, 8, maps), 0)
        g = first_row + jnp.where(r < rows + 4, r, r - tall)
        b0 = jnp.where((g >= 0) & (g < total_rows - 1), 1.0, 0.0).astype(F32)
        sub = lax.broadcasted_iota(jnp.int32, (tall, 8, maps), 1)

        def keep(out, values, at):
            turn[...] = values.reshape(tall * 8, maps)
            column = turn[pl.ds(at, tall, 8), :]
            out[...] = column

        def strip(nearer, further, dnearer, dfurther, offset, is_left):
            def pick(i):
                return jnp.where(sub < 4, nearer[i], further[i])

            g = first_col + offset + sub
            b1 = jnp.where((g >= 0) & (g < total_cols - 1), 1.0, 0.0).astype(F32)
            s = 0.5 * pick(0) - 0.05 * jnp.where(sub < 4, dnearer[0], dfurther[0])
            u, v = jnp.clip(pick(1), -b0, b0), jnp.clip(pick(2), -b1, b1)
            for p in range(PASSES):
                if is_left:
                    keep(lefts.at[p], v, 3)
                uu = jnp.concatenate([u[tall - 1 :], u[: tall - 1]], axis=0)
                z = s - 0.125 * (u - uu + (v - pltpu.roll(v, 1, 1)))
                if not is_left:
                    keep(rights.at[p], z, 4)
                zd = jnp.concatenate([z[1:], z[:1]], axis=0)
                zr = pltpu.roll(z, 7, 1)
                u = jnp.clip(u + (zd - z), -b0, b0)
                v = jnp.clip(v + (zr - z), -b1, b1)
            if is_left:
                keep(lefts.at[PASSES], v, 3)

        strip(left_ref, own_ref, dleft_ref, down_ref, -4, True)
        strip(own_ref, right_ref, down_ref, dright_ref, 252, False)

    lane = lax.broadcasted_iota(jnp.int32, (tall, 128), 1)
    at_start, at_end = lane == 0, lane == 127
    b1 = jnp.where(first_col + 128 + lane < total_cols - 1, 1.0, 0.0).astype(F32)
    r = lax.broadcasted_iota(jnp.int32, (tall, 128), 0)
    g = first_row + jnp.where(r < rows + 4, r, r - tall)
    b0 = jnp.where((g >= 0) & (g < total_rows - 1), 1.0, 0.0).astype(F32)

    def by_map(ref, c, h):
        cols = pl.ds(128 * c, 128)
        tiles = [
            jnp.swapaxes(ref[pl.ds(8 * i, 8), :, cols].astype(F32)[:, 8 * h : 8 * h + 8], 0, 1)
            for i in range(ref.shape[0] // 8)
        ]
        return tiles[0] if len(tiles) == 1 else jnp.concatenate(tiles, axis=1)

    for h in range(block // 8):
        s, u, v, z = {}, {}, {}, {}
        for c in range(2):
            cols = pl.ds(128 * c, 128)
            d = jnp.concatenate([by_map(d_ref, c, h), by_map(drim_ref, c, h)], axis=1)
            rim = [by_map(rim_ref.at[i], c, h) for i in range(3)]
            for k in range(8):
                m = 8 * h + k
                main = ab_ref[m, :, cols], q_ref[0, m, :, cols], q_ref[1, m, :, cols]
                full = [jnp.concatenate([main[i], rim[i][k]], axis=0) for i in range(3)]
                s[k, c] = 0.5 * full[0] - 0.05 * d[k]
                u[k, c] = jnp.clip(full[1], -b0, b0)
                v[k, c] = jnp.clip(full[2], -b1, b1) if c else full[2]
        gms = [pl.program_id(0) * block + 8 * h + k for k in range(8)]

        def field(p, k):
            edge = pltpu.roll(lefts[p], lax.rem(128 - gms[k], 128), 1)
            t = [pltpu.roll(v[k, c], 1, 1) for c in range(2)]
            before = jnp.where(at_start, edge, t[0]), jnp.where(at_start, t[0], t[1])
            for c in range(2):
                vertical = u[k, c] - pltpu.roll(u[k, c], 1, 0)
                z[k, c] = s[k, c] - 0.125 * (vertical + (v[k, c] - before[c]))

        for p in range(PASSES):
            for k in range(8):
                field(p, k)
            for k in range(8):
                edge = pltpu.roll(rights[p], 127 - gms[k], 1)
                t = [pltpu.roll(z[k, c], 127, 1) for c in range(2)]
                after = jnp.where(at_end, t[1], t[0]), jnp.where(at_end, edge, t[1])
                for c in range(2):
                    below = pltpu.roll(z[k, c], tall - 1, 0)
                    bound = b1 if c else 1.0
                    u[k, c] = jnp.clip(u[k, c] + (below - z[k, c]), -b0, b0)
                    v[k, c] = jnp.clip(v[k, c] + (after[c] - z[k, c]), -bound, bound)
        for k in range(8):
            field(PASSES, k)
            m = 8 * h + k
            for c in range(2):
                cols = pl.ds(128 * c, 128)
                abn_ref[m, :, cols] = jnp.maximum(2.0 * z[k, c][:rows] - 0.02, 0.0)
                qn_ref[0, m, :, cols] = u[k, c][:rows]
                qn_ref[1, m, :, cols] = v[k, c][:rows]


def tv(origin, abundance, duals, rim, d, drim, strips, dstrips):
    maps, rows, cols = abundance.shape
    block = 16
    tall = rows + 8
    tile = pl.BlockSpec((block, rows, cols), lambda i: (i, 0, 0))
    pair = pl.BlockSpec((2, block, rows, cols), lambda i: (0, i, 0, 0))

    def by_row(count):
        return pl.BlockSpec((count, block, cols), lambda i: (0, i, 0))

    return pl.pallas_call(
        tv_kernel,
        grid=(maps // block,),
        out_shape=(
            jax.ShapeDtypeStruct(abundance.shape, F32),
            jax.ShapeDtypeStruct(duals.shape, F32),
        ),
        in_specs=[
            SCALARS,
            tile,
            pair,
            pl.BlockSpec((3, 8, block, cols), lambda i: (0, 0, i, 0)),
            by_row(rows),
            by_row(8),
        ]
        + [WHOLE] * 6,
        out_specs=(tile, pair),
        scratch_shapes=[
            pltpu.VMEM((PASSES + 1, tall, maps), F32),
            pltpu.VMEM((PASSES, tall, maps), F32),
            pltpu.VMEM((tall * 8, maps), F32),
        ],
        compiler_params=pltpu.CompilerParams(vmem_limit_bytes=56 * MIB),
        name="tv",
    )(origin, abundance, duals, rim, d, drim, *strips, *dstrips)


def on_device(abundance, duals, reflectance, library):
    maps, height, width = abundance.shape
    share = height // 8
    me = lax.axis_index(LIB)
    compact, columns = front_abundance(abundance, library)
    blocks = to_all(compact)
    observed = lax.dynamic_slice_in_dim(reflectance, me * share, share, 1).transpose(1, 0, 2)

    first, last, dual_columns = front_duals(duals, compact)
    own = compact[:, : share * maps].reshape(height, maps, width)
    first = jnp.concatenate([own[None, :4], first])
    last = jnp.concatenate([own[None, height - 4 :], last])
    rim = jnp.concatenate([shifted(first, "row", -1), shifted(last, "row", 1)], axis=1)
    columns = jnp.concatenate([columns[None], dual_columns], axis=0)
    strips = beside(jnp.concatenate([columns, outer_columns_of(rim, "rim_columns")], axis=1))

    d = to_all(middle(blocks, observed, maps, [rim]))
    d, strips = lax.optimization_barrier((d, strips))
    d = d.reshape(height, maps, width)
    drim = below_then_above(d, 0)
    dcolumns = outer_columns_of(d[None], "descent_columns")
    dcolumns = jnp.concatenate([dcolumns, outer_columns_of(drim[None], "descent_rim_columns")], axis=1)
    dstrips = beside(dcolumns)
    origin = jnp.stack(
        [
            lax.axis_index("row") * height,
            lax.axis_index("col") * width,
            height * lax.axis_size("row"),
            width * lax.axis_size("col"),
        ]
    )
    return tv(origin, abundance, duals, rim, d, drim, strips, dstrips)


def solution(mesh):
    torus = Mesh(
        mesh.devices.reshape(4, 2, mesh.shape["row"], mesh.shape["col"]),
        ("lib_0", "lib_1", "row", "col"),
    )
    placed = (P(LIB, "row", "col"), P(None, LIB, "row", "col"), P(None, "row", "col"), P(None, LIB))
    return jax.shard_map(
        on_device,
        mesh=torus,
        in_specs=placed,
        out_specs=(P(LIB, "row", "col"), P(None, LIB, "row", "col")),
        check_vma=False,
    )
```

time: 356 us -> 132 us (0.37)
  local copies, waits for them, and re-layouts: 102 us -> 8.14 us
  other arithmetic: 75.3 us -> 2.32 us
  waiting for transfers between devices: 108 us -> 38.8 us
  Pallas kernels: 0 us -> 40 us
  between operations: 14.6 us -> 0.88 us
  matrix products: 8.38 us -> 0 us
  starting transfers between devices: 46.3 us -> 40.3 us
    reduce_scatter x2 -> x0, waiting for transfers between devices: 96.1 us -> none  [sum_by_axis(): nearer = lax.psum_scatter(array, axes[0], scatter_dimension=dim, tiled=True)]
    unnamed x35 -> x27, local copies, waits for them, and re-layouts: 52 us -> 4.67 us
    pallas_call x0 -> x7, Pallas kernels: none -> 40 us  [the longest x1 21.8 us: tv(): pl.pallas_call(tv_kernel, grid=(maps // block,), out_shape=(jax.ShapeDtyp...]
    slice x25 -> x2, local copies, waits for them, and re-layouts: 35.1 us -> 0.07 us  [the longest x1 0.04 us: on_device(): last = jnp.concatenate([own[None, height - 4:], last])]
    ppermute x14 -> x8, waiting for transfers between devices: 4.64 us -> 37.8 us  [shifted(): return lax.ppermute(array, axis, pairs)]
    min x3 -> x0, other arithmetic: 22.5 us -> none  [on_device(): dual = jnp.clip(dual + 0.5 * jnp.stack([down, right]), -1.0, 1.0)]
    sub x3 -> x0, other arithmetic: 15.9 us -> none  [inner_field(): return start - 0.25 * (current[0] - first_prev + (current[1] - second_prev))]
    mul x4 -> x0, other arithmetic: 13.4 us -> none  [the longest x3 8.54 us: on_device(): dual = jnp.stack([duals[0] * keep_rows, duals[1] * keep_cols])]
  transfers between devices with their start and end apart: 18 -> 10, of which waited for: 8 -> 7; matrix products, arithmetic and copies ran while one was open for 23% -> 4% of each run, Pallas kernels for 0% -> 7%
where the time goes in v2:
time: 132 us; the launch traced here: 130 us
  starting transfers between devices  40.3 us (31%)
  Pallas kernels  40 us (30%)
  waiting for transfers between devices  38.8 us (29%)
  local copies, waits for them, and re-layouts  8.14 us (6%)
  other arithmetic  2.32 us (2%)
    ppermute x8, waiting for transfers between devices, shifted(): return lax.ppermute(array, axis, pairs)  37.8 us
    ppermute x8, starting transfers between devices, shifted(): return lax.ppermute(array, axis, pairs)  26.6 us
    pallas_call x1, Pallas kernels, tv(): pl.pallas_call(tv_kernel, grid=(maps // block,), out_shape=(jax.ShapeDtyp...  21.8 us
    all_to_all x2, starting transfers between devices, to_all(): return lax.all_to_all(array, LIB, 0, 0, tiled=True)  13.7 us
    pallas_call x1, Pallas kernels, front_duals(): pl.pallas_call(functools.partial(front_kernel, False), grid=(2, height //...  7.78 us
    pallas_call x1, Pallas kernels, front_abundance(): pl.pallas_call(functools.partial(front_kernel, True), grid=(height // 8,)...  5.7 us
    unnamed x27, local copies, waits for them, and re-layouts  4.67 us
    pallas_call x1, Pallas kernels, middle(): pl.pallas_call(middle_kernel, out_shape=jax.ShapeDtypeStruct((8, share, m...  3.49 us
  transfers between devices with their start and end apart: 10, of which 7 were waited for; matrix products, arithmetic and copies ran while one was open for 4% of the time, Pallas kernels for 7%

profile of v2, /device:TPU:1, one launch (start us, length us, event | category | flops | bytes accessed | tf_op | source)
XLA Modules:
  0.0 130.4 jit_solution(16388518698612433776)
XLA Ops:
  2.0 5.7 %front_abundance.1 = (bf16[8,624,256]{2,1,0:T(8,128)(2,1)}, f32[32,8,128]{2,1,0:T(8,128)}) custom-call(f32[128,4,16,128]{3,2,1,0:T(8,128)} %bitcast.30, bf16[112,256]{1,0:T(8,128)(2,1)} %pad_maximum_fusion.4.refs_1_), custom_call_target="tpu_custom_call" | custom-call | tf_op jit(solution)/shard_map/front_abundance/pallas_call | solution.py:85
  7.7 7.6 %all-to-all-start = ((bf16[8,624,256]{2,1,0:T(8,128)(2,1)}), bf16[8,624,256]{2,1,0:T(8,128)(2,1)}, u32[]{:S(2)}, u32[]{:S(2)}) async-start(bf16[8,624,256]{2,1,0:T(8,128)(2,1)} %get-tuple-element.11.refs_1_), calls=%async_computation | async-start | bytes 5111808 | tf_op jit(solution)/shard_map/all_to_all | solution.py:27
  15.4 7.8 %front_duals.1 = (bf16[2,4,128,256]{3,2,1,0:T(8,128)(2,1)S(1)}, bf16[2,4,128,256]{3,2,1,0:T(8,128)(2,1)S(1)}, f32[2,32,8,128]{3,2,1,0:T(8,128)S(1)}) custom-call(f32[2,128,4,16,128]{4,3,2,1,0:T(8,128)} %bitcast.29, bf16[8,624,256]{2,1,0:T(8,128)(2,1)S(1)} %copy-done.3), custom_call_target="tpu_custom_call" | custom-call | bytes 8000000 | tf_op jit(solution)/shard_map/front_duals/pallas_call | solution.py:104
  23.3 1.3 collective-permute-start
  25.5 5.1 %collective-permute-start.1 = (bf16[3,4,128,256]{3,2,1,0:T(8,128)(2,1)}, bf16[3,4,128,256]{3,2,1,0:T(8,128)(2,1)}, u32[]{:S(2)}, u32[]{:S(2)}) collective-permute-start(bf16[3,4,128,256]{3,2,1,0:T(8,128)(2,1)} %pad_maximum_fusion.1), channel_id=1, source_target_pairs={{0,4},{4,8},{8,12},{1,5},{5,9},{9,13},{2,6},{6,10},{10,14},{3,7},{... | collective-permute-start | bytes 2359304 | tf_op jit(solution)/shard_map/ppermute | solution.py:23
  30.6 1.4 %constant_dynamic-slice_fusion = bf16[224,4,256]{2,1,0:T(4,128)(2,1)S(1)} fusion(bf16[224,32,256]{2,1,0:T(8,128)(2,1)} %param.6, s32[]{:T(128)S(6)} %select_n.3), kind=kLoop, calls=%fused_computation.13 | loop fusion | bytes 917508 | tf_op jit(solution)/shard_map/dynamic_slice | solution.py:357
  32.1 11.7 %collective-permute-done = bf16[3,4,128,256]{3,2,1,0:T(8,128)(2,1)} collective-permute-done((bf16[3,4,128,256]{3,2,1,0:T(8,128)(2,1)S(1)}, bf16[3,4,128,256]{3,2,1,0:T(8,128)(2,1)}, u32[]{:S(2)}, u32[]{:S(2)}) %collective-permute-start) | collective-permute-done | bytes 786464 | tf_op jit(solution)/shard_map/ppermute | solution.py:23
  43.7 1.2 constant_dynamic-update-slice_fusion.1
  45.8 1.2 constant_dynamic-update-slice_fusion.refs_0_.in_ref.rim_ref
  47.9 3.5 %middle.1 = bf16[8,4,128,256]{3,2,1,0:T(8,128)(2,1)S(1)} custom-call(bf16[8,624,256]{2,1,0:T(8,128)(2,1)} %all-to-all-done.blocks, bf16[4,224,256]{2,1,0:T(8,128)(2,1)S(1)} %bitcast.28, bf16[3,8,128,256]{3,2,1,0:T(8,128)(2,1)S(1)} %constant_dynamic-update-slice_fusion.refs_0_.in_ref.rim_ref), custom_call_target="tpu_custom_call" | custom-call | tf_op jit(solution)/shard_map/middle/pallas_call | solution.py:147
  51.4 1.3 %copy-done.4 = bf16[8,4,128,256]{3,2,1,0:T(8,128)(2,1)} copy-done((bf16[8,4,128,256]{3,2,1,0:T(8,128)(2,1)}, bf16[8,4,128,256]{3,2,1,0:T(8,128)(2,1)S(1)}, u32[]{:S(2)}) %copy-start.4) | copy-done | bytes 2097176
  52.7 6.1 %all-to-all-start.1 = ((bf16[8,4,128,256]{3,2,1,0:T(8,128)(2,1)}), bf16[8,4,128,256]{3,2,1,0:T(8,128)(2,1)S(1)}, u32[]{:S(2)}, u32[]{:S(2)}) async-start(bf16[8,4,128,256]{3,2,1,0:T(8,128)(2,1)} %copy-done.4), calls=%async_computation.1 | async-start | bytes 4194304 | tf_op jit(solution)/shard_map/all_to_all | solution.py:27
  58.9 1.4 %copy-done.2 = bf16[3,8,128,256]{3,2,1,0:T(8,128)(2,1)S(1)} copy-done((bf16[3,8,128,256]{3,2,1,0:T(8,128)(2,1)S(1)}, bf16[3,8,128,256]{3,2,1,0:T(8,128)(2,1)}, u32[]{:S(2)}) %copy-start.2) | copy-done | bytes 1572888
  60.8 4.4 %collective-permute-start.3 = (f32[3,40,8,128]{3,2,1,0:T(8,128)S(1)}, f32[3,40,8,128]{3,2,1,0:T(8,128)S(1)}, u32[]{:S(2)}, u32[]{:S(2)}) collective-permute-start(f32[3,40,8,128]{3,2,1,0:T(8,128)S(1)} %pad_maximum_fusion.2.own_ref), channel_id=1, source_target_pairs={{1,0},{2,1},{3,2},{5,4},{6,5},{7,6},{9,8},{10,9},{11,10},{13,12},{... | collective-permute-start | bytes 1474568 | tf_op jit(solution)/shard_map/ppermute | solution.py:23
  65.2 2.1 %collective-permute-start.2 = (f32[3,40,8,128]{3,2,1,0:T(8,128)S(1)}, f32[3,40,8,128]{3,2,1,0:T(8,128)}, u32[]{:S(2)}, u32[]{:S(2)}) collective-permute-start(f32[3,40,8,128]{3,2,1,0:T(8,128)S(1)} %pad_maximum_fusion.2.own_ref), channel_id=1, source_target_pairs={{0,1},{1,2},{2,3},{4,5},{5,6},{6,7},{8,9},{9,10},{10,11},{12,13},{... | collective-permute-start | bytes 1474568 | tf_op jit(solution)/shard_map/ppermute | solution.py:23
  67.3 21.0 %collective-permute-done.3.right_ref = f32[3,40,8,128]{3,2,1,0:T(8,128)S(1)} collective-permute-done((f32[3,40,8,128]{3,2,1,0:T(8,128)S(1)}, f32[3,40,8,128]{3,2,1,0:T(8,128)S(1)}, u32[]{:S(2)}, u32[]{:S(2)}) %collective-permute-start.3) | collective-permute-done | bytes 491552 | tf_op jit(solution)/shard_map/ppermute | solution.py:23
  88.4 1.3 collective-permute-start.4
  89.7 4.8 %collective-permute-start.5 = (bf16[4,128,256]{2,1,0:T(8,128)(2,1)S(1)}, bf16[4,128,256]{2,1,0:T(8,128)(2,1)S(1)}, u32[]{:S(2)}, u32[]{:S(2)}) collective-permute-start(bf16[4,128,256]{2,1,0:T(8,128)(2,1)S(1)} %get-tuple-element.22), channel_id=1, source_target_pairs={{0,4},{4,8},{8,12},{1,5},{5,9},{9,13},{2,6},{6,10},{10,14},{3,7},{... | collective-permute-start | bytes 786440 | tf_op jit(solution)/shard_map/ppermute | solution.py:23
  95.0 1.3 collective-permute-done.4
  96.3 1.5 %collective-permute-done.5 = bf16[4,128,256]{2,1,0:T(8,128)(2,1)S(1)} collective-permute-done((bf16[4,128,256]{2,1,0:T(8,128)(2,1)S(1)}, bf16[4,128,256]{2,1,0:T(8,128)(2,1)S(1)}, u32[]{:S(2)}, u32[]{:S(2)}) %collective-permute-start.5) | collective-permute-done | bytes 262176 | tf_op jit(solution)/shard_map/ppermute | solution.py:23
  98.0 5.7 %collective-permute-start.7 = (f32[1,40,8,128]{3,2,1,0:T(8,128)S(1)}, f32[1,40,8,128]{3,2,1,0:T(8,128)S(1)}, u32[]{:S(2)}, u32[]{:S(2)}) collective-permute-start(f32[1,40,8,128]{3,2,1,0:T(8,128)S(1)} %pad_maximum_fusion.3.down_ref), channel_id=1, source_target_pairs={{1,0},{2,1},{3,2},{5,4},{6,5},{7,6},{9,8},{10,9},{11,10},{13,12},{... | collective-permute-start | bytes 491528 | tf_op jit(solution)/shard_map/ppermute | solution.py:23
  103.7 1.9 %collective-permute-start.6 = (f32[1,40,8,128]{3,2,1,0:T(8,128)S(1)}, f32[1,40,8,128]{3,2,1,0:T(8,128)S(1)}, u32[]{:S(2)}, u32[]{:S(2)}) collective-permute-start(f32[1,40,8,128]{3,2,1,0:T(8,128)S(1)} %pad_maximum_fusion.3.down_ref), channel_id=1, source_target_pairs={{0,1},{1,2},{2,3},{4,5},{5,6},{6,7},{8,9},{9,10},{10,11},{12,13},{... | collective-permute-start | bytes 491528 | tf_op jit(solution)/shard_map/ppermute | solution.py:23
  106.3 1.6 %collective-permute-done.6.dleft_ref = f32[1,40,8,128]{3,2,1,0:T(8,128)S(1)} collective-permute-done((f32[1,40,8,128]{3,2,1,0:T(8,128)S(1)}, f32[1,40,8,128]{3,2,1,0:T(8,128)S(1)}, u32[]{:S(2)}, u32[]{:S(2)}) %collective-permute-start.6) | collective-permute-done | bytes 163872 | tf_op jit(solution)/shard_map/ppermute | solution.py:23
  108.6 21.8 %tv.1 = (f32[128,32,256]{2,1,0:T(8,128)}, f32[2,128,32,256]{3,2,1,0:T(8,128)}) custom-call(s32[4]{0:T(128)} %pad_add_fusion.origin, f32[128,32,256]{2,1,0:T(8,128)} %ab_ref.1, f32[2,128,32,256]{3,2,1,0:T(8,128)} %q_ref.1, bf16[3,8,128,256]{3,2,1,0:T(8,128)(2,1)} %copy-done.1, bf16[32,128,256]{2,1,0:T(8,128)(2,1)} %bitcast.26, ...), custom_call_target="tpu_custom_call" | custom-call | tf_op jit(solution)/shard_map/tv/pallas_call | solution.py:324
  (42 shorter events, 6.9 us)
Async XLA Ops:
  7.7 7.6 %copy-start.3 = (bf16[8,624,256]{2,1,0:T(8,128)(2,1)S(1)}, bf16[8,624,256]{2,1,0:T(8,128)(2,1)}, u32[]{:S(2)}) copy-start(bf16[8,624,256]{2,1,0:T(8,128)(2,1)} %get-tuple-element.11.refs_1_) | copy-start | bytes 7667716
  7.7 40.2 %all-to-all-start = ((bf16[8,624,256]{2,1,0:T(8,128)(2,1)}), bf16[8,624,256]{2,1,0:T(8,128)(2,1)}, u32[]{:S(2)}, u32[]{:S(2)}) async-start(bf16[8,624,256]{2,1,0:T(8,128)(2,1)} %get-tuple-element.11.refs_1_), calls=%async_computation | async-start | bytes 5111808 | tf_op jit(solution)/shard_map/all_to_all | solution.py:27
  23.3 20.5 %collective-permute-start = (bf16[3,4,128,256]{3,2,1,0:T(8,128)(2,1)S(1)}, bf16[3,4,128,256]{3,2,1,0:T(8,128)(2,1)}, u32[]{:S(2)}, u32[]{:S(2)}) collective-permute-start(bf16[3,4,128,256]{3,2,1,0:T(8,128)(2,1)S(1)} %pad_maximum_fusion), channel_id=1, source_target_pairs={{4,0},{8,4},{12,8},{5,1},{9,5},{13,9},{6,2},{10,6},{14,10},{7,3},{... | collective-permute-start | bytes 2359304 | tf_op jit(solution)/shard_map/ppermute | solution.py:23
  25.5 20.2 %collective-permute-start.1 = (bf16[3,4,128,256]{3,2,1,0:T(8,128)(2,1)}, bf16[3,4,128,256]{3,2,1,0:T(8,128)(2,1)}, u32[]{:S(2)}, u32[]{:S(2)}) collective-permute-start(bf16[3,4,128,256]{3,2,1,0:T(8,128)(2,1)} %pad_maximum_fusion.1), channel_id=1, source_target_pairs={{0,4},{4,8},{8,12},{1,5},{5,9},{9,13},{2,6},{6,10},{10,14},{3,7},{... | collective-permute-start | bytes 2359304 | tf_op jit(solution)/shard_map/ppermute | solution.py:23
  47.0 4.4 %copy-start.1 = (bf16[3,8,128,256]{3,2,1,0:T(8,128)(2,1)}, bf16[3,8,128,256]{3,2,1,0:T(8,128)(2,1)S(1)}, u32[]{:S(2)}) copy-start(bf16[3,8,128,256]{3,2,1,0:T(8,128)(2,1)S(1)} %constant_dynamic-update-slice_fusion.refs_0_.in_ref.rim_ref) | copy-start | bytes 4718596
  51.4 1.3 %copy-start.4 = (bf16[8,4,128,256]{3,2,1,0:T(8,128)(2,1)}, bf16[8,4,128,256]{3,2,1,0:T(8,128)(2,1)S(1)}, u32[]{:S(2)}) copy-start(bf16[8,4,128,256]{3,2,1,0:T(8,128)(2,1)S(1)} %middle.1) | copy-start | bytes 6291460
  52.7 8.0 %copy-start.11 = (f32[32,8,128]{2,1,0:T(8,128)S(1)}, f32[32,8,128]{2,1,0:T(8,128)}, u32[]{:S(2)}) copy-start(f32[32,8,128]{2,1,0:T(8,128)} %get-tuple-element.14) | copy-start | bytes 393220
  52.7 35.6 %all-to-all-start.1 = ((bf16[8,4,128,256]{3,2,1,0:T(8,128)(2,1)}), bf16[8,4,128,256]{3,2,1,0:T(8,128)(2,1)S(1)}, u32[]{:S(2)}, u32[]{:S(2)}) async-start(bf16[8,4,128,256]{3,2,1,0:T(8,128)(2,1)} %copy-done.4), calls=%async_computation.1 | async-start | bytes 4194304 | tf_op jit(solution)/shard_map/all_to_all | solution.py:27
  58.9 1.4 %copy-start.2 = (bf16[3,8,128,256]{3,2,1,0:T(8,128)(2,1)S(1)}, bf16[3,8,128,256]{3,2,1,0:T(8,128)(2,1)}, u32[]{:S(2)}) copy-start(bf16[3,8,128,256]{3,2,1,0:T(8,128)(2,1)} %copy-done.1) | copy-start | bytes 4718596
  60.7 37.3 %copy-start.6 = (f32[3,40,8,128]{3,2,1,0:T(8,128)}, f32[3,40,8,128]{3,2,1,0:T(8,128)S(1)}, u32[]{:S(2)}) copy-start(f32[3,40,8,128]{3,2,1,0:T(8,128)S(1)} %pad_maximum_fusion.2.own_ref) | copy-start | bytes 1474564
  60.8 27.6 %collective-permute-start.3 = (f32[3,40,8,128]{3,2,1,0:T(8,128)S(1)}, f32[3,40,8,128]{3,2,1,0:T(8,128)S(1)}, u32[]{:S(2)}, u32[]{:S(2)}) collective-permute-start(f32[3,40,8,128]{3,2,1,0:T(8,128)S(1)} %pad_maximum_fusion.2.own_ref), channel_id=1, source_target_pairs={{1,0},{2,1},{3,2},{5,4},{6,5},{7,6},{9,8},{10,9},{11,10},{13,12},{... | collective-permute-start | bytes 1474568 | tf_op jit(solution)/shard_map/ppermute | solution.py:23
  65.2 23.2 %collective-permute-start.2 = (f32[3,40,8,128]{3,2,1,0:T(8,128)S(1)}, f32[3,40,8,128]{3,2,1,0:T(8,128)}, u32[]{:S(2)}, u32[]{:S(2)}) collective-permute-start(f32[3,40,8,128]{3,2,1,0:T(8,128)S(1)} %pad_maximum_fusion.2.own_ref), channel_id=1, source_target_pairs={{0,1},{1,2},{2,3},{4,5},{5,6},{6,7},{8,9},{9,10},{10,11},{12,13},{... | collective-permute-start | bytes 1474568 | tf_op jit(solution)/shard_map/ppermute | solution.py:23
  88.3 6.7 %copy-start.8 = (f32[3,40,8,128]{3,2,1,0:T(8,128)}, f32[3,40,8,128]{3,2,1,0:T(8,128)S(1)}, u32[]{:S(2)}) copy-start(f32[3,40,8,128]{3,2,1,0:T(8,128)S(1)} %collective-permute-done.3.right_ref) | copy-start | bytes 1474564
  88.4 9.7 %copy-start = (bf16[8,4,128,256]{3,2,1,0:T(8,128)(2,1)}, bf16[8,4,128,256]{3,2,1,0:T(8,128)(2,1)S(1)}, u32[]{:S(2)}) copy-start(bf16[8,4,128,256]{3,2,1,0:T(8,128)(2,1)S(1)} %all-to-all-done.1) | copy-start | bytes 6291460
  88.4 7.9 %collective-permute-start.4 = (bf16[4,128,256]{2,1,0:T(8,128)(2,1)S(1)}, bf16[4,128,256]{2,1,0:T(8,128)(2,1)S(1)}, u32[]{:S(2)}, u32[]{:S(2)}) collective-permute-start(bf16[4,128,256]{2,1,0:T(8,128)(2,1)S(1)} %get-tuple-element.23), channel_id=1, source_target_pairs={{4,0},{8,4},{12,8},{5,1},{9,5},{13,9},{6,2},{10,6},{14,10},{7,3},{... | collective-permute-start | bytes 786440 | tf_op jit(solution)/shard_map/ppermute | solution.py:23
  89.7 8.0 %collective-permute-start.5 = (bf16[4,128,256]{2,1,0:T(8,128)(2,1)S(1)}, bf16[4,128,256]{2,1,0:T(8,128)(2,1)S(1)}, u32[]{:S(2)}, u32[]{:S(2)}) collective-permute-start(bf16[4,128,256]{2,1,0:T(8,128)(2,1)S(1)} %get-tuple-element.22), channel_id=1, source_target_pairs={{0,4},{4,8},{8,12},{1,5},{5,9},{9,13},{2,6},{6,10},{10,14},{3,7},{... | collective-permute-start | bytes 786440 | tf_op jit(solution)/shard_map/ppermute | solution.py:23
  97.8 10.1 %copy-start.5 = (bf16[8,128,256]{2,1,0:T(8,128)(2,1)}, bf16[8,128,256]{2,1,0:T(8,128)(2,1)S(1)}, u32[]{:S(2)}) copy-start(bf16[8,128,256]{2,1,0:T(8,128)(2,1)S(1)} %constant_dynamic-update-slice_fusion.2.drim_ref) | copy-start | bytes 1572868
  98.0 9.9 %copy-start.7 = (f32[1,40,8,128]{3,2,1,0:T(8,128)}, f32[1,40,8,128]{3,2,1,0:T(8,128)S(1)}, u32[]{:S(2)}) copy-start(f32[1,40,8,128]{3,2,1,0:T(8,128)S(1)} %pad_maximum_fusion.3.down_ref) | copy-start | bytes 491524
  98.0 8.3 %collective-permute-start.7 = (f32[1,40,8,128]{3,2,1,0:T(8,128)S(1)}, f32[1,40,8,128]{3,2,1,0:T(8,128)S(1)}, u32[]{:S(2)}, u32[]{:S(2)}) collective-permute-start(f32[1,40,8,128]{3,2,1,0:T(8,128)S(1)} %pad_maximum_fusion.3.down_ref), channel_id=1, source_target_pairs={{1,0},{2,1},{3,2},{5,4},{6,5},{7,6},{9,8},{10,9},{11,10},{13,12},{... | collective-permute-start | bytes 491528 | tf_op jit(solution)/shard_map/ppermute | solution.py:23
  103.7 4.2 %collective-permute-start.6 = (f32[1,40,8,128]{3,2,1,0:T(8,128)S(1)}, f32[1,40,8,128]{3,2,1,0:T(8,128)S(1)}, u32[]{:S(2)}, u32[]{:S(2)}) collective-permute-start(f32[1,40,8,128]{3,2,1,0:T(8,128)S(1)} %pad_maximum_fusion.3.down_ref), channel_id=1, source_target_pairs={{0,1},{1,2},{2,3},{4,5},{5,6},{6,7},{8,9},{9,10},{10,11},{12,13},{... | collective-permute-start | bytes 491528 | tf_op jit(solution)/shard_map/ppermute | solution.py:23
  106.3 1.6 %copy-start.9 = (f32[1,40,8,128]{3,2,1,0:T(8,128)}, f32[1,40,8,128]{3,2,1,0:T(8,128)S(1)}, u32[]{:S(2)}) copy-start(f32[1,40,8,128]{3,2,1,0:T(8,128)S(1)} %collective-permute-done.7.dright_ref) | copy-start | bytes 491524
  107.9 0.7 copy-start.10

commit v3 on v2

--- a/solution.py
+++ b/solution.py
@@ -59,11 +59,22 @@
     if with_compact:
         library, out = refs[0], refs[1]
         share = (out.shape[1] - library.shape[0]) // maps
+        height = 8 * share
         for j in range(8):
+            row = pl.program_id(0) * 8 + j
+            inner = jnp.clip(row - 4, 0, height - 9)
+            outer = (row < 4) | (row >= height - 4)
+            owner = jnp.where(outer, jnp.where(row < 4, row, row - height + 8), inner // (share - 1))
+            slot = jnp.where(outer, 0, 1 + inner % (share - 1))
+            at = pl.ds(pl.multiple_of(slot * maps, maps), maps)
             for c, half in enumerate(rows(j)):
-                out[j // share, pl.ds(j % share * maps, maps), pl.ds(128 * c, 128)] = half.astype(BF16)
-        for k in range(8 // share):
-            out[k, pl.ds(share * maps, library.shape[0])] = library[...]
+                out[owner, at, pl.ds(128 * c, 128)] = half.astype(BF16)
+
+        @pl.when(pl.program_id(0) == 0)
+        def _():
+            for k in range(8):
+                out[k, pl.ds(share * maps, library.shape[0])] = library[...]
+
     else:
         step = pl.program_id(1)
         for at, out, start in ((0, refs[0], 0), (pl.num_programs(1) - 1, refs[1], 4)):
@@ -91,7 +102,7 @@
         ),
         in_specs=[pl.BlockSpec((maps, 1, 16, 128), lambda i: (0, i, 0, 0)), WHOLE],
         out_specs=(
-            pl.BlockSpec((8 // share, length, width), lambda i: (i, 0, 0)),
+            pl.BlockSpec((8, length, width), lambda i: (0, 0, 0)),
             pl.BlockSpec((8, 8, maps), lambda i: (i, 0, 0)),
         ),
         compiler_params=pltpu.CompilerParams(vmem_limit_bytes=56 * MIB),
@@ -125,9 +136,11 @@
 
 
 def middle_kernel(blocks, observed, *refs):
-    descents = refs[-1]
-    parts, share, maps, width = descents.shape
+    outer, inner = refs[-2:]
+    parts, more, maps, width = inner.shape
+    share, bands, _ = observed.shape
     start = share * maps
+    lane = lax.broadcasted_iota(jnp.int32, (bands, 128), 1)
 
     def library(k):
         flat = blocks[k, start:]
@@ -135,20 +148,38 @@
 
     wide = jnp.concatenate([library(k) for k in range(parts)], axis=1)
     tall = jnp.concatenate([library(k).astype(F32).T.astype(BF16) for k in range(parts)])
+    packed = jnp.zeros((bands, 128), F32)
     for r in range(share):
         pixels = jnp.concatenate([blocks[k, r * maps : r * maps + maps] for k in range(parts)])
         total = jnp.dot(wide, pixels, preferred_element_type=F32) - observed[r].astype(F32)
-        d = jnp.dot(tall, total.astype(BF16), preferred_element_type=F32).astype(BF16)
-        descents[:, r] = d.reshape(parts, maps, width)
+        rb = total.astype(BF16)
+        d = jnp.dot(tall, rb, preferred_element_type=F32).astype(BF16).reshape(parts, maps, width)
+        if r == 0:
+            outer[:, :maps] = d
+        else:
+            inner[:, r - 1] = d
+        exact = rb.astype(F32)
+        moved = outer_columns([exact[:, :128], exact[:, 128:]], lane, r)
+        packed = jnp.where(lane // 8 == r, moved, packed)
+    columns = packed.T[: 8 * share].astype(BF16)
+    d = jnp.dot(columns, wide, preferred_element_type=F32).astype(BF16)
+    half = 4 * share
+    for k in range(parts):
+        for c in range(2):
+            piece = d[half * c : half * c + half, k * maps : k * maps + maps]
+            outer[k, pl.ds(maps, half), pl.ds(128 * c, 128)] = piece
 
 
 def middle(blocks, observed, maps, first):
     share, _, width = observed.shape
     return pl.pallas_call(
         middle_kernel,
-        out_shape=jax.ShapeDtypeStruct((8, share, maps, width), BF16),
+        out_shape=(
+            jax.ShapeDtypeStruct((8, maps + 4 * share, width), BF16),
+            jax.ShapeDtypeStruct((8, share - 1, maps, width), BF16),
+        ),
         in_specs=[WHOLE] * 2 + [pl.BlockSpec(memory_space=pl.ANY)] * len(first),
-        out_specs=WHOLE,
+        out_specs=(WHOLE, WHOLE),
         compiler_params=pltpu.CompilerParams(vmem_limit_bytes=16 * MIB),
         name="middle",
     )(blocks, observed, *first)
@@ -194,7 +225,8 @@
     ab_ref,
     q_ref,
     rim_ref,
-    d_ref,
+    douter_ref,
+    dinner_ref,
     drim_ref,
     own_ref,
     left_ref,
@@ -209,7 +241,7 @@
     turn,
 ):
     block = ab_ref.shape[0]
-    rows = d_ref.shape[0]
+    rows = ab_ref.shape[1]
     tall = rows + 8
     maps = own_ref.shape[-1]
     first_row, first_col, total_rows, total_cols = (origin[i] for i in range(4))
@@ -258,20 +290,22 @@
     g = first_row + jnp.where(r < rows + 4, r, r - tall)
     b0 = jnp.where((g >= 0) & (g < total_rows - 1), 1.0, 0.0).astype(F32)
 
-    def by_map(ref, c, h):
+    def by_map(c, h, *pieces):
         cols = pl.ds(128 * c, 128)
-        tiles = [
-            jnp.swapaxes(ref[pl.ds(8 * i, 8), :, cols].astype(F32)[:, 8 * h : 8 * h + 8], 0, 1)
-            for i in range(ref.shape[0] // 8)
-        ]
-        return tiles[0] if len(tiles) == 1 else jnp.concatenate(tiles, axis=1)
+        found = [ref[pl.ds(at, n), :, cols].astype(F32)[:, 8 * h : 8 * h + 8] for ref, at, n in pieces]
+        return jnp.swapaxes(found[0] if len(found) == 1 else jnp.concatenate(found), 0, 1)
+
+    inner = rows - 8
+    descents = [[(douter_ref, 0, 4), (dinner_ref, 0, 4)]]
+    descents += [[(dinner_ref, at, 8)] for at in range(4, inner - 4, 8)]
+    descents += [[(dinner_ref, inner - 4, 4), (douter_ref, 4, 4)], [(drim_ref, 0, 8)]]
 
     for h in range(block // 8):
         s, u, v, z = {}, {}, {}, {}
         for c in range(2):
             cols = pl.ds(128 * c, 128)
-            d = jnp.concatenate([by_map(d_ref, c, h), by_map(drim_ref, c, h)], axis=1)
-            rim = [by_map(rim_ref.at[i], c, h) for i in range(3)]
+            d = jnp.concatenate([by_map(c, h, *pieces) for pieces in descents], axis=1)
+            rim = [by_map(c, h, (rim_ref.at[i], 0, 8)) for i in range(3)]
             for k in range(8):
                 m = 8 * h + k
                 main = ab_ref[m, :, cols], q_ref[0, m, :, cols], q_ref[1, m, :, cols]
@@ -311,7 +345,7 @@
                 qn_ref[1, m, :, cols] = v[k, c][:rows]
 
 
-def tv(origin, abundance, duals, rim, d, drim, strips, dstrips):
+def tv(origin, abundance, duals, rim, douter, dinner, drim, strips, dstrips):
     maps, rows, cols = abundance.shape
     block = 16
     tall = rows + 8
@@ -333,7 +367,8 @@
             tile,
             pair,
             pl.BlockSpec((3, 8, block, cols), lambda i: (0, 0, i, 0)),
-            by_row(rows),
+            by_row(8),
+            by_row(rows - 8),
             by_row(8),
         ]
         + [WHOLE] * 6,
@@ -345,7 +380,7 @@
         ],
         compiler_params=pltpu.CompilerParams(vmem_limit_bytes=56 * MIB),
         name="tv",
-    )(origin, abundance, duals, rim, d, drim, *strips, *dstrips)
+    )(origin, abundance, duals, rim, douter, dinner, drim, *strips, *dstrips)
 
 
 def on_device(abundance, duals, reflectance, library):
@@ -354,23 +389,31 @@
     me = lax.axis_index(LIB)
     compact, columns = front_abundance(abundance, library)
     blocks = to_all(compact)
-    observed = lax.dynamic_slice_in_dim(reflectance, me * share, share, 1).transpose(1, 0, 2)
+    outer_row = jnp.where(me < 4, me, me + height - 8)
+    observed = [
+        lax.dynamic_slice_in_dim(reflectance, outer_row, 1, 1),
+        lax.dynamic_slice_in_dim(reflectance, 4 + me * (share - 1), share - 1, 1),
+    ]
+    observed = jnp.concatenate(observed, axis=1).transpose(1, 0, 2)
 
     first, last, dual_columns = front_duals(duals, compact)
-    own = compact[:, : share * maps].reshape(height, maps, width)
-    first = jnp.concatenate([own[None, :4], first])
-    last = jnp.concatenate([own[None, height - 4 :], last])
+    first = jnp.concatenate([compact[None, :4, :maps], first])
+    last = jnp.concatenate([compact[None, 4:, :maps], last])
     rim = jnp.concatenate([shifted(first, "row", -1), shifted(last, "row", 1)], axis=1)
     columns = jnp.concatenate([columns[None], dual_columns], axis=0)
     strips = beside(jnp.concatenate([columns, outer_columns_of(rim, "rim_columns")], axis=1))
 
-    d = to_all(middle(blocks, observed, maps, [rim]))
-    d, strips = lax.optimization_barrier((d, strips))
-    d = d.reshape(height, maps, width)
-    drim = below_then_above(d, 0)
-    dcolumns = outer_columns_of(d[None], "descent_columns")
-    dcolumns = jnp.concatenate([dcolumns, outer_columns_of(drim[None], "descent_rim_columns")], axis=1)
-    dstrips = beside(dcolumns)
+    outer, inner = middle(blocks, observed, maps, [rim])
+    outer = to_all(outer)
+    inner, outer, strips = lax.optimization_barrier((inner, outer, strips))
+    dinner = to_all(inner).reshape(height - 8, maps, width)
+    douter = outer[:, :maps]
+    sides = [half.reshape(8, share // 2, 8, maps) for half in jnp.split(outer[:, maps:], 2, axis=2)]
+    sides = jnp.concatenate(sides, axis=1).astype(F32)
+    middle_rows = sides[:, 1:].reshape(height - 8, 8, maps)
+    drim = below_then_above(douter, 0)
+    above = outer_columns_of(drim[None], "descent_rim_columns")[0]
+    dstrips = beside(jnp.concatenate([sides[:4, 0], middle_rows, sides[4:, 0], above])[None])
     origin = jnp.stack(
         [
             lax.axis_index("row") * height,
@@ -379,7 +422,7 @@
             width * lax.axis_size("col"),
         ]
     )
-    return tv(origin, abundance, duals, rim, d, drim, strips, dstrips)
+    return tv(origin, abundance, duals, rim, douter, dinner, drim, strips, dstrips)
 
 
 def solution(mesh):

time: 132 us -> 125 us (0.947)
  waiting for transfers between devices: 38.8 us -> 23 us
  starting transfers between devices: 40.3 us -> 46.4 us
  local copies, waits for them, and re-layouts: 8.14 us -> 9.76 us
    ppermute x8, waiting for transfers between devices: 37.8 us -> 21 us  [shifted(): return lax.ppermute(array, axis, pairs)]
    all_to_all x2 -> x3, starting transfers between devices: 13.7 us -> 20.9 us  [to_all(): return lax.all_to_all(array, LIB, 0, 0, tiled=True)]
    dynamic_slice x1 -> x2, local copies, waits for them, and re-layouts: 1.42 us -> 3.26 us  [the longest x1 1.84 us: on_device(): lax.dynamic_slice_in_dim(reflectance, 4 + me * (share - 1), share - 1, 1)]
    unnamed x27 -> x26, local copies, waits for them, and re-layouts: 4.67 us -> 3.6 us
  transfers between devices with their start and end apart: 10 -> 11, of which waited for: 7 -> 8; matrix products, arithmetic and copies ran while one was open for 4% -> 7% of each run, Pallas kernels for 7% -> 7%
where the time goes in v3:
time: 125 us; the launch traced here: 123 us
  starting transfers between devices  46.4 us (37%)
  Pallas kernels  40.6 us (32%)
  waiting for transfers between devices  23 us (18%)
  local copies, waits for them, and re-layouts  9.76 us (8%)
  other arithmetic  2.41 us (2%)
    ppermute x8, starting transfers between devices, shifted(): return lax.ppermute(array, axis, pairs)  25.5 us
    pallas_call x1, Pallas kernels, tv(): pl.pallas_call(tv_kernel, grid=(maps // block,), out_shape=(jax.ShapeDtyp...  21.9 us
    ppermute x8, waiting for transfers between devices, shifted(): return lax.ppermute(array, axis, pairs)  21 us
    all_to_all x3, starting transfers between devices, to_all(): return lax.all_to_all(array, LIB, 0, 0, tiled=True)  20.9 us
    pallas_call x1, Pallas kernels, front_duals(): pl.pallas_call(functools.partial(front_kernel, False), grid=(2, height //...  7.78 us
    pallas_call x1, Pallas kernels, front_abundance(): pl.pallas_call(functools.partial(front_kernel, True), grid=(height // 8,)...  6.36 us
    pallas_call x1, Pallas kernels, middle(): pl.pallas_call(middle_kernel, out_shape=(jax.ShapeDtypeStruct((8, maps +...  3.98 us
    unnamed x26, local copies, waits for them, and re-layouts  3.6 us
  transfers between devices with their start and end apart: 11, of which 8 were waited for; matrix products, arithmetic and copies ran while one was open for 7% of the time, Pallas kernels for 7%

profile of v3, /device:TPU:1, one launch (start us, length us, event | category | flops | bytes accessed | tf_op | source)
XLA Modules:
  0.0 123.0 jit_solution(6976040150527151201)
XLA Ops:
  2.0 6.4 %front_abundance.1 = (bf16[8,624,256]{2,1,0:T(8,128)(2,1)}, f32[32,8,128]{2,1,0:T(8,128)}) custom-call(f32[128,4,16,128]{3,2,1,0:T(8,128)} %bitcast.36, bf16[112,256]{1,0:T(8,128)(2,1)} %pad_maximum_fusion.4.refs_1_), custom_call_target="tpu_custom_call" | custom-call | tf_op jit(solution)/shard_map/front_abundance/pallas_call | solution.py:96
  8.4 7.6 %all-to-all-start = ((bf16[8,624,256]{2,1,0:T(8,128)(2,1)}), bf16[8,624,256]{2,1,0:T(8,128)(2,1)}, u32[]{:S(2)}, u32[]{:S(2)}) async-start(bf16[8,624,256]{2,1,0:T(8,128)(2,1)} %get-tuple-element.14.refs_1_), calls=%async_computation | async-start | bytes 5111808 | tf_op jit(solution)/shard_map/all_to_all | solution.py:27
  16.0 7.8 %front_duals.1 = (bf16[2,4,128,256]{3,2,1,0:T(8,128)(2,1)S(1)}, bf16[2,4,128,256]{3,2,1,0:T(8,128)(2,1)S(1)}, f32[2,32,8,128]{3,2,1,0:T(8,128)S(1)}) custom-call(f32[2,128,4,16,128]{4,3,2,1,0:T(8,128)} %bitcast.35, bf16[8,624,256]{2,1,0:T(8,128)(2,1)S(1)} %copy-done.1), custom_call_target="tpu_custom_call" | custom-call | bytes 8000000 | tf_op jit(solution)/shard_map/front_duals/pallas_call | solution.py:115
  23.9 1.3 %collective-permute-start = (bf16[3,4,128,256]{3,2,1,0:T(8,128)(2,1)S(1)}, bf16[3,4,128,256]{3,2,1,0:T(8,128)(2,1)}, u32[]{:S(2)}, u32[]{:S(2)}) collective-permute-start(bf16[3,4,128,256]{3,2,1,0:T(8,128)(2,1)S(1)} %pad_maximum_fusion), channel_id=1, source_target_pairs={{4,0},{8,4},{12,8},{5,1},{9,5},{13,9},{6,2},{10,6},{14,10},{7,3},{... | collective-permute-start | bytes 2359304 | tf_op jit(solution)/shard_map/ppermute | solution.py:23
  26.2 5.1 %collective-permute-start.1 = (bf16[3,4,128,256]{3,2,1,0:T(8,128)(2,1)}, bf16[3,4,128,256]{3,2,1,0:T(8,128)(2,1)}, u32[]{:S(2)}, u32[]{:S(2)}) collective-permute-start(bf16[3,4,128,256]{3,2,1,0:T(8,128)(2,1)} %pad_maximum_fusion.1), channel_id=1, source_target_pairs={{0,4},{4,8},{8,12},{1,5},{5,9},{9,13},{2,6},{6,10},{10,14},{3,7},{... | collective-permute-start | bytes 2359304 | tf_op jit(solution)/shard_map/ppermute | solution.py:23
  31.3 1.4 %constant_dynamic-slice_fusion.1 = bf16[224,1,256]{2,1,0:T(2,128)(2,1)S(1)} fusion(bf16[224,32,256]{2,1,0:T(8,128)(2,1)} %param.6, s32[]{:T(128)S(6)} %select_n.11), kind=kLoop, calls=%fused_computation.20 | loop fusion | bytes 229380 | tf_op jit(solution)/shard_map/dynamic_slice | solution.py:394
  32.7 1.8 %constant_dynamic-slice_fusion = bf16[224,3,256]{2,1,0:T(4,128)(2,1)S(1)} fusion(bf16[224,32,256]{2,1,0:T(8,128)(2,1)} %param.6, s32[]{:T(128)S(6)} %select_n.12), kind=kLoop, calls=%fused_computation.19 | loop fusion | bytes 688132 | tf_op jit(solution)/shard_map/dynamic_slice | solution.py:395
  34.7 9.7 %collective-permute-done = bf16[3,4,128,256]{3,2,1,0:T(8,128)(2,1)} collective-permute-done((bf16[3,4,128,256]{3,2,1,0:T(8,128)(2,1)S(1)}, bf16[3,4,128,256]{3,2,1,0:T(8,128)(2,1)}, u32[]{:S(2)}, u32[]{:S(2)}) %collective-permute-start) | collective-permute-done | bytes 786464 | tf_op jit(solution)/shard_map/ppermute | solution.py:23
  44.4 1.2 constant_dynamic-update-slice_fusion.1
  46.4 1.2 constant_dynamic-update-slice_fusion.refs_0_.in_ref.rim_ref
  48.6 4.0 %middle.1 = (bf16[8,144,256]{2,1,0:T(8,128)(2,1)}, bf16[8,3,128,256]{3,2,1,0:T(8,128)(2,1)S(1)}) custom-call(bf16[8,624,256]{2,1,0:T(8,128)(2,1)} %all-to-all-done.blocks, bf16[4,224,256]{2,1,0:T(8,128)(2,1)S(1)} %maximum_bitcast_fusion.observed, bf16[3,8,128,256]{3,2,1,0:T(8,128)(2,1)S(1)} %constant_dynamic-update-slice_fusion.refs_0_.in_ref.rim_ref), custom_call_target="tpu_custom_call" | custom-call | tf_op jit(solution)/shard_map/middle/pallas_call | solution.py:175
  53.7 6.0 %all-to-all-start.1 = ((bf16[8,144,256]{2,1,0:T(8,128)(2,1)}), bf16[8,144,256]{2,1,0:T(8,128)(2,1)S(1)}, u32[]{:S(2)}, u32[]{:S(2)}) async-start(bf16[8,144,256]{2,1,0:T(8,128)(2,1)} %get-tuple-element.18), calls=%async_computation.1 | async-start | bytes 1179648 | tf_op jit(solution)/shard_map/all_to_all | solution.py:27
  59.7 4.4 %collective-permute-start.3 = (f32[3,40,8,128]{3,2,1,0:T(8,128)S(1)}, f32[3,40,8,128]{3,2,1,0:T(8,128)S(1)}, u32[]{:S(2)}, u32[]{:S(2)}) collective-permute-start(f32[3,40,8,128]{3,2,1,0:T(8,128)S(1)} %pad_maximum_fusion.2.own_ref), channel_id=1, source_target_pairs={{1,0},{2,1},{3,2},{5,4},{6,5},{7,6},{9,8},{10,9},{11,10},{13,12},{... | collective-permute-start | bytes 1474568 | tf_op jit(solution)/shard_map/ppermute | solution.py:23
  64.2 2.1 %collective-permute-start.2 = (f32[3,40,8,128]{3,2,1,0:T(8,128)S(1)}, f32[3,40,8,128]{3,2,1,0:T(8,128)}, u32[]{:S(2)}, u32[]{:S(2)}) collective-permute-start(f32[3,40,8,128]{3,2,1,0:T(8,128)S(1)} %pad_maximum_fusion.2.own_ref), channel_id=1, source_target_pairs={{0,1},{1,2},{2,3},{4,5},{5,6},{6,7},{8,9},{9,10},{10,11},{12,13},{... | collective-permute-start | bytes 1474568 | tf_op jit(solution)/shard_map/ppermute | solution.py:23
  66.3 6.4 %collective-permute-done.3.right_ref = f32[3,40,8,128]{3,2,1,0:T(8,128)S(1)} collective-permute-done((f32[3,40,8,128]{3,2,1,0:T(8,128)S(1)}, f32[3,40,8,128]{3,2,1,0:T(8,128)S(1)}, u32[]{:S(2)}, u32[]{:S(2)}) %collective-permute-start.3) | collective-permute-done | bytes 491552 | tf_op jit(solution)/shard_map/ppermute | solution.py:23
  72.7 7.3 %all-to-all-start.2 = ((bf16[8,3,128,256]{3,2,1,0:T(8,128)(2,1)}), bf16[8,3,128,256]{3,2,1,0:T(8,128)(2,1)S(1)}, u32[]{:S(2)}, u32[]{:S(2)}) async-start(bf16[8,3,128,256]{3,2,1,0:T(8,128)(2,1)} %copy-done.3), calls=%async_computation.2 | async-start | bytes 3145728 | tf_op jit(solution)/shard_map/all_to_all | solution.py:27
  80.0 1.3 %collective-permute-start.4 = (bf16[4,128,256]{2,1,0:T(8,128)(2,1)S(1)}, bf16[4,128,256]{2,1,0:T(8,128)(2,1)S(1)}, u32[]{:S(2)}, u32[]{:S(2)}) collective-permute-start(bf16[4,128,256]{2,1,0:T(8,128)(2,1)S(1)} %get-tuple-element.31), channel_id=1, source_target_pairs={{4,0},{8,4},{12,8},{5,1},{9,5},{13,9},{6,2},{10,6},{14,10},{7,3},{... | collective-permute-start | bytes 786440 | tf_op jit(solution)/shard_map/ppermute | solution.py:23
  81.4 4.7 %collective-permute-start.5 = (bf16[4,128,256]{2,1,0:T(8,128)(2,1)S(1)}, bf16[4,128,256]{2,1,0:T(8,128)(2,1)S(1)}, u32[]{:S(2)}, u32[]{:S(2)}) collective-permute-start(bf16[4,128,256]{2,1,0:T(8,128)(2,1)S(1)} %get-tuple-element.30), channel_id=1, source_target_pairs={{0,4},{4,8},{8,12},{1,5},{5,9},{9,13},{2,6},{6,10},{10,14},{3,7},{... | collective-permute-start | bytes 786440 | tf_op jit(solution)/shard_map/ppermute | solution.py:23
  86.2 2.0 %collective-permute-done.4 = bf16[4,128,256]{2,1,0:T(8,128)(2,1)S(1)} collective-permute-done((bf16[4,128,256]{2,1,0:T(8,128)(2,1)S(1)}, bf16[4,128,256]{2,1,0:T(8,128)(2,1)S(1)}, u32[]{:S(2)}, u32[]{:S(2)}) %collective-permute-start.4) | collective-permute-done | bytes 262176 | tf_op jit(solution)/shard_map/ppermute | solution.py:23
  88.2 1.2 collective-permute-done.5
  89.7 1.9 %collective-permute-start.7 = (f32[1,40,8,128]{3,2,1,0:T(8,128)S(1)}, f32[1,40,8,128]{3,2,1,0:T(8,128)S(1)}, u32[]{:S(2)}, u32[]{:S(2)}) collective-permute-start(f32[1,40,8,128]{3,2,1,0:T(8,128)S(1)} %maximum_bitcast_fusion.1.down_ref), channel_id=1, source_target_pairs={{1,0},{2,1},{3,2},{5,4},{6,5},{7,6},{9,8},{10,9},{11,10},{13,12},{... | collective-permute-start | bytes 491528 | tf_op jit(solution)/shard_map/ppermute | solution.py:23
  91.6 4.6 %collective-permute-start.6 = (f32[1,40,8,128]{3,2,1,0:T(8,128)S(1)}, f32[1,40,8,128]{3,2,1,0:T(8,128)S(1)}, u32[]{:S(2)}, u32[]{:S(2)}) collective-permute-start(f32[1,40,8,128]{3,2,1,0:T(8,128)S(1)} %maximum_bitcast_fusion.1.down_ref), channel_id=1, source_target_pairs={{0,1},{1,2},{2,3},{4,5},{5,6},{6,7},{8,9},{9,10},{10,11},{12,13},{... | collective-permute-start | bytes 491528 | tf_op jit(solution)/shard_map/ppermute | solution.py:23
  98.5 1.5 %all-to-all-done.2 = bf16[8,3,128,256]{3,2,1,0:T(8,128)(2,1)S(1)} async-done(((bf16[8,3,128,256]{3,2,1,0:T(8,128)(2,1)}), bf16[8,3,128,256]{3,2,1,0:T(8,128)(2,1)S(1)}, u32[]{:S(2)}, u32[]{:S(2)}) %all-to-all-start.2) | async-done | bytes 1572896 | tf_op jit(solution)/shard_map/all_to_all | solution.py:27
  101.2 21.9 %tv.1 = (f32[128,32,256]{2,1,0:T(8,128)}, f32[2,128,32,256]{3,2,1,0:T(8,128)}) custom-call(s32[4]{0:T(128)} %pad_add_fusion.origin, f32[128,32,256]{2,1,0:T(8,128)} %ab_ref.1, f32[2,128,32,256]{3,2,1,0:T(8,128)} %q_ref.1, bf16[3,8,128,256]{3,2,1,0:T(8,128)(2,1)} %copy-done, bf16[8,128,256]{2,1,0:T(8,128)(2,1)} %slice.31.douter_ref, ...), custom_call_target="tpu_custom_call" | custom-call | tf_op jit(solution)/shard_map/tv/pallas_call | solution.py:358
  (50 shorter events, 9.2 us)
Async XLA Ops:
  8.4 7.6 %copy-start.1 = (bf16[8,624,256]{2,1,0:T(8,128)(2,1)S(1)}, bf16[8,624,256]{2,1,0:T(8,128)(2,1)}, u32[]{:S(2)}) copy-start(bf16[8,624,256]{2,1,0:T(8,128)(2,1)} %get-tuple-element.14.refs_1_) | copy-start | bytes 7667716
  8.4 40.2 %all-to-all-start = ((bf16[8,624,256]{2,1,0:T(8,128)(2,1)}), bf16[8,624,256]{2,1,0:T(8,128)(2,1)}, u32[]{:S(2)}, u32[]{:S(2)}) async-start(bf16[8,624,256]{2,1,0:T(8,128)(2,1)} %get-tuple-element.14.refs_1_), calls=%async_computation | async-start | bytes 5111808 | tf_op jit(solution)/shard_map/all_to_all | solution.py:27
  23.9 20.5 %collective-permute-start = (bf16[3,4,128,256]{3,2,1,0:T(8,128)(2,1)S(1)}, bf16[3,4,128,256]{3,2,1,0:T(8,128)(2,1)}, u32[]{:S(2)}, u32[]{:S(2)}) collective-permute-start(bf16[3,4,128,256]{3,2,1,0:T(8,128)(2,1)S(1)} %pad_maximum_fusion), channel_id=1, source_target_pairs={{4,0},{8,4},{12,8},{5,1},{9,5},{13,9},{6,2},{10,6},{14,10},{7,3},{... | collective-permute-start | bytes 2359304 | tf_op jit(solution)/shard_map/ppermute | solution.py:23
  26.2 20.2 %collective-permute-start.1 = (bf16[3,4,128,256]{3,2,1,0:T(8,128)(2,1)}, bf16[3,4,128,256]{3,2,1,0:T(8,128)(2,1)}, u32[]{:S(2)}, u32[]{:S(2)}) collective-permute-start(bf16[3,4,128,256]{3,2,1,0:T(8,128)(2,1)} %pad_maximum_fusion.1), channel_id=1, source_target_pairs={{0,4},{4,8},{8,12},{1,5},{5,9},{9,13},{2,6},{6,10},{10,14},{3,7},{... | collective-permute-start | bytes 2359304 | tf_op jit(solution)/shard_map/ppermute | solution.py:23
  47.6 4.9 %copy-start = (bf16[3,8,128,256]{3,2,1,0:T(8,128)(2,1)}, bf16[3,8,128,256]{3,2,1,0:T(8,128)(2,1)S(1)}, u32[]{:S(2)}) copy-start(bf16[3,8,128,256]{3,2,1,0:T(8,128)(2,1)S(1)} %constant_dynamic-update-slice_fusion.refs_0_.in_ref.rim_ref) | copy-start | bytes 4718596
  48.1 11.6 %copy-start.10 = (f32[32,8,128]{2,1,0:T(8,128)S(1)}, f32[32,8,128]{2,1,0:T(8,128)}, u32[]{:S(2)}) copy-start(f32[32,8,128]{2,1,0:T(8,128)} %get-tuple-element.19) | copy-start | bytes 393220
  52.5 1.1 copy-start.3
  53.7 19.0 %all-to-all-start.1 = ((bf16[8,144,256]{2,1,0:T(8,128)(2,1)}), bf16[8,144,256]{2,1,0:T(8,128)(2,1)S(1)}, u32[]{:S(2)}, u32[]{:S(2)}) async-start(bf16[8,144,256]{2,1,0:T(8,128)(2,1)} %get-tuple-element.18), calls=%async_computation.1 | async-start | bytes 1179648 | tf_op jit(solution)/shard_map/all_to_all | solution.py:27
  59.7 13.0 %copy-start.5 = (f32[3,40,8,128]{3,2,1,0:T(8,128)}, f32[3,40,8,128]{3,2,1,0:T(8,128)S(1)}, u32[]{:S(2)}) copy-start(f32[3,40,8,128]{3,2,1,0:T(8,128)S(1)} %pad_maximum_fusion.2.own_ref) | copy-start | bytes 1474564
  59.7 13.0 %collective-permute-start.3 = (f32[3,40,8,128]{3,2,1,0:T(8,128)S(1)}, f32[3,40,8,128]{3,2,1,0:T(8,128)S(1)}, u32[]{:S(2)}, u32[]{:S(2)}) collective-permute-start(f32[3,40,8,128]{3,2,1,0:T(8,128)S(1)} %pad_maximum_fusion.2.own_ref), channel_id=1, source_target_pairs={{1,0},{2,1},{3,2},{5,4},{6,5},{7,6},{9,8},{10,9},{11,10},{13,12},{... | collective-permute-start | bytes 1474568 | tf_op jit(solution)/shard_map/ppermute | solution.py:23
  64.2 8.6 %collective-permute-start.2 = (f32[3,40,8,128]{3,2,1,0:T(8,128)S(1)}, f32[3,40,8,128]{3,2,1,0:T(8,128)}, u32[]{:S(2)}, u32[]{:S(2)}) collective-permute-start(f32[3,40,8,128]{3,2,1,0:T(8,128)S(1)} %pad_maximum_fusion.2.own_ref), channel_id=1, source_target_pairs={{0,1},{1,2},{2,3},{4,5},{5,6},{6,7},{8,9},{9,10},{10,11},{12,13},{... | collective-permute-start | bytes 1474568 | tf_op jit(solution)/shard_map/ppermute | solution.py:23
  72.7 15.5 %copy-start.7 = (f32[3,40,8,128]{3,2,1,0:T(8,128)}, f32[3,40,8,128]{3,2,1,0:T(8,128)S(1)}, u32[]{:S(2)}) copy-start(f32[3,40,8,128]{3,2,1,0:T(8,128)S(1)} %collective-permute-done.3.right_ref) | copy-start | bytes 1474564
  72.7 27.2 %all-to-all-start.2 = ((bf16[8,3,128,256]{3,2,1,0:T(8,128)(2,1)}), bf16[8,3,128,256]{3,2,1,0:T(8,128)(2,1)S(1)}, u32[]{:S(2)}, u32[]{:S(2)}) async-start(bf16[8,3,128,256]{3,2,1,0:T(8,128)(2,1)} %copy-done.3), calls=%async_computation.2 | async-start | bytes 3145728 | tf_op jit(solution)/shard_map/all_to_all | solution.py:27
  80.0 8.2 %collective-permute-start.4 = (bf16[4,128,256]{2,1,0:T(8,128)(2,1)S(1)}, bf16[4,128,256]{2,1,0:T(8,128)(2,1)S(1)}, u32[]{:S(2)}, u32[]{:S(2)}) collective-permute-start(bf16[4,128,256]{2,1,0:T(8,128)(2,1)S(1)} %get-tuple-element.31), channel_id=1, source_target_pairs={{4,0},{8,4},{12,8},{5,1},{9,5},{13,9},{6,2},{10,6},{14,10},{7,3},{... | collective-permute-start | bytes 786440 | tf_op jit(solution)/shard_map/ppermute | solution.py:23
  81.4 8.0 %collective-permute-start.5 = (bf16[4,128,256]{2,1,0:T(8,128)(2,1)S(1)}, bf16[4,128,256]{2,1,0:T(8,128)(2,1)S(1)}, u32[]{:S(2)}, u32[]{:S(2)}) collective-permute-start(bf16[4,128,256]{2,1,0:T(8,128)(2,1)S(1)} %get-tuple-element.30), channel_id=1, source_target_pairs={{0,4},{4,8},{8,12},{1,5},{5,9},{9,13},{2,6},{6,10},{10,14},{3,7},{... | collective-permute-start | bytes 786440 | tf_op jit(solution)/shard_map/ppermute | solution.py:23
  89.5 10.5 %copy-start.2 = (bf16[8,128,256]{2,1,0:T(8,128)(2,1)}, bf16[8,128,256]{2,1,0:T(8,128)(2,1)S(1)}, u32[]{:S(2)}) copy-start(bf16[8,128,256]{2,1,0:T(8,128)(2,1)S(1)} %constant_dynamic-update-slice_fusion.2.drim_ref) | copy-start | bytes 1572868
  89.7 10.3 %copy-start.6 = (f32[1,40,8,128]{3,2,1,0:T(8,128)}, f32[1,40,8,128]{3,2,1,0:T(8,128)S(1)}, u32[]{:S(2)}) copy-start(f32[1,40,8,128]{3,2,1,0:T(8,128)S(1)} %maximum_bitcast_fusion.1.down_ref) | copy-start | bytes 491524
  89.7 8.0 %collective-permute-start.7 = (f32[1,40,8,128]{3,2,1,0:T(8,128)S(1)}, f32[1,40,8,128]{3,2,1,0:T(8,128)S(1)}, u32[]{:S(2)}, u32[]{:S(2)}) collective-permute-start(f32[1,40,8,128]{3,2,1,0:T(8,128)S(1)} %maximum_bitcast_fusion.1.down_ref), channel_id=1, source_target_pairs={{1,0},{2,1},{3,2},{5,4},{6,5},{7,6},{9,8},{10,9},{11,10},{13,12},{... | collective-permute-start | bytes 491528 | tf_op jit(solution)/shard_map/ppermute | solution.py:23
  91.6 6.8 %collective-permute-start.6 = (f32[1,40,8,128]{3,2,1,0:T(8,128)S(1)}, f32[1,40,8,128]{3,2,1,0:T(8,128)S(1)}, u32[]{:S(2)}, u32[]{:S(2)}) collective-permute-start(f32[1,40,8,128]{3,2,1,0:T(8,128)S(1)} %maximum_bitcast_fusion.1.down_ref), channel_id=1, source_target_pairs={{0,1},{1,2},{2,3},{4,5},{5,6},{6,7},{8,9},{9,10},{10,11},{12,13},{... | collective-permute-start | bytes 491528 | tf_op jit(solution)/shard_map/ppermute | solution.py:23
  97.7 2.3 %copy-start.8 = (f32[1,40,8,128]{3,2,1,0:T(8,128)}, f32[1,40,8,128]{3,2,1,0:T(8,128)S(1)}, u32[]{:S(2)}) copy-start(f32[1,40,8,128]{3,2,1,0:T(8,128)S(1)} %collective-permute-done.7.dright_ref) | copy-start | bytes 491524
  98.5 1.5 %copy-start.9 = (f32[1,40,8,128]{3,2,1,0:T(8,128)}, f32[1,40,8,128]{3,2,1,0:T(8,128)S(1)}, u32[]{:S(2)}) copy-start(f32[1,40,8,128]{3,2,1,0:T(8,128)S(1)} %collective-permute-done.6.dleft_ref) | copy-start | bytes 491524
  100.0 1.2 copy-start.4

commit v4 on v3

--- a/solution.py
+++ b/solution.py
@@ -49,16 +49,20 @@
 
 
 def front_kernel(with_compact, *refs):
-    in_ref, refs = refs[0], refs[1 if with_compact else 2 :]
-    maps = in_ref.shape[-4]
-    flat = in_ref.reshape(maps * 16, 128)
+    in_ref, by_row, refs = refs[0], refs[-1], refs[1 if with_compact else 2 : -1]
+    in_ref = in_ref if with_compact else in_ref.at[0]
+    maps = in_ref.shape[0]
+    for at in range(0, maps, 8):
+        for c in range(2):
+            tile = jnp.swapaxes(in_ref[at : at + 8, 0, 8 * c : 8 * c + 8, :], 0, 1)
+            by_row[:, at : at + 8, 128 * c : 128 * c + 128] = tile
 
     def rows(j):
-        return [flat[pl.ds(8 * c + j, maps, 16), :] for c in range(2)]
+        return [by_row[j, :, 128 * c : 128 * c + 128] for c in range(2)]
 
     if with_compact:
         library, out = refs[0], refs[1]
-        share = (out.shape[1] - library.shape[0]) // maps
+        share = (out.shape[1] - library.shape[0] // 2) // maps
         height = 8 * share
         for j in range(8):
             row = pl.program_id(0) * 8 + j
@@ -72,8 +76,11 @@
 
         @pl.when(pl.program_id(0) == 0)
         def _():
+            half = library.shape[0] // 2
             for k in range(8):
-                out[k, pl.ds(share * maps, library.shape[0])] = library[...]
+                for c in range(2):
+                    piece = library[half * c : half * c + half]
+                    out[k, pl.ds(share * maps, half), pl.ds(128 * c, 128)] = piece
 
     else:
         step = pl.program_id(1)
@@ -91,8 +98,7 @@
 def front_abundance(abundance, library):
     maps, height, width = abundance.shape
     share = height // 8
-    flat = jnp.concatenate(jnp.split(library, 2), axis=1)
-    length = share * maps + flat.shape[0]
+    length = share * maps + library.shape[0] // 2
     return pl.pallas_call(
         functools.partial(front_kernel, True),
         grid=(height // 8,),
@@ -105,9 +111,10 @@
             pl.BlockSpec((8, length, width), lambda i: (0, 0, 0)),
             pl.BlockSpec((8, 8, maps), lambda i: (i, 0, 0)),
         ),
+        scratch_shapes=[pltpu.VMEM((8, maps, width), F32)],
         compiler_params=pltpu.CompilerParams(vmem_limit_bytes=56 * MIB),
         name="front_abundance",
-    )(tiles_of(abundance), flat)
+    )(tiles_of(abundance), library)
 
 
 def front_duals(duals, after):
@@ -129,6 +136,7 @@
             pl.BlockSpec((1, 4, maps, width), lambda k, i: (k, 0, 0, 0)),
             pl.BlockSpec((1, 8, 8, maps), lambda k, i: (k, i, 0, 0)),
         ),
+        scratch_shapes=[pltpu.VMEM((8, maps, width), F32)],
         compiler_params=pltpu.CompilerParams(vmem_limit_bytes=48 * MIB),
         cost_estimate=pl.CostEstimate(flops=0, bytes_accessed=8_000_000, transcendentals=0),
         name="front_duals",

time: 125 us -> 122 us (0.976)
  no operation moved by 1% of the time
where the time goes in v4:
time: 122 us; the launch traced here: 121 us
  starting transfers between devices  46.1 us (38%)
  Pallas kernels  39.5 us (32%)
  waiting for transfers between devices  23.3 us (19%)
  local copies, waits for them, and re-layouts  9.01 us (7%)
  other arithmetic  1.71 us (1%)
    ppermute x8, starting transfers between devices, shifted(): return lax.ppermute(array, axis, pairs)  25.5 us
    pallas_call x1, Pallas kernels, tv(): pl.pallas_call(tv_kernel, grid=(maps // block,), out_shape=(jax.ShapeDtyp...  21.9 us
    ppermute x8, waiting for transfers between devices, shifted(): return lax.ppermute(array, axis, pairs)  21 us
    all_to_all x3, starting transfers between devices, to_all(): return lax.all_to_all(array, LIB, 0, 0, tiled=True)  20.6 us
    pallas_call x1, Pallas kernels, front_duals(): pl.pallas_call(functools.partial(front_kernel, False), grid=(2, height //...  7.54 us
    pallas_call x1, Pallas kernels, front_abundance(): pl.pallas_call(functools.partial(front_kernel, True), grid=(height // 8,)...  5.5 us
    pallas_call x1, Pallas kernels, middle(): pl.pallas_call(middle_kernel, out_shape=(jax.ShapeDtypeStruct((8, maps +...  3.98 us
    unnamed x26, local copies, waits for them, and re-layouts  3.61 us
  transfers between devices with their start and end apart: 11, of which 8 were waited for; matrix products, arithmetic and copies ran while one was open for 7% of the time, Pallas kernels for 7%

profile of v4, /device:TPU:1, one launch (start us, length us, event | category | flops | bytes accessed | tf_op | source)
XLA Modules:
  0.0 120.5 jit_solution(2920259212962474153)
XLA Ops:
  0.6 5.5 %front_abundance.1 = (bf16[8,624,256]{2,1,0:T(8,128)(2,1)}, f32[32,8,128]{2,1,0:T(8,128)}) custom-call(f32[128,4,16,128]{3,2,1,0:T(8,128)} %bitcast.36, bf16[224,128]{1,0:T(8,128)(2,1)} %refs_1_.1), custom_call_target="tpu_custom_call" | custom-call | tf_op jit(solution)/shard_map/front_abundance/pallas_call | solution.py:102
  6.1 7.6 %all-to-all-start = ((bf16[8,624,256]{2,1,0:T(8,128)(2,1)}), bf16[8,624,256]{2,1,0:T(8,128)(2,1)}, u32[]{:S(2)}, u32[]{:S(2)}) async-start(bf16[8,624,256]{2,1,0:T(8,128)(2,1)} %get-tuple-element.14.refs_1_), calls=%async_computation | async-start | bytes 5111808 | tf_op jit(solution)/shard_map/all_to_all | solution.py:27
  13.7 7.5 %front_duals.1 = (bf16[2,4,128,256]{3,2,1,0:T(8,128)(2,1)S(1)}, bf16[2,4,128,256]{3,2,1,0:T(8,128)(2,1)S(1)}, f32[2,32,8,128]{3,2,1,0:T(8,128)S(1)}) custom-call(f32[2,128,4,16,128]{4,3,2,1,0:T(8,128)} %bitcast.35, bf16[8,624,256]{2,1,0:T(8,128)(2,1)S(1)} %copy-done.1), custom_call_target="tpu_custom_call" | custom-call | bytes 8000000 | tf_op jit(solution)/shard_map/front_duals/pallas_call | solution.py:122
  21.4 1.3 %collective-permute-start = (bf16[3,4,128,256]{3,2,1,0:T(8,128)(2,1)S(1)}, bf16[3,4,128,256]{3,2,1,0:T(8,128)(2,1)}, u32[]{:S(2)}, u32[]{:S(2)}) collective-permute-start(bf16[3,4,128,256]{3,2,1,0:T(8,128)(2,1)S(1)} %pad_maximum_fusion), channel_id=1, source_target_pairs={{4,0},{8,4},{12,8},{5,1},{9,5},{13,9},{6,2},{10,6},{14,10},{7,3},{... | collective-permute-start | bytes 2359304 | tf_op jit(solution)/shard_map/ppermute | solution.py:23
  23.7 5.1 %collective-permute-start.1 = (bf16[3,4,128,256]{3,2,1,0:T(8,128)(2,1)}, bf16[3,4,128,256]{3,2,1,0:T(8,128)(2,1)}, u32[]{:S(2)}, u32[]{:S(2)}) collective-permute-start(bf16[3,4,128,256]{3,2,1,0:T(8,128)(2,1)} %pad_maximum_fusion.1), channel_id=1, source_target_pairs={{0,4},{4,8},{8,12},{1,5},{5,9},{9,13},{2,6},{6,10},{10,14},{3,7},{... | collective-permute-start | bytes 2359304 | tf_op jit(solution)/shard_map/ppermute | solution.py:23
  28.8 1.4 %constant_dynamic-slice_fusion.1 = bf16[224,1,256]{2,1,0:T(2,128)(2,1)S(1)} fusion(bf16[224,32,256]{2,1,0:T(8,128)(2,1)} %param.6, s32[]{:T(128)S(6)} %select_n.11), kind=kLoop, calls=%fused_computation.19 | loop fusion | bytes 229380 | tf_op jit(solution)/shard_map/dynamic_slice | solution.py:402
  30.2 1.8 %constant_dynamic-slice_fusion = bf16[224,3,256]{2,1,0:T(4,128)(2,1)S(1)} fusion(bf16[224,32,256]{2,1,0:T(8,128)(2,1)} %param.6, s32[]{:T(128)S(6)} %select_n.12), kind=kLoop, calls=%fused_computation.18 | loop fusion | bytes 688132 | tf_op jit(solution)/shard_map/dynamic_slice | solution.py:403
  32.2 9.7 %collective-permute-done = bf16[3,4,128,256]{3,2,1,0:T(8,128)(2,1)} collective-permute-done((bf16[3,4,128,256]{3,2,1,0:T(8,128)(2,1)S(1)}, bf16[3,4,128,256]{3,2,1,0:T(8,128)(2,1)}, u32[]{:S(2)}, u32[]{:S(2)}) %collective-permute-start) | collective-permute-done | bytes 786464 | tf_op jit(solution)/shard_map/ppermute | solution.py:23
  41.9 1.2 constant_dynamic-update-slice_fusion.1
  43.9 1.2 constant_dynamic-update-slice_fusion.refs_0_.in_ref.rim_ref
  46.3 4.0 %middle.1 = (bf16[8,144,256]{2,1,0:T(8,128)(2,1)}, bf16[8,3,128,256]{3,2,1,0:T(8,128)(2,1)S(1)}) custom-call(bf16[8,624,256]{2,1,0:T(8,128)(2,1)} %all-to-all-done.blocks, bf16[4,224,256]{2,1,0:T(8,128)(2,1)S(1)} %maximum_bitcast_fusion.observed, bf16[3,8,128,256]{3,2,1,0:T(8,128)(2,1)S(1)} %constant_dynamic-update-slice_fusion.refs_0_.in_ref.rim_ref), custom_call_target="tpu_custom_call" | custom-call | tf_op jit(solution)/shard_map/middle/pallas_call | solution.py:183
  51.4 5.7 %all-to-all-start.1 = ((bf16[8,144,256]{2,1,0:T(8,128)(2,1)}), bf16[8,144,256]{2,1,0:T(8,128)(2,1)S(1)}, u32[]{:S(2)}, u32[]{:S(2)}) async-start(bf16[8,144,256]{2,1,0:T(8,128)(2,1)} %get-tuple-element.18), calls=%async_computation.1 | async-start | bytes 1179648 | tf_op jit(solution)/shard_map/all_to_all | solution.py:27
  57.2 4.4 %collective-permute-start.3 = (f32[3,40,8,128]{3,2,1,0:T(8,128)S(1)}, f32[3,40,8,128]{3,2,1,0:T(8,128)S(1)}, u32[]{:S(2)}, u32[]{:S(2)}) collective-permute-start(f32[3,40,8,128]{3,2,1,0:T(8,128)S(1)} %pad_maximum_fusion.2.own_ref), channel_id=1, source_target_pairs={{1,0},{2,1},{3,2},{5,4},{6,5},{7,6},{9,8},{10,9},{11,10},{13,12},{... | collective-permute-start | bytes 1474568 | tf_op jit(solution)/shard_map/ppermute | solution.py:23
  61.7 2.1 %collective-permute-start.2 = (f32[3,40,8,128]{3,2,1,0:T(8,128)S(1)}, f32[3,40,8,128]{3,2,1,0:T(8,128)}, u32[]{:S(2)}, u32[]{:S(2)}) collective-permute-start(f32[3,40,8,128]{3,2,1,0:T(8,128)S(1)} %pad_maximum_fusion.2.own_ref), channel_id=1, source_target_pairs={{0,1},{1,2},{2,3},{4,5},{5,6},{6,7},{8,9},{9,10},{10,11},{12,13},{... | collective-permute-start | bytes 1474568 | tf_op jit(solution)/shard_map/ppermute | solution.py:23
  63.8 6.4 %collective-permute-done.3.right_ref = f32[3,40,8,128]{3,2,1,0:T(8,128)S(1)} collective-permute-done((f32[3,40,8,128]{3,2,1,0:T(8,128)S(1)}, f32[3,40,8,128]{3,2,1,0:T(8,128)S(1)}, u32[]{:S(2)}, u32[]{:S(2)}) %collective-permute-start.3) | collective-permute-done | bytes 491552 | tf_op jit(solution)/shard_map/ppermute | solution.py:23
  70.2 7.3 %all-to-all-start.2 = ((bf16[8,3,128,256]{3,2,1,0:T(8,128)(2,1)}), bf16[8,3,128,256]{3,2,1,0:T(8,128)(2,1)S(1)}, u32[]{:S(2)}, u32[]{:S(2)}) async-start(bf16[8,3,128,256]{3,2,1,0:T(8,128)(2,1)} %copy-done.3), calls=%async_computation.2 | async-start | bytes 3145728 | tf_op jit(solution)/shard_map/all_to_all | solution.py:27
  77.5 1.3 %collective-permute-start.4 = (bf16[4,128,256]{2,1,0:T(8,128)(2,1)S(1)}, bf16[4,128,256]{2,1,0:T(8,128)(2,1)S(1)}, u32[]{:S(2)}, u32[]{:S(2)}) collective-permute-start(bf16[4,128,256]{2,1,0:T(8,128)(2,1)S(1)} %get-tuple-element.31), channel_id=1, source_target_pairs={{4,0},{8,4},{12,8},{5,1},{9,5},{13,9},{6,2},{10,6},{14,10},{7,3},{... | collective-permute-start | bytes 786440 | tf_op jit(solution)/shard_map/ppermute | solution.py:23
  78.9 4.7 %collective-permute-start.5 = (bf16[4,128,256]{2,1,0:T(8,128)(2,1)S(1)}, bf16[4,128,256]{2,1,0:T(8,128)(2,1)S(1)}, u32[]{:S(2)}, u32[]{:S(2)}) collective-permute-start(bf16[4,128,256]{2,1,0:T(8,128)(2,1)S(1)} %get-tuple-element.30), channel_id=1, source_target_pairs={{0,4},{4,8},{8,12},{1,5},{5,9},{9,13},{2,6},{6,10},{10,14},{3,7},{... | collective-permute-start | bytes 786440 | tf_op jit(solution)/shard_map/ppermute | solution.py:23
  83.7 2.0 %collective-permute-done.4 = bf16[4,128,256]{2,1,0:T(8,128)(2,1)S(1)} collective-permute-done((bf16[4,128,256]{2,1,0:T(8,128)(2,1)S(1)}, bf16[4,128,256]{2,1,0:T(8,128)(2,1)S(1)}, u32[]{:S(2)}, u32[]{:S(2)}) %collective-permute-start.4) | collective-permute-done | bytes 262176 | tf_op jit(solution)/shard_map/ppermute | solution.py:23
  85.7 1.2 %collective-permute-done.5 = bf16[4,128,256]{2,1,0:T(8,128)(2,1)S(1)} collective-permute-done((bf16[4,128,256]{2,1,0:T(8,128)(2,1)S(1)}, bf16[4,128,256]{2,1,0:T(8,128)(2,1)S(1)}, u32[]{:S(2)}, u32[]{:S(2)}) %collective-permute-start.5) | collective-permute-done | bytes 262176 | tf_op jit(solution)/shard_map/ppermute | solution.py:23
  87.2 1.9 %collective-permute-start.7 = (f32[1,40,8,128]{3,2,1,0:T(8,128)S(1)}, f32[1,40,8,128]{3,2,1,0:T(8,128)S(1)}, u32[]{:S(2)}, u32[]{:S(2)}) collective-permute-start(f32[1,40,8,128]{3,2,1,0:T(8,128)S(1)} %maximum_bitcast_fusion.1.down_ref), channel_id=1, source_target_pairs={{1,0},{2,1},{3,2},{5,4},{6,5},{7,6},{9,8},{10,9},{11,10},{13,12},{... | collective-permute-start | bytes 491528 | tf_op jit(solution)/shard_map/ppermute | solution.py:23
  89.1 4.6 %collective-permute-start.6 = (f32[1,40,8,128]{3,2,1,0:T(8,128)S(1)}, f32[1,40,8,128]{3,2,1,0:T(8,128)S(1)}, u32[]{:S(2)}, u32[]{:S(2)}) collective-permute-start(f32[1,40,8,128]{3,2,1,0:T(8,128)S(1)} %maximum_bitcast_fusion.1.down_ref), channel_id=1, source_target_pairs={{0,1},{1,2},{2,3},{4,5},{5,6},{6,7},{8,9},{9,10},{10,11},{12,13},{... | collective-permute-start | bytes 491528 | tf_op jit(solution)/shard_map/ppermute | solution.py:23
  96.0 1.5 %all-to-all-done.2 = bf16[8,3,128,256]{3,2,1,0:T(8,128)(2,1)S(1)} async-done(((bf16[8,3,128,256]{3,2,1,0:T(8,128)(2,1)}), bf16[8,3,128,256]{3,2,1,0:T(8,128)(2,1)S(1)}, u32[]{:S(2)}, u32[]{:S(2)}) %all-to-all-start.2) | async-done | bytes 1572896 | tf_op jit(solution)/shard_map/all_to_all | solution.py:27
  98.7 21.9 %tv.1 = (f32[128,32,256]{2,1,0:T(8,128)}, f32[2,128,32,256]{3,2,1,0:T(8,128)}) custom-call(s32[4]{0:T(128)} %pad_add_fusion.origin, f32[128,32,256]{2,1,0:T(8,128)} %ab_ref.1, f32[2,128,32,256]{3,2,1,0:T(8,128)} %q_ref.1, bf16[3,8,128,256]{3,2,1,0:T(8,128)(2,1)} %copy-done, bf16[8,128,256]{2,1,0:T(8,128)(2,1)} %slice.31.douter_ref, ...), custom_call_target="tpu_custom_call" | custom-call | tf_op jit(solution)/shard_map/tv/pallas_call | solution.py:366
  (48 shorter events, 8.1 us)
Async XLA Ops:
  6.1 7.6 %copy-start.1 = (bf16[8,624,256]{2,1,0:T(8,128)(2,1)S(1)}, bf16[8,624,256]{2,1,0:T(8,128)(2,1)}, u32[]{:S(2)}) copy-start(bf16[8,624,256]{2,1,0:T(8,128)(2,1)} %get-tuple-element.14.refs_1_) | copy-start | bytes 7667716
  6.1 40.2 %all-to-all-start = ((bf16[8,624,256]{2,1,0:T(8,128)(2,1)}), bf16[8,624,256]{2,1,0:T(8,128)(2,1)}, u32[]{:S(2)}, u32[]{:S(2)}) async-start(bf16[8,624,256]{2,1,0:T(8,128)(2,1)} %get-tuple-element.14.refs_1_), calls=%async_computation | async-start | bytes 5111808 | tf_op jit(solution)/shard_map/all_to_all | solution.py:27
  21.4 20.5 %collective-permute-start = (bf16[3,4,128,256]{3,2,1,0:T(8,128)(2,1)S(1)}, bf16[3,4,128,256]{3,2,1,0:T(8,128)(2,1)}, u32[]{:S(2)}, u32[]{:S(2)}) collective-permute-start(bf16[3,4,128,256]{3,2,1,0:T(8,128)(2,1)S(1)} %pad_maximum_fusion), channel_id=1, source_target_pairs={{4,0},{8,4},{12,8},{5,1},{9,5},{13,9},{6,2},{10,6},{14,10},{7,3},{... | collective-permute-start | bytes 2359304 | tf_op jit(solution)/shard_map/ppermute | solution.py:23
  23.7 20.2 %collective-permute-start.1 = (bf16[3,4,128,256]{3,2,1,0:T(8,128)(2,1)}, bf16[3,4,128,256]{3,2,1,0:T(8,128)(2,1)}, u32[]{:S(2)}, u32[]{:S(2)}) collective-permute-start(bf16[3,4,128,256]{3,2,1,0:T(8,128)(2,1)} %pad_maximum_fusion.1), channel_id=1, source_target_pairs={{0,4},{4,8},{8,12},{1,5},{5,9},{9,13},{2,6},{6,10},{10,14},{3,7},{... | collective-permute-start | bytes 2359304 | tf_op jit(solution)/shard_map/ppermute | solution.py:23
  45.1 5.2 %copy-start = (bf16[3,8,128,256]{3,2,1,0:T(8,128)(2,1)}, bf16[3,8,128,256]{3,2,1,0:T(8,128)(2,1)S(1)}, u32[]{:S(2)}) copy-start(bf16[3,8,128,256]{3,2,1,0:T(8,128)(2,1)S(1)} %constant_dynamic-update-slice_fusion.refs_0_.in_ref.rim_ref) | copy-start | bytes 4718596
  45.5 11.6 %copy-start.10 = (f32[32,8,128]{2,1,0:T(8,128)S(1)}, f32[32,8,128]{2,1,0:T(8,128)}, u32[]{:S(2)}) copy-start(f32[32,8,128]{2,1,0:T(8,128)} %get-tuple-element.19) | copy-start | bytes 393220
  50.3 1.1 copy-start.3
  51.4 18.8 %all-to-all-start.1 = ((bf16[8,144,256]{2,1,0:T(8,128)(2,1)}), bf16[8,144,256]{2,1,0:T(8,128)(2,1)S(1)}, u32[]{:S(2)}, u32[]{:S(2)}) async-start(bf16[8,144,256]{2,1,0:T(8,128)(2,1)} %get-tuple-element.18), calls=%async_computation.1 | async-start | bytes 1179648 | tf_op jit(solution)/shard_map/all_to_all | solution.py:27
  57.2 13.0 %copy-start.5 = (f32[3,40,8,128]{3,2,1,0:T(8,128)}, f32[3,40,8,128]{3,2,1,0:T(8,128)S(1)}, u32[]{:S(2)}) copy-start(f32[3,40,8,128]{3,2,1,0:T(8,128)S(1)} %pad_maximum_fusion.2.own_ref) | copy-start | bytes 1474564
  57.2 13.0 %collective-permute-start.3 = (f32[3,40,8,128]{3,2,1,0:T(8,128)S(1)}, f32[3,40,8,128]{3,2,1,0:T(8,128)S(1)}, u32[]{:S(2)}, u32[]{:S(2)}) collective-permute-start(f32[3,40,8,128]{3,2,1,0:T(8,128)S(1)} %pad_maximum_fusion.2.own_ref), channel_id=1, source_target_pairs={{1,0},{2,1},{3,2},{5,4},{6,5},{7,6},{9,8},{10,9},{11,10},{13,12},{... | collective-permute-start | bytes 1474568 | tf_op jit(solution)/shard_map/ppermute | solution.py:23
  61.7 8.6 %collective-permute-start.2 = (f32[3,40,8,128]{3,2,1,0:T(8,128)S(1)}, f32[3,40,8,128]{3,2,1,0:T(8,128)}, u32[]{:S(2)}, u32[]{:S(2)}) collective-permute-start(f32[3,40,8,128]{3,2,1,0:T(8,128)S(1)} %pad_maximum_fusion.2.own_ref), channel_id=1, source_target_pairs={{0,1},{1,2},{2,3},{4,5},{5,6},{6,7},{8,9},{9,10},{10,11},{12,13},{... | collective-permute-start | bytes 1474568 | tf_op jit(solution)/shard_map/ppermute | solution.py:23
  70.2 15.5 %copy-start.7 = (f32[3,40,8,128]{3,2,1,0:T(8,128)}, f32[3,40,8,128]{3,2,1,0:T(8,128)S(1)}, u32[]{:S(2)}) copy-start(f32[3,40,8,128]{3,2,1,0:T(8,128)S(1)} %collective-permute-done.3.right_ref) | copy-start | bytes 1474564
  70.2 27.2 %all-to-all-start.2 = ((bf16[8,3,128,256]{3,2,1,0:T(8,128)(2,1)}), bf16[8,3,128,256]{3,2,1,0:T(8,128)(2,1)S(1)}, u32[]{:S(2)}, u32[]{:S(2)}) async-start(bf16[8,3,128,256]{3,2,1,0:T(8,128)(2,1)} %copy-done.3), calls=%async_computation.2 | async-start | bytes 3145728 | tf_op jit(solution)/shard_map/all_to_all | solution.py:27
  77.5 8.2 %collective-permute-start.4 = (bf16[4,128,256]{2,1,0:T(8,128)(2,1)S(1)}, bf16[4,128,256]{2,1,0:T(8,128)(2,1)S(1)}, u32[]{:S(2)}, u32[]{:S(2)}) collective-permute-start(bf16[4,128,256]{2,1,0:T(8,128)(2,1)S(1)} %get-tuple-element.31), channel_id=1, source_target_pairs={{4,0},{8,4},{12,8},{5,1},{9,5},{13,9},{6,2},{10,6},{14,10},{7,3},{... | collective-permute-start | bytes 786440 | tf_op jit(solution)/shard_map/ppermute | solution.py:23
  78.9 8.0 %collective-permute-start.5 = (bf16[4,128,256]{2,1,0:T(8,128)(2,1)S(1)}, bf16[4,128,256]{2,1,0:T(8,128)(2,1)S(1)}, u32[]{:S(2)}, u32[]{:S(2)}) collective-permute-start(bf16[4,128,256]{2,1,0:T(8,128)(2,1)S(1)} %get-tuple-element.30), channel_id=1, source_target_pairs={{0,4},{4,8},{8,12},{1,5},{5,9},{9,13},{2,6},{6,10},{10,14},{3,7},{... | collective-permute-start | bytes 786440 | tf_op jit(solution)/shard_map/ppermute | solution.py:23
  87.0 10.5 %copy-start.2 = (bf16[8,128,256]{2,1,0:T(8,128)(2,1)}, bf16[8,128,256]{2,1,0:T(8,128)(2,1)S(1)}, u32[]{:S(2)}) copy-start(bf16[8,128,256]{2,1,0:T(8,128)(2,1)S(1)} %constant_dynamic-update-slice_fusion.2.drim_ref) | copy-start | bytes 1572868
  87.2 10.3 %copy-start.6 = (f32[1,40,8,128]{3,2,1,0:T(8,128)}, f32[1,40,8,128]{3,2,1,0:T(8,128)S(1)}, u32[]{:S(2)}) copy-start(f32[1,40,8,128]{3,2,1,0:T(8,128)S(1)} %maximum_bitcast_fusion.1.down_ref) | copy-start | bytes 491524
  87.2 8.0 %collective-permute-start.7 = (f32[1,40,8,128]{3,2,1,0:T(8,128)S(1)}, f32[1,40,8,128]{3,2,1,0:T(8,128)S(1)}, u32[]{:S(2)}, u32[]{:S(2)}) collective-permute-start(f32[1,40,8,128]{3,2,1,0:T(8,128)S(1)} %maximum_bitcast_fusion.1.down_ref), channel_id=1, source_target_pairs={{1,0},{2,1},{3,2},{5,4},{6,5},{7,6},{9,8},{10,9},{11,10},{13,12},{... | collective-permute-start | bytes 491528 | tf_op jit(solution)/shard_map/ppermute | solution.py:23
  89.1 6.8 %collective-permute-start.6 = (f32[1,40,8,128]{3,2,1,0:T(8,128)S(1)}, f32[1,40,8,128]{3,2,1,0:T(8,128)S(1)}, u32[]{:S(2)}, u32[]{:S(2)}) collective-permute-start(f32[1,40,8,128]{3,2,1,0:T(8,128)S(1)} %maximum_bitcast_fusion.1.down_ref), channel_id=1, source_target_pairs={{0,1},{1,2},{2,3},{4,5},{5,6},{6,7},{8,9},{9,10},{10,11},{12,13},{... | collective-permute-start | bytes 491528 | tf_op jit(solution)/shard_map/ppermute | solution.py:23
  95.2 2.3 %copy-start.8 = (f32[1,40,8,128]{3,2,1,0:T(8,128)}, f32[1,40,8,128]{3,2,1,0:T(8,128)S(1)}, u32[]{:S(2)}) copy-start(f32[1,40,8,128]{3,2,1,0:T(8,128)S(1)} %collective-permute-done.7.dright_ref) | copy-start | bytes 491524
  96.0 1.5 %copy-start.9 = (f32[1,40,8,128]{3,2,1,0:T(8,128)}, f32[1,40,8,128]{3,2,1,0:T(8,128)S(1)}, u32[]{:S(2)}) copy-start(f32[1,40,8,128]{3,2,1,0:T(8,128)S(1)} %collective-permute-done.6.dleft_ref) | copy-start | bytes 491524
  97.5 1.2 copy-start.4

commit v5 on v4

--- a/solution.py
+++ b/solution.py
@@ -386,7 +386,7 @@
             pltpu.VMEM((PASSES, tall, maps), F32),
             pltpu.VMEM((tall * 8, maps), F32),
         ],
-        compiler_params=pltpu.CompilerParams(vmem_limit_bytes=56 * MIB),
+        compiler_params=pltpu.CompilerParams(vmem_limit_bytes=52 * MIB),
         name="tv",
     )(origin, abundance, duals, rim, douter, dinner, drim, *strips, *dstrips)
 

time: 122 us -> 121 us (level)
  waiting for transfers between devices: 23.3 us -> 25.2 us
    unnamed x26 -> x14, local copies, waits for them, and re-layouts: 3.61 us -> 2.42 us
  transfers between devices with their start and end apart: 11 -> 11, of which waited for: 8 -> 9; matrix products, arithmetic and copies ran while one was open for 7% -> 7% of each run, Pallas kernels for 7% -> 7%
where the time goes in v5:
time: 121 us; the launch traced here: 119 us
  starting transfers between devices  45.5 us (38%)
  Pallas kernels  38.8 us (32%)
  waiting for transfers between devices  25.2 us (21%)
  local copies, waits for them, and re-layouts  7.81 us (6%)
    ppermute x8, starting transfers between devices, shifted(): return lax.ppermute(array, axis, pairs)  24.9 us
    ppermute x8, waiting for transfers between devices, shifted(): return lax.ppermute(array, axis, pairs)  22.1 us
    pallas_call x1, Pallas kernels, tv(): pl.pallas_call(tv_kernel, grid=(maps // block,), out_shape=(jax.ShapeDtyp...  21.1 us
    all_to_all x3, starting transfers between devices, to_all(): return lax.all_to_all(array, LIB, 0, 0, tiled=True)  20.6 us
    pallas_call x1, Pallas kernels, front_duals(): pl.pallas_call(functools.partial(front_kernel, False), grid=(2, height //...  7.54 us
    pallas_call x1, Pallas kernels, front_abundance(): pl.pallas_call(functools.partial(front_kernel, True), grid=(height // 8,)...  5.5 us
    pallas_call x1, Pallas kernels, middle(): pl.pallas_call(middle_kernel, out_shape=(jax.ShapeDtypeStruct((8, maps +...  3.98 us
    all_to_all x3, waiting for transfers between devices, to_all(): return lax.all_to_all(array, LIB, 0, 0, tiled=True)  3.14 us
  transfers between devices with their start and end apart: 11, of which 9 were waited for; matrix products, arithmetic and copies ran while one was open for 7% of the time, Pallas kernels for 7%

profile of v5, /device:TPU:1, one launch (start us, length us, event | category | flops | bytes accessed | tf_op | source)
XLA Modules:
  0.0 119.4 jit_solution(1785982921382272755)
XLA Ops:
  0.6 5.5 %front_abundance.1 = (bf16[8,624,256]{2,1,0:T(8,128)(2,1)}, f32[32,8,128]{2,1,0:T(8,128)}) custom-call(f32[128,4,16,128]{3,2,1,0:T(8,128)} %bitcast.36, bf16[224,128]{1,0:T(8,128)(2,1)} %refs_1_.1), custom_call_target="tpu_custom_call" | custom-call | tf_op jit(solution)/shard_map/front_abundance/pallas_call | solution.py:102
  6.1 7.6 %all-to-all-start = ((bf16[8,624,256]{2,1,0:T(8,128)(2,1)}), bf16[8,624,256]{2,1,0:T(8,128)(2,1)}, u32[]{:S(2)}, u32[]{:S(2)}) async-start(bf16[8,624,256]{2,1,0:T(8,128)(2,1)} %get-tuple-element.14.refs_1_), calls=%async_computation | async-start | bytes 5111808 | tf_op jit(solution)/shard_map/all_to_all | solution.py:27
  13.7 7.5 %front_duals.1 = (bf16[2,4,128,256]{3,2,1,0:T(8,128)(2,1)S(1)}, bf16[2,4,128,256]{3,2,1,0:T(8,128)(2,1)S(1)}, f32[2,32,8,128]{3,2,1,0:T(8,128)S(1)}) custom-call(f32[2,128,4,16,128]{4,3,2,1,0:T(8,128)} %bitcast.35, bf16[8,624,256]{2,1,0:T(8,128)(2,1)S(1)} %copy-done.1), custom_call_target="tpu_custom_call" | custom-call | bytes 8000000 | tf_op jit(solution)/shard_map/front_duals/pallas_call | solution.py:122
  21.4 1.3 %collective-permute-start = (bf16[3,4,128,256]{3,2,1,0:T(8,128)(2,1)S(1)}, bf16[3,4,128,256]{3,2,1,0:T(8,128)(2,1)}, u32[]{:S(2)}, u32[]{:S(2)}) collective-permute-start(bf16[3,4,128,256]{3,2,1,0:T(8,128)(2,1)S(1)} %pad_maximum_fusion), channel_id=1, source_target_pairs={{4,0},{8,4},{12,8},{5,1},{9,5},{13,9},{6,2},{10,6},{14,10},{7,3},{... | collective-permute-start | bytes 2359304 | tf_op jit(solution)/shard_map/ppermute | solution.py:23
  23.7 5.1 %collective-permute-start.1 = (bf16[3,4,128,256]{3,2,1,0:T(8,128)(2,1)}, bf16[3,4,128,256]{3,2,1,0:T(8,128)(2,1)}, u32[]{:S(2)}, u32[]{:S(2)}) collective-permute-start(bf16[3,4,128,256]{3,2,1,0:T(8,128)(2,1)} %pad_maximum_fusion.1), channel_id=1, source_target_pairs={{0,4},{4,8},{8,12},{1,5},{5,9},{9,13},{2,6},{6,10},{10,14},{3,7},{... | collective-permute-start | bytes 2359304 | tf_op jit(solution)/shard_map/ppermute | solution.py:23
  28.8 1.4 %constant_dynamic-slice_fusion.1 = bf16[224,1,256]{2,1,0:T(2,128)(2,1)S(1)} fusion(bf16[224,32,256]{2,1,0:T(8,128)(2,1)} %param.6, s32[]{:T(128)S(6)} %select_n.11), kind=kLoop, calls=%fused_computation.19 | loop fusion | bytes 229380 | tf_op jit(solution)/shard_map/dynamic_slice | solution.py:402
  30.2 1.8 %constant_dynamic-slice_fusion = bf16[224,3,256]{2,1,0:T(4,128)(2,1)S(1)} fusion(bf16[224,32,256]{2,1,0:T(8,128)(2,1)} %param.6, s32[]{:T(128)S(6)} %select_n.12), kind=kLoop, calls=%fused_computation.18 | loop fusion | bytes 688132 | tf_op jit(solution)/shard_map/dynamic_slice | solution.py:403
  32.2 9.7 %collective-permute-done = bf16[3,4,128,256]{3,2,1,0:T(8,128)(2,1)} collective-permute-done((bf16[3,4,128,256]{3,2,1,0:T(8,128)(2,1)S(1)}, bf16[3,4,128,256]{3,2,1,0:T(8,128)(2,1)}, u32[]{:S(2)}, u32[]{:S(2)}) %collective-permute-start) | collective-permute-done | bytes 786464 | tf_op jit(solution)/shard_map/ppermute | solution.py:23
  41.9 1.2 constant_dynamic-update-slice_fusion.1
  43.9 1.2 constant_dynamic-update-slice_fusion.refs_0_.in_ref.rim_ref
  46.3 4.0 %middle.1 = (bf16[8,144,256]{2,1,0:T(8,128)(2,1)}, bf16[8,3,128,256]{3,2,1,0:T(8,128)(2,1)S(1)}) custom-call(bf16[8,624,256]{2,1,0:T(8,128)(2,1)} %all-to-all-done.blocks, bf16[4,224,256]{2,1,0:T(8,128)(2,1)S(1)} %maximum_bitcast_fusion.observed, bf16[3,8,128,256]{3,2,1,0:T(8,128)(2,1)S(1)} %constant_dynamic-update-slice_fusion.refs_0_.in_ref.rim_ref), custom_call_target="tpu_custom_call" | custom-call | tf_op jit(solution)/shard_map/middle/pallas_call | solution.py:183
  51.4 5.7 %all-to-all-start.1 = ((bf16[8,144,256]{2,1,0:T(8,128)(2,1)}), bf16[8,144,256]{2,1,0:T(8,128)(2,1)S(1)}, u32[]{:S(2)}, u32[]{:S(2)}) async-start(bf16[8,144,256]{2,1,0:T(8,128)(2,1)} %get-tuple-element.18), calls=%async_computation.1 | async-start | bytes 1179648 | tf_op jit(solution)/shard_map/all_to_all | solution.py:27
  57.2 4.4 %collective-permute-start.3 = (f32[3,40,8,128]{3,2,1,0:T(8,128)S(1)}, f32[3,40,8,128]{3,2,1,0:T(8,128)S(1)}, u32[]{:S(2)}, u32[]{:S(2)}) collective-permute-start(f32[3,40,8,128]{3,2,1,0:T(8,128)S(1)} %pad_maximum_fusion.2.own_ref), channel_id=1, source_target_pairs={{1,0},{2,1},{3,2},{5,4},{6,5},{7,6},{9,8},{10,9},{11,10},{13,12},{... | collective-permute-start | bytes 1474568 | tf_op jit(solution)/shard_map/ppermute | solution.py:23
  61.6 2.1 %collective-permute-start.2 = (f32[3,40,8,128]{3,2,1,0:T(8,128)S(1)}, f32[3,40,8,128]{3,2,1,0:T(8,128)S(1)}, u32[]{:S(2)}, u32[]{:S(2)}) collective-permute-start(f32[3,40,8,128]{3,2,1,0:T(8,128)S(1)} %pad_maximum_fusion.2.own_ref), channel_id=1, source_target_pairs={{0,1},{1,2},{2,3},{4,5},{5,6},{6,7},{8,9},{9,10},{10,11},{12,13},{... | collective-permute-start | bytes 1474568 | tf_op jit(solution)/shard_map/ppermute | solution.py:23
  63.8 6.4 %collective-permute-done.3.right_ref = f32[3,40,8,128]{3,2,1,0:T(8,128)S(1)} collective-permute-done((f32[3,40,8,128]{3,2,1,0:T(8,128)S(1)}, f32[3,40,8,128]{3,2,1,0:T(8,128)S(1)}, u32[]{:S(2)}, u32[]{:S(2)}) %collective-permute-start.3) | collective-permute-done | bytes 491552 | tf_op jit(solution)/shard_map/ppermute | solution.py:23
  70.2 7.3 %all-to-all-start.2 = ((bf16[8,3,128,256]{3,2,1,0:T(8,128)(2,1)}), bf16[8,3,128,256]{3,2,1,0:T(8,128)(2,1)}, u32[]{:S(2)}, u32[]{:S(2)}) async-start(bf16[8,3,128,256]{3,2,1,0:T(8,128)(2,1)} %copy-done.3), calls=%async_computation.2 | async-start | bytes 3145728 | tf_op jit(solution)/shard_map/all_to_all | solution.py:27
  77.5 1.3 %collective-permute-start.4 = (bf16[4,128,256]{2,1,0:T(8,128)(2,1)S(1)}, bf16[4,128,256]{2,1,0:T(8,128)(2,1)S(1)}, u32[]{:S(2)}, u32[]{:S(2)}) collective-permute-start(bf16[4,128,256]{2,1,0:T(8,128)(2,1)S(1)} %get-tuple-element.31), channel_id=1, source_target_pairs={{4,0},{8,4},{12,8},{5,1},{9,5},{13,9},{6,2},{10,6},{14,10},{7,3},{... | collective-permute-start | bytes 786440 | tf_op jit(solution)/shard_map/ppermute | solution.py:23
  78.9 4.7 %collective-permute-start.5 = (bf16[4,128,256]{2,1,0:T(8,128)(2,1)S(1)}, bf16[4,128,256]{2,1,0:T(8,128)(2,1)S(1)}, u32[]{:S(2)}, u32[]{:S(2)}) collective-permute-start(bf16[4,128,256]{2,1,0:T(8,128)(2,1)S(1)} %get-tuple-element.30), channel_id=1, source_target_pairs={{0,4},{4,8},{8,12},{1,5},{5,9},{9,13},{2,6},{6,10},{10,14},{3,7},{... | collective-permute-start | bytes 786440 | tf_op jit(solution)/shard_map/ppermute | solution.py:23
  83.6 2.3 %collective-permute-done.4 = bf16[4,128,256]{2,1,0:T(8,128)(2,1)S(1)} collective-permute-done((bf16[4,128,256]{2,1,0:T(8,128)(2,1)S(1)}, bf16[4,128,256]{2,1,0:T(8,128)(2,1)S(1)}, u32[]{:S(2)}, u32[]{:S(2)}) %collective-permute-start.4) | collective-permute-done | bytes 262176 | tf_op jit(solution)/shard_map/ppermute | solution.py:23
  86.0 1.4 %collective-permute-done.5 = bf16[4,128,256]{2,1,0:T(8,128)(2,1)S(1)} collective-permute-done((bf16[4,128,256]{2,1,0:T(8,128)(2,1)S(1)}, bf16[4,128,256]{2,1,0:T(8,128)(2,1)S(1)}, u32[]{:S(2)}, u32[]{:S(2)}) %collective-permute-start.5) | collective-permute-done | bytes 262176 | tf_op jit(solution)/shard_map/ppermute | solution.py:23
  87.7 1.9 %collective-permute-start.7 = (f32[1,40,8,128]{3,2,1,0:T(8,128)S(1)}, f32[1,40,8,128]{3,2,1,0:T(8,128)S(1)}, u32[]{:S(2)}, u32[]{:S(2)}) collective-permute-start(f32[1,40,8,128]{3,2,1,0:T(8,128)S(1)} %maximum_bitcast_fusion.1.down_ref), channel_id=1, source_target_pairs={{1,0},{2,1},{3,2},{5,4},{6,5},{7,6},{9,8},{10,9},{11,10},{13,12},{... | collective-permute-start | bytes 491528 | tf_op jit(solution)/shard_map/ppermute | solution.py:23
  89.6 4.0 %collective-permute-start.6 = (f32[1,40,8,128]{3,2,1,0:T(8,128)S(1)}, f32[1,40,8,128]{3,2,1,0:T(8,128)S(1)}, u32[]{:S(2)}, u32[]{:S(2)}) collective-permute-start(f32[1,40,8,128]{3,2,1,0:T(8,128)S(1)} %maximum_bitcast_fusion.1.down_ref), channel_id=1, source_target_pairs={{0,1},{1,2},{2,3},{4,5},{5,6},{6,7},{8,9},{9,10},{10,11},{12,13},{... | collective-permute-start | bytes 491528 | tf_op jit(solution)/shard_map/ppermute | solution.py:23
  95.8 2.4 %all-to-all-done.2 = bf16[8,3,128,256]{3,2,1,0:T(8,128)(2,1)} async-done(((bf16[8,3,128,256]{3,2,1,0:T(8,128)(2,1)}), bf16[8,3,128,256]{3,2,1,0:T(8,128)(2,1)}, u32[]{:S(2)}, u32[]{:S(2)}) %all-to-all-start.2) | async-done | bytes 1572896 | tf_op jit(solution)/shard_map/all_to_all | solution.py:27
  98.3 21.1 %tv.1 = (f32[128,32,256]{2,1,0:T(8,128)}, f32[2,128,32,256]{3,2,1,0:T(8,128)}) custom-call(s32[4]{0:T(128)S(1)} %pad_add_fusion.origin, f32[128,32,256]{2,1,0:T(8,128)} %ab_ref.1, f32[2,128,32,256]{3,2,1,0:T(8,128)} %q_ref.1, bf16[3,8,128,256]{3,2,1,0:T(8,128)(2,1)} %copy-done, bf16[8,128,256]{2,1,0:T(8,128)(2,1)} %slice.31.douter_ref, ...), custom_call_target="tpu_custom_call" | custom-call | tf_op jit(solution)/shard_map/tv/pallas_call | solution.py:366
  (36 shorter events, 6.9 us)
Async XLA Ops:
  6.1 7.6 %copy-start.1 = (bf16[8,624,256]{2,1,0:T(8,128)(2,1)S(1)}, bf16[8,624,256]{2,1,0:T(8,128)(2,1)}, u32[]{:S(2)}) copy-start(bf16[8,624,256]{2,1,0:T(8,128)(2,1)} %get-tuple-element.14.refs_1_) | copy-start | bytes 7667716
  6.1 40.2 %all-to-all-start = ((bf16[8,624,256]{2,1,0:T(8,128)(2,1)}), bf16[8,624,256]{2,1,0:T(8,128)(2,1)}, u32[]{:S(2)}, u32[]{:S(2)}) async-start(bf16[8,624,256]{2,1,0:T(8,128)(2,1)} %get-tuple-element.14.refs_1_), calls=%async_computation | async-start | bytes 5111808 | tf_op jit(solution)/shard_map/all_to_all | solution.py:27
  21.4 20.5 %collective-permute-start = (bf16[3,4,128,256]{3,2,1,0:T(8,128)(2,1)S(1)}, bf16[3,4,128,256]{3,2,1,0:T(8,128)(2,1)}, u32[]{:S(2)}, u32[]{:S(2)}) collective-permute-start(bf16[3,4,128,256]{3,2,1,0:T(8,128)(2,1)S(1)} %pad_maximum_fusion), channel_id=1, source_target_pairs={{4,0},{8,4},{12,8},{5,1},{9,5},{13,9},{6,2},{10,6},{14,10},{7,3},{... | collective-permute-start | bytes 2359304 | tf_op jit(solution)/shard_map/ppermute | solution.py:23
  23.7 20.2 %collective-permute-start.1 = (bf16[3,4,128,256]{3,2,1,0:T(8,128)(2,1)}, bf16[3,4,128,256]{3,2,1,0:T(8,128)(2,1)}, u32[]{:S(2)}, u32[]{:S(2)}) collective-permute-start(bf16[3,4,128,256]{3,2,1,0:T(8,128)(2,1)} %pad_maximum_fusion.1), channel_id=1, source_target_pairs={{0,4},{4,8},{8,12},{1,5},{5,9},{9,13},{2,6},{6,10},{10,14},{3,7},{... | collective-permute-start | bytes 2359304 | tf_op jit(solution)/shard_map/ppermute | solution.py:23
  45.1 5.2 %copy-start = (bf16[3,8,128,256]{3,2,1,0:T(8,128)(2,1)}, bf16[3,8,128,256]{3,2,1,0:T(8,128)(2,1)S(1)}, u32[]{:S(2)}) copy-start(bf16[3,8,128,256]{3,2,1,0:T(8,128)(2,1)S(1)} %constant_dynamic-update-slice_fusion.refs_0_.in_ref.rim_ref) | copy-start | bytes 4718596
  45.5 11.6 %copy-start.4 = (f32[32,8,128]{2,1,0:T(8,128)S(1)}, f32[32,8,128]{2,1,0:T(8,128)}, u32[]{:S(2)}) copy-start(f32[32,8,128]{2,1,0:T(8,128)} %get-tuple-element.19) | copy-start | bytes 393220
  50.3 1.1 copy-start.3
  51.4 18.8 %all-to-all-start.1 = ((bf16[8,144,256]{2,1,0:T(8,128)(2,1)}), bf16[8,144,256]{2,1,0:T(8,128)(2,1)S(1)}, u32[]{:S(2)}, u32[]{:S(2)}) async-start(bf16[8,144,256]{2,1,0:T(8,128)(2,1)} %get-tuple-element.18), calls=%async_computation.1 | async-start | bytes 1179648 | tf_op jit(solution)/shard_map/all_to_all | solution.py:27
  57.2 13.0 %collective-permute-start.3 = (f32[3,40,8,128]{3,2,1,0:T(8,128)S(1)}, f32[3,40,8,128]{3,2,1,0:T(8,128)S(1)}, u32[]{:S(2)}, u32[]{:S(2)}) collective-permute-start(f32[3,40,8,128]{3,2,1,0:T(8,128)S(1)} %pad_maximum_fusion.2.own_ref), channel_id=1, source_target_pairs={{1,0},{2,1},{3,2},{5,4},{6,5},{7,6},{9,8},{10,9},{11,10},{13,12},{... | collective-permute-start | bytes 1474568 | tf_op jit(solution)/shard_map/ppermute | solution.py:23
  61.6 8.6 %collective-permute-start.2 = (f32[3,40,8,128]{3,2,1,0:T(8,128)S(1)}, f32[3,40,8,128]{3,2,1,0:T(8,128)S(1)}, u32[]{:S(2)}, u32[]{:S(2)}) collective-permute-start(f32[3,40,8,128]{3,2,1,0:T(8,128)S(1)} %pad_maximum_fusion.2.own_ref), channel_id=1, source_target_pairs={{0,1},{1,2},{2,3},{4,5},{5,6},{6,7},{8,9},{9,10},{10,11},{12,13},{... | collective-permute-start | bytes 1474568 | tf_op jit(solution)/shard_map/ppermute | solution.py:23
  70.2 28.0 %all-to-all-start.2 = ((bf16[8,3,128,256]{3,2,1,0:T(8,128)(2,1)}), bf16[8,3,128,256]{3,2,1,0:T(8,128)(2,1)}, u32[]{:S(2)}, u32[]{:S(2)}) async-start(bf16[8,3,128,256]{3,2,1,0:T(8,128)(2,1)} %copy-done.3), calls=%async_computation.2 | async-start | bytes 3145728 | tf_op jit(solution)/shard_map/all_to_all | solution.py:27
  77.5 8.5 %collective-permute-start.4 = (bf16[4,128,256]{2,1,0:T(8,128)(2,1)S(1)}, bf16[4,128,256]{2,1,0:T(8,128)(2,1)S(1)}, u32[]{:S(2)}, u32[]{:S(2)}) collective-permute-start(bf16[4,128,256]{2,1,0:T(8,128)(2,1)S(1)} %get-tuple-element.31), channel_id=1, source_target_pairs={{4,0},{8,4},{12,8},{5,1},{9,5},{13,9},{6,2},{10,6},{14,10},{7,3},{... | collective-permute-start | bytes 786440 | tf_op jit(solution)/shard_map/ppermute | solution.py:23
  78.9 8.5 %collective-permute-start.5 = (bf16[4,128,256]{2,1,0:T(8,128)(2,1)S(1)}, bf16[4,128,256]{2,1,0:T(8,128)(2,1)S(1)}, u32[]{:S(2)}, u32[]{:S(2)}) collective-permute-start(bf16[4,128,256]{2,1,0:T(8,128)(2,1)S(1)} %get-tuple-element.30), channel_id=1, source_target_pairs={{0,4},{4,8},{8,12},{1,5},{5,9},{9,13},{2,6},{6,10},{10,14},{3,7},{... | collective-permute-start | bytes 786440 | tf_op jit(solution)/shard_map/ppermute | solution.py:23
  87.4 10.8 %copy-start.2 = (bf16[8,128,256]{2,1,0:T(8,128)(2,1)}, bf16[8,128,256]{2,1,0:T(8,128)(2,1)S(1)}, u32[]{:S(2)}) copy-start(bf16[8,128,256]{2,1,0:T(8,128)(2,1)S(1)} %constant_dynamic-update-slice_fusion.2.drim_ref) | copy-start | bytes 1572868
  87.7 7.4 %collective-permute-start.7 = (f32[1,40,8,128]{3,2,1,0:T(8,128)S(1)}, f32[1,40,8,128]{3,2,1,0:T(8,128)S(1)}, u32[]{:S(2)}, u32[]{:S(2)}) collective-permute-start(f32[1,40,8,128]{3,2,1,0:T(8,128)S(1)} %maximum_bitcast_fusion.1.down_ref), channel_id=1, source_target_pairs={{1,0},{2,1},{3,2},{5,4},{6,5},{7,6},{9,8},{10,9},{11,10},{13,12},{... | collective-permute-start | bytes 491528 | tf_op jit(solution)/shard_map/ppermute | solution.py:23
  89.6 6.3 %collective-permute-start.6 = (f32[1,40,8,128]{3,2,1,0:T(8,128)S(1)}, f32[1,40,8,128]{3,2,1,0:T(8,128)S(1)}, u32[]{:S(2)}, u32[]{:S(2)}) collective-permute-start(f32[1,40,8,128]{3,2,1,0:T(8,128)S(1)} %maximum_bitcast_fusion.1.down_ref), channel_id=1, source_target_pairs={{0,1},{1,2},{2,3},{4,5},{5,6},{6,7},{8,9},{9,10},{10,11},{12,13},{... | collective-permute-start | bytes 491528 | tf_op jit(solution)/shard_map/ppermute | solution.py:23

commit v6 on v5

--- a/solution.py
+++ b/solution.py
@@ -188,7 +188,7 @@
         ),
         in_specs=[WHOLE] * 2 + [pl.BlockSpec(memory_space=pl.ANY)] * len(first),
         out_specs=(WHOLE, WHOLE),
-        compiler_params=pltpu.CompilerParams(vmem_limit_bytes=16 * MIB),
+        compiler_params=pltpu.CompilerParams(vmem_limit_bytes=56 * MIB),
         name="middle",
     )(blocks, observed, *first)
 

time: 121 us -> 120 us (level)
  local copies, waits for them, and re-layouts: 7.81 us -> 5.55 us
    unnamed x14 -> x12, local copies, waits for them, and re-layouts: 2.42 us -> 0.15 us
  transfers between devices with their start and end apart: 11 -> 11, of which waited for: 9 -> 9; matrix products, arithmetic and copies ran while one was open for 7% -> 6% of each run, Pallas kernels for 7% -> 7%
where the time goes in v6:
time: 120 us; the launch traced here: 119 us
  starting transfers between devices  46 us (38%)
  Pallas kernels  39.4 us (33%)
  waiting for transfers between devices  25.6 us (21%)
  local copies, waits for them, and re-layouts  5.55 us (5%)
  other arithmetic  1.99 us (2%)
    ppermute x8, starting transfers between devices, shifted(): return lax.ppermute(array, axis, pairs)  24.9 us
    ppermute x8, waiting for transfers between devices, shifted(): return lax.ppermute(array, axis, pairs)  22.5 us
    all_to_all x3, starting transfers between devices, to_all(): return lax.all_to_all(array, LIB, 0, 0, tiled=True)  21.2 us
    pallas_call x1, Pallas kernels, tv(): pl.pallas_call(tv_kernel, grid=(maps // block,), out_shape=(jax.ShapeDtyp...  21.1 us
    pallas_call x1, Pallas kernels, front_duals(): pl.pallas_call(functools.partial(front_kernel, False), grid=(2, height //...  7.54 us
    pallas_call x1, Pallas kernels, front_abundance(): pl.pallas_call(functools.partial(front_kernel, True), grid=(height // 8,)...  5.51 us
    pallas_call x1, Pallas kernels, middle(): pl.pallas_call(middle_kernel, out_shape=(jax.ShapeDtypeStruct((8, maps +...  4.57 us
    all_to_all x3, waiting for transfers between devices, to_all(): return lax.all_to_all(array, LIB, 0, 0, tiled=True)  3.15 us
  transfers between devices with their start and end apart: 11, of which 9 were waited for; matrix products, arithmetic and copies ran while one was open for 6% of the time, Pallas kernels for 7%

profile of v6, /device:TPU:1, one launch (start us, length us, event | category | flops | bytes accessed | tf_op | source)
XLA Modules:
  0.0 119.4 jit_solution(17857504563031848922)
XLA Ops:
  0.6 5.5 %front_abundance.1 = (bf16[8,624,256]{2,1,0:T(8,128)(2,1)}, f32[32,8,128]{2,1,0:T(8,128)}) custom-call(f32[128,4,16,128]{3,2,1,0:T(8,128)} %bitcast.36, bf16[224,128]{1,0:T(8,128)(2,1)} %refs_1_.1), custom_call_target="tpu_custom_call" | custom-call | tf_op jit(solution)/shard_map/front_abundance/pallas_call | solution.py:102
  6.1 7.6 %all-to-all-start = ((bf16[8,624,256]{2,1,0:T(8,128)(2,1)}), bf16[8,624,256]{2,1,0:T(8,128)(2,1)}, u32[]{:S(2)}, u32[]{:S(2)}) async-start(bf16[8,624,256]{2,1,0:T(8,128)(2,1)} %get-tuple-element.14.refs_1_), calls=%async_computation | async-start | bytes 5111808 | tf_op jit(solution)/shard_map/all_to_all | solution.py:27
  13.8 7.5 %front_duals.1 = (bf16[2,4,128,256]{3,2,1,0:T(8,128)(2,1)S(1)}, bf16[2,4,128,256]{3,2,1,0:T(8,128)(2,1)S(1)}, f32[2,32,8,128]{3,2,1,0:T(8,128)S(1)}) custom-call(f32[2,128,4,16,128]{4,3,2,1,0:T(8,128)} %bitcast.35, bf16[8,624,256]{2,1,0:T(8,128)(2,1)S(1)} %copy-done.1), custom_call_target="tpu_custom_call" | custom-call | bytes 8000000 | tf_op jit(solution)/shard_map/front_duals/pallas_call | solution.py:122
  21.4 1.3 %collective-permute-start = (bf16[3,4,128,256]{3,2,1,0:T(8,128)(2,1)S(1)}, bf16[3,4,128,256]{3,2,1,0:T(8,128)(2,1)S(1)}, u32[]{:S(2)}, u32[]{:S(2)}) collective-permute-start(bf16[3,4,128,256]{3,2,1,0:T(8,128)(2,1)S(1)} %pad_maximum_fusion), channel_id=1, source_target_pairs={{4,0},{8,4},{12,8},{5,1},{9,5},{13,9},{6,2},{10,6},{14,10},{7,3},{... | collective-permute-start | bytes 2359304 | tf_op jit(solution)/shard_map/ppermute | solution.py:23
  23.7 5.0 %collective-permute-start.1 = (bf16[3,4,128,256]{3,2,1,0:T(8,128)(2,1)}, bf16[3,4,128,256]{3,2,1,0:T(8,128)(2,1)}, u32[]{:S(2)}, u32[]{:S(2)}) collective-permute-start(bf16[3,4,128,256]{3,2,1,0:T(8,128)(2,1)} %pad_maximum_fusion.1), channel_id=1, source_target_pairs={{0,4},{4,8},{8,12},{1,5},{5,9},{9,13},{2,6},{6,10},{10,14},{3,7},{... | collective-permute-start | bytes 2359304 | tf_op jit(solution)/shard_map/ppermute | solution.py:23
  28.7 1.4 %constant_dynamic-slice_fusion.1 = bf16[224,1,256]{2,1,0:T(2,128)(2,1)S(1)} fusion(bf16[224,32,256]{2,1,0:T(8,128)(2,1)} %param.6, s32[]{:T(128)S(6)} %select_n.11), kind=kLoop, calls=%fused_computation.19 | loop fusion | bytes 229380 | tf_op jit(solution)/shard_map/dynamic_slice | solution.py:402
  30.2 1.8 %constant_dynamic-slice_fusion = bf16[224,3,256]{2,1,0:T(4,128)(2,1)S(1)} fusion(bf16[224,32,256]{2,1,0:T(8,128)(2,1)} %param.6, s32[]{:T(128)S(6)} %select_n.12), kind=kLoop, calls=%fused_computation.18 | loop fusion | bytes 688132 | tf_op jit(solution)/shard_map/dynamic_slice | solution.py:403
  32.9 8.9 %collective-permute-done = bf16[3,4,128,256]{3,2,1,0:T(8,128)(2,1)S(1)} collective-permute-done((bf16[3,4,128,256]{3,2,1,0:T(8,128)(2,1)S(1)}, bf16[3,4,128,256]{3,2,1,0:T(8,128)(2,1)S(1)}, u32[]{:S(2)}, u32[]{:S(2)}) %collective-permute-start) | collective-permute-done | bytes 786464 | tf_op jit(solution)/shard_map/ppermute | solution.py:23
  41.9 2.1 %collective-permute-done.1 = bf16[3,4,128,256]{3,2,1,0:T(8,128)(2,1)} collective-permute-done((bf16[3,4,128,256]{3,2,1,0:T(8,128)(2,1)}, bf16[3,4,128,256]{3,2,1,0:T(8,128)(2,1)}, u32[]{:S(2)}, u32[]{:S(2)}) %collective-permute-start.1) | collective-permute-done | bytes 786464 | tf_op jit(solution)/shard_map/ppermute | solution.py:23
  43.9 1.2 constant_dynamic-update-slice_fusion.refs_0_.in_ref.rim_ref
  46.3 4.6 %middle.1 = (bf16[8,144,256]{2,1,0:T(8,128)(2,1)}, bf16[8,3,128,256]{3,2,1,0:T(8,128)(2,1)}) custom-call(bf16[8,624,256]{2,1,0:T(8,128)(2,1)} %all-to-all-done.blocks, bf16[4,224,256]{2,1,0:T(8,128)(2,1)} %maximum_bitcast_fusion.observed, bf16[3,8,128,256]{3,2,1,0:T(8,128)(2,1)} %copy-done), custom_call_target="tpu_custom_call" | custom-call | tf_op jit(solution)/shard_map/middle/pallas_call | solution.py:183
  50.9 6.3 %all-to-all-start.1 = ((bf16[8,144,256]{2,1,0:T(8,128)(2,1)}), bf16[8,144,256]{2,1,0:T(8,128)(2,1)S(1)}, u32[]{:S(2)}, u32[]{:S(2)}) async-start(bf16[8,144,256]{2,1,0:T(8,128)(2,1)} %get-tuple-element.18), calls=%async_computation.1 | async-start | bytes 1179648 | tf_op jit(solution)/shard_map/all_to_all | solution.py:27
  57.2 4.4 %collective-permute-start.3 = (f32[3,40,8,128]{3,2,1,0:T(8,128)S(1)}, f32[3,40,8,128]{3,2,1,0:T(8,128)S(1)}, u32[]{:S(2)}, u32[]{:S(2)}) collective-permute-start(f32[3,40,8,128]{3,2,1,0:T(8,128)S(1)} %pad_maximum_fusion.2.own_ref), channel_id=1, source_target_pairs={{1,0},{2,1},{3,2},{5,4},{6,5},{7,6},{9,8},{10,9},{11,10},{13,12},{... | collective-permute-start | bytes 1474568 | tf_op jit(solution)/shard_map/ppermute | solution.py:23
  61.7 2.1 %collective-permute-start.2 = (f32[3,40,8,128]{3,2,1,0:T(8,128)S(1)}, f32[3,40,8,128]{3,2,1,0:T(8,128)S(1)}, u32[]{:S(2)}, u32[]{:S(2)}) collective-permute-start(f32[3,40,8,128]{3,2,1,0:T(8,128)S(1)} %pad_maximum_fusion.2.own_ref), channel_id=1, source_target_pairs={{0,1},{1,2},{2,3},{4,5},{5,6},{6,7},{8,9},{9,10},{10,11},{12,13},{... | collective-permute-start | bytes 1474568 | tf_op jit(solution)/shard_map/ppermute | solution.py:23
  63.8 6.4 %collective-permute-done.3.right_ref = f32[3,40,8,128]{3,2,1,0:T(8,128)S(1)} collective-permute-done((f32[3,40,8,128]{3,2,1,0:T(8,128)S(1)}, f32[3,40,8,128]{3,2,1,0:T(8,128)S(1)}, u32[]{:S(2)}, u32[]{:S(2)}) %collective-permute-start.3) | collective-permute-done | bytes 491552 | tf_op jit(solution)/shard_map/ppermute | solution.py:23
  70.2 7.3 %all-to-all-start.2 = ((bf16[8,3,128,256]{3,2,1,0:T(8,128)(2,1)}), bf16[8,3,128,256]{3,2,1,0:T(8,128)(2,1)}, u32[]{:S(2)}, u32[]{:S(2)}) async-start(bf16[8,3,128,256]{3,2,1,0:T(8,128)(2,1)} %get-tuple-element.22), calls=%async_computation.2 | async-start | bytes 3145728 | tf_op jit(solution)/shard_map/all_to_all | solution.py:27
  77.5 1.3 %collective-permute-start.4 = (bf16[4,128,256]{2,1,0:T(8,128)(2,1)S(1)}, bf16[4,128,256]{2,1,0:T(8,128)(2,1)S(1)}, u32[]{:S(2)}, u32[]{:S(2)}) collective-permute-start(bf16[4,128,256]{2,1,0:T(8,128)(2,1)S(1)} %get-tuple-element.31), channel_id=1, source_target_pairs={{4,0},{8,4},{12,8},{5,1},{9,5},{13,9},{6,2},{10,6},{14,10},{7,3},{... | collective-permute-start | bytes 786440 | tf_op jit(solution)/shard_map/ppermute | solution.py:23
  78.9 4.7 %collective-permute-start.5 = (bf16[4,128,256]{2,1,0:T(8,128)(2,1)S(1)}, bf16[4,128,256]{2,1,0:T(8,128)(2,1)S(1)}, u32[]{:S(2)}, u32[]{:S(2)}) collective-permute-start(bf16[4,128,256]{2,1,0:T(8,128)(2,1)S(1)} %get-tuple-element.30), channel_id=1, source_target_pairs={{0,4},{4,8},{8,12},{1,5},{5,9},{9,13},{2,6},{6,10},{10,14},{3,7},{... | collective-permute-start | bytes 786440 | tf_op jit(solution)/shard_map/ppermute | solution.py:23
  83.7 2.3 %collective-permute-done.4 = bf16[4,128,256]{2,1,0:T(8,128)(2,1)S(1)} collective-permute-done((bf16[4,128,256]{2,1,0:T(8,128)(2,1)S(1)}, bf16[4,128,256]{2,1,0:T(8,128)(2,1)S(1)}, u32[]{:S(2)}, u32[]{:S(2)}) %collective-permute-start.4) | collective-permute-done | bytes 262176 | tf_op jit(solution)/shard_map/ppermute | solution.py:23
  86.1 1.4 %collective-permute-done.5 = bf16[4,128,256]{2,1,0:T(8,128)(2,1)S(1)} collective-permute-done((bf16[4,128,256]{2,1,0:T(8,128)(2,1)S(1)}, bf16[4,128,256]{2,1,0:T(8,128)(2,1)S(1)}, u32[]{:S(2)}, u32[]{:S(2)}) %collective-permute-start.5) | collective-permute-done | bytes 262176 | tf_op jit(solution)/shard_map/ppermute | solution.py:23
  87.7 1.9 %collective-permute-start.7 = (f32[1,40,8,128]{3,2,1,0:T(8,128)S(1)}, f32[1,40,8,128]{3,2,1,0:T(8,128)S(1)}, u32[]{:S(2)}, u32[]{:S(2)}) collective-permute-start(f32[1,40,8,128]{3,2,1,0:T(8,128)S(1)} %maximum_bitcast_fusion.1.down_ref), channel_id=1, source_target_pairs={{1,0},{2,1},{3,2},{5,4},{6,5},{7,6},{9,8},{10,9},{11,10},{13,12},{... | collective-permute-start | bytes 491528 | tf_op jit(solution)/shard_map/ppermute | solution.py:23
  89.6 4.0 %collective-permute-start.6 = (f32[1,40,8,128]{3,2,1,0:T(8,128)S(1)}, f32[1,40,8,128]{3,2,1,0:T(8,128)S(1)}, u32[]{:S(2)}, u32[]{:S(2)}) collective-permute-start(f32[1,40,8,128]{3,2,1,0:T(8,128)S(1)} %maximum_bitcast_fusion.1.down_ref), channel_id=1, source_target_pairs={{0,1},{1,2},{2,3},{4,5},{5,6},{6,7},{8,9},{9,10},{10,11},{12,13},{... | collective-permute-start | bytes 491528 | tf_op jit(solution)/shard_map/ppermute | solution.py:23
  95.9 2.4 %all-to-all-done.2 = bf16[8,3,128,256]{3,2,1,0:T(8,128)(2,1)} async-done(((bf16[8,3,128,256]{3,2,1,0:T(8,128)(2,1)}), bf16[8,3,128,256]{3,2,1,0:T(8,128)(2,1)}, u32[]{:S(2)}, u32[]{:S(2)}) %all-to-all-start.2) | async-done | bytes 1572896 | tf_op jit(solution)/shard_map/all_to_all | solution.py:27
  98.3 21.1 %tv.1 = (f32[128,32,256]{2,1,0:T(8,128)}, f32[2,128,32,256]{3,2,1,0:T(8,128)}) custom-call(s32[4]{0:T(128)S(1)} %pad_add_fusion.origin, f32[128,32,256]{2,1,0:T(8,128)} %ab_ref.1, f32[2,128,32,256]{3,2,1,0:T(8,128)} %q_ref.1, bf16[3,8,128,256]{3,2,1,0:T(8,128)(2,1)} %copy-done, bf16[8,128,256]{2,1,0:T(8,128)(2,1)} %slice.31.douter_ref, ...), custom_call_target="tpu_custom_call" | custom-call | tf_op jit(solution)/shard_map/tv/pallas_call | solution.py:366
  (34 shorter events, 5.8 us)
Async XLA Ops:
  6.1 7.6 %copy-start.1 = (bf16[8,624,256]{2,1,0:T(8,128)(2,1)S(1)}, bf16[8,624,256]{2,1,0:T(8,128)(2,1)}, u32[]{:S(2)}) copy-start(bf16[8,624,256]{2,1,0:T(8,128)(2,1)} %get-tuple-element.14.refs_1_) | copy-start | bytes 7667716
  6.1 40.2 %all-to-all-start = ((bf16[8,624,256]{2,1,0:T(8,128)(2,1)}), bf16[8,624,256]{2,1,0:T(8,128)(2,1)}, u32[]{:S(2)}, u32[]{:S(2)}) async-start(bf16[8,624,256]{2,1,0:T(8,128)(2,1)} %get-tuple-element.14.refs_1_), calls=%async_computation | async-start | bytes 5111808 | tf_op jit(solution)/shard_map/all_to_all | solution.py:27
  21.4 20.4 %collective-permute-start = (bf16[3,4,128,256]{3,2,1,0:T(8,128)(2,1)S(1)}, bf16[3,4,128,256]{3,2,1,0:T(8,128)(2,1)S(1)}, u32[]{:S(2)}, u32[]{:S(2)}) collective-permute-start(bf16[3,4,128,256]{3,2,1,0:T(8,128)(2,1)S(1)} %pad_maximum_fusion), channel_id=1, source_target_pairs={{4,0},{8,4},{12,8},{5,1},{9,5},{13,9},{6,2},{10,6},{14,10},{7,3},{... | collective-permute-start | bytes 2359304 | tf_op jit(solution)/shard_map/ppermute | solution.py:23
  23.7 20.2 %collective-permute-start.1 = (bf16[3,4,128,256]{3,2,1,0:T(8,128)(2,1)}, bf16[3,4,128,256]{3,2,1,0:T(8,128)(2,1)}, u32[]{:S(2)}, u32[]{:S(2)}) collective-permute-start(bf16[3,4,128,256]{3,2,1,0:T(8,128)(2,1)} %pad_maximum_fusion.1), channel_id=1, source_target_pairs={{0,4},{4,8},{8,12},{1,5},{5,9},{9,13},{2,6},{6,10},{10,14},{3,7},{... | collective-permute-start | bytes 2359304 | tf_op jit(solution)/shard_map/ppermute | solution.py:23
  45.1 1.2 copy-start
  45.6 11.6 %copy-start.3 = (f32[32,8,128]{2,1,0:T(8,128)S(1)}, f32[32,8,128]{2,1,0:T(8,128)}, u32[]{:S(2)}) copy-start(f32[32,8,128]{2,1,0:T(8,128)} %get-tuple-element.19) | copy-start | bytes 393220
  50.9 19.4 %all-to-all-start.1 = ((bf16[8,144,256]{2,1,0:T(8,128)(2,1)}), bf16[8,144,256]{2,1,0:T(8,128)(2,1)S(1)}, u32[]{:S(2)}, u32[]{:S(2)}) async-start(bf16[8,144,256]{2,1,0:T(8,128)(2,1)} %get-tuple-element.18), calls=%async_computation.1 | async-start | bytes 1179648 | tf_op jit(solution)/shard_map/all_to_all | solution.py:27
  57.2 13.0 %collective-permute-start.3 = (f32[3,40,8,128]{3,2,1,0:T(8,128)S(1)}, f32[3,40,8,128]{3,2,1,0:T(8,128)S(1)}, u32[]{:S(2)}, u32[]{:S(2)}) collective-permute-start(f32[3,40,8,128]{3,2,1,0:T(8,128)S(1)} %pad_maximum_fusion.2.own_ref), channel_id=1, source_target_pairs={{1,0},{2,1},{3,2},{5,4},{6,5},{7,6},{9,8},{10,9},{11,10},{13,12},{... | collective-permute-start | bytes 1474568 | tf_op jit(solution)/shard_map/ppermute | solution.py:23
  61.7 8.6 %collective-permute-start.2 = (f32[3,40,8,128]{3,2,1,0:T(8,128)S(1)}, f32[3,40,8,128]{3,2,1,0:T(8,128)S(1)}, u32[]{:S(2)}, u32[]{:S(2)}) collective-permute-start(f32[3,40,8,128]{3,2,1,0:T(8,128)S(1)} %pad_maximum_fusion.2.own_ref), channel_id=1, source_target_pairs={{0,1},{1,2},{2,3},{4,5},{5,6},{6,7},{8,9},{9,10},{10,11},{12,13},{... | collective-permute-start | bytes 1474568 | tf_op jit(solution)/shard_map/ppermute | solution.py:23
  70.2 28.1 %all-to-all-start.2 = ((bf16[8,3,128,256]{3,2,1,0:T(8,128)(2,1)}), bf16[8,3,128,256]{3,2,1,0:T(8,128)(2,1)}, u32[]{:S(2)}, u32[]{:S(2)}) async-start(bf16[8,3,128,256]{3,2,1,0:T(8,128)(2,1)} %get-tuple-element.22), calls=%async_computation.2 | async-start | bytes 3145728 | tf_op jit(solution)/shard_map/all_to_all | solution.py:27
  77.5 8.5 %collective-permute-start.4 = (bf16[4,128,256]{2,1,0:T(8,128)(2,1)S(1)}, bf16[4,128,256]{2,1,0:T(8,128)(2,1)S(1)}, u32[]{:S(2)}, u32[]{:S(2)}) collective-permute-start(bf16[4,128,256]{2,1,0:T(8,128)(2,1)S(1)} %get-tuple-element.31), channel_id=1, source_target_pairs={{4,0},{8,4},{12,8},{5,1},{9,5},{13,9},{6,2},{10,6},{14,10},{7,3},{... | collective-permute-start | bytes 786440 | tf_op jit(solution)/shard_map/ppermute | solution.py:23
  78.9 8.6 %collective-permute-start.5 = (bf16[4,128,256]{2,1,0:T(8,128)(2,1)S(1)}, bf16[4,128,256]{2,1,0:T(8,128)(2,1)S(1)}, u32[]{:S(2)}, u32[]{:S(2)}) collective-permute-start(bf16[4,128,256]{2,1,0:T(8,128)(2,1)S(1)} %get-tuple-element.30), channel_id=1, source_target_pairs={{0,4},{4,8},{8,12},{1,5},{5,9},{9,13},{2,6},{6,10},{10,14},{3,7},{... | collective-permute-start | bytes 786440 | tf_op jit(solution)/shard_map/ppermute | solution.py:23
  87.5 10.8 %copy-start.2 = (bf16[8,128,256]{2,1,0:T(8,128)(2,1)}, bf16[8,128,256]{2,1,0:T(8,128)(2,1)S(1)}, u32[]{:S(2)}) copy-start(bf16[8,128,256]{2,1,0:T(8,128)(2,1)S(1)} %constant_dynamic-update-slice_fusion.2.drim_ref) | copy-start | bytes 1572868
  87.7 7.4 %collective-permute-start.7 = (f32[1,40,8,128]{3,2,1,0:T(8,128)S(1)}, f32[1,40,8,128]{3,2,1,0:T(8,128)S(1)}, u32[]{:S(2)}, u32[]{:S(2)}) collective-permute-start(f32[1,40,8,128]{3,2,1,0:T(8,128)S(1)} %maximum_bitcast_fusion.1.down_ref), channel_id=1, source_target_pairs={{1,0},{2,1},{3,2},{5,4},{6,5},{7,6},{9,8},{10,9},{11,10},{13,12},{... | collective-permute-start | bytes 491528 | tf_op jit(solution)/shard_map/ppermute | solution.py:23
  89.6 6.2 %collective-permute-start.6 = (f32[1,40,8,128]{3,2,1,0:T(8,128)S(1)}, f32[1,40,8,128]{3,2,1,0:T(8,128)S(1)}, u32[]{:S(2)}, u32[]{:S(2)}) collective-permute-start(f32[1,40,8,128]{3,2,1,0:T(8,128)S(1)} %maximum_bitcast_fusion.1.down_ref), channel_id=1, source_target_pairs={{0,1},{1,2},{2,3},{4,5},{5,6},{6,7},{8,9},{9,10},{10,11},{12,13},{... | collective-permute-start | bytes 491528 | tf_op jit(solution)/shard_map/ppermute | solution.py:23
